TPU v7x, 128 devices: a whole 4x4x4 slice. The times are simulated.
128 devices in a mesh: tensor: 8 (over z_lo, x), decode: 16 (over z_hi, y, core).
Axes of the slice: x: 4, y: 4, z: 4 (z_hi: 2, z_lo: 2; z = z_hi * 2 + z_lo), core: 2. Of those that a mesh axis runs over, the one named last changes fastest.
Arguments:
- hidden_in: bfloat16 [16, 512, 8192], P('decode', 'tensor'), may hold values from -640 to 640
- norm_gain: float32 [8192], replicated, may hold values from 0.5 to 2
- w_query: bfloat16 [8192, 4096], P('decode', 'tensor'), may hold values from -0.0625 to 0.0625
- w_key: bfloat16 [8192, 1024], P('decode', 'tensor'), may hold values from -0.0625 to 0.0625
- w_value: bfloat16 [8192, 1024], P('decode', 'tensor'), may hold values from -0.0625 to 0.0625
- w_out: bfloat16 [4096, 8192], P('tensor', 'decode'), may hold values from -3 to 3
- cache_k: bfloat16 [16, 8, 8192, 128], P('decode', 'tensor'), may hold values from -128 to 128
- cache_v: bfloat16 [16, 8, 8192, 128], P('decode', 'tensor'), may hold values from -6 to 6
- prefix_len: int32 [16], P('decode'), may hold values from 2048 to 8192, as said below
- page_owner: int32 [16, 4], P('decode'), may hold values from 0 to 15, as said below
Outputs:
- attn_out: bfloat16 [16, 512, 8192], P('decode', 'tensor')
- owned_pages: bfloat16 [16, 32, 2, 128, 1024], P('decode', None, None, None, 'tensor')
- owned_scales: bfloat16 [16, 32, 2, 8], P('decode', None, None, 'tensor')
- owned_ids: int32 [16, 32], P('decode')
Inputs may be any that keep to these rules, and one draw needn't show every extreme that they name: `prefix_len`: one prompt has 8192 live positions and another 8192 // 4. `page_owner`: no prompt sends more than 2 pages to one owner, and some prompt sends exactly 2 pages to some owner.
All inputs are finite; a program needn't handle non-finite values.
Results may differ from a plain program's by a relative error of at most 0.02.
Values may be sent and summed in bfloat16 or wider, within the bound.
No kernel may reach another device: no remote copies, remote signals or barrier semaphores. Data moves between devices by JAX's collectives and lax.ppermute only.
A program may use at most 192 MiB of HBM per device.

v0:
```python
import math

import jax
import jax.numpy as jnp
from jax import lax
from jax.sharding import PartitionSpec as P

CAP = 2


THETA = 500000.0
EPS = 1e-05


def rope_tables(positions, width):
    half = width // 2
    steps = jnp.arange(half, dtype=jnp.float32) * (2.0 / width)
    freqs = jnp.exp(-math.log(THETA) * steps)
    angles = positions.astype(jnp.float32)[:, None] * freqs[None, :]
    return (jnp.cos(angles), jnp.sin(angles))


def rotate(values, cosine, sine):
    half = values.shape[-1] // 2
    first = values[..., :half]
    second = values[..., half:]
    cos_part = cosine[:, None, :]
    sin_part = sine[:, None, :]
    return jnp.concatenate(
        [first * cos_part - second * sin_part, second * cos_part + first * sin_part], axis=-1
    )


def attend_head(query, keys, values, allowed, factor):
    scores = jnp.dot(query, keys.T, preferred_element_type=jnp.float32) * factor
    scores = jnp.where(allowed, scores, -jnp.inf)
    top = jnp.max(scores, axis=1, keepdims=True)
    expo = jnp.exp(scores - top)
    total = jnp.sum(expo, axis=1, keepdims=True)
    weights = (expo / total).astype(jnp.bfloat16)
    return jnp.dot(weights, values, preferred_element_type=jnp.float32).astype(jnp.bfloat16)


def send_pages(keys, new_values, page_owner):
    groups = lax.axis_size("decode")
    count = page_owner.shape[1]
    width = keys.shape[1]
    page = keys.shape[0] // count
    both = jnp.stack(
        [keys.reshape(count, page, width), new_values.reshape(count, page, width)], axis=1
    )
    magnitude = jnp.max(jnp.abs(both.astype(jnp.float32)), axis=(2, 3))
    page_scale = (magnitude + 1e-06).astype(jnp.bfloat16)
    scaled = (both.astype(jnp.float32) / page_scale.astype(jnp.float32)[:, :, None, None]).astype(
        jnp.bfloat16
    )
    owners = page_owner[0]
    index = jnp.arange(count, dtype=jnp.int32)
    same = owners[:, None] == owners[None, :]
    earlier = index[None, :] < index[:, None]
    rank = jnp.sum((same & earlier).astype(jnp.int32), axis=1)
    target = owners * CAP + rank
    slot_ids = jnp.arange(groups * CAP, dtype=jnp.int32)[:, None]
    onehot = slot_ids == target[None, :]
    picker = onehot.astype(jnp.bfloat16)
    placed = jnp.dot(picker, scaled.reshape(count, -1), preferred_element_type=jnp.float32).astype(
        jnp.bfloat16
    )
    placed_scale = jnp.dot(picker, page_scale, preferred_element_type=jnp.float32).astype(
        jnp.bfloat16
    )
    numbered = jnp.where(onehot, index[None, :].astype(jnp.float32) + 1.0, 0.0)
    placed_id = (jnp.sum(numbered, axis=1) - 1.0).astype(jnp.bfloat16)
    got_pages, got_scale, got_id = (
        lax.all_to_all(
            placed.reshape(groups, CAP, 2, page, width),
            "decode",
            split_axis=0,
            concat_axis=0,
            tiled=True,
        ),
        lax.all_to_all(
            placed_scale.reshape(groups, CAP, 2), "decode", split_axis=0, concat_axis=0, tiled=True
        ),
        lax.all_to_all(
            placed_id.reshape(groups, CAP), "decode", split_axis=0, concat_axis=0, tiled=True
        ),
    )
    owned_pages = got_pages.reshape(1, groups * CAP, 2, page, width)
    owned_scales = got_scale.reshape(1, groups * CAP, 2, 1)
    owned_ids = got_id.reshape(1, groups * CAP).astype(jnp.int32)
    return (owned_pages, owned_scales, owned_ids)


def body(
    hidden_in, norm_gain, w_query, w_key, w_value, w_out, cache_k, cache_v, prefix_len, page_owner
):
    rows = hidden_in[0].astype(jnp.float32)
    mean_sq = jnp.mean(rows * rows, axis=1, keepdims=True)
    normed = (rows * lax.rsqrt(mean_sq + EPS) * norm_gain).astype(jnp.bfloat16)
    gathered = lax.all_gather(normed, "tensor", axis=0, tiled=True)
    span = gathered.shape[0]
    width = cache_k.shape[-1]
    prefix = cache_k.shape[2]
    q_cols = w_query.shape[1]
    heads = q_cols // width
    factor = 1.0 / math.sqrt(width)
    live = prefix_len[0]
    positions = live + jnp.arange(span, dtype=jnp.int32)
    cosine, sine = rope_tables(positions, width)

    def add_rows(piece):
        return jnp.dot(gathered, piece, preferred_element_type=jnp.float32)

    q_raw = add_rows(lax.all_gather(w_query, "decode", axis=0, tiled=True))
    key_raw = add_rows(lax.all_gather(w_key, "decode", axis=0, tiled=True))
    value_raw = add_rows(lax.all_gather(w_value, "decode", axis=0, tiled=True))
    keys = rotate(key_raw[:, None, :], cosine, sine)[:, 0, :].astype(jnp.bfloat16)
    keys, new_values = (keys, value_raw.astype(jnp.bfloat16))
    queries = rotate(q_raw.reshape(span, heads, width), cosine, sine).astype(jnp.bfloat16)
    all_keys = jnp.concatenate([cache_k[0, 0], keys], axis=0)
    all_values = jnp.concatenate([cache_v[0, 0], new_values], axis=0)
    column = jnp.arange(prefix + span, dtype=jnp.int32)[None, :]
    row = jnp.arange(span, dtype=jnp.int32)[:, None]
    allowed = jnp.where(column < prefix, column < live, column - prefix <= row)
    outs = [
        attend_head(queries[:, j, :], all_keys, all_values, allowed, factor) for j in range(heads)
    ]
    attended = jnp.concatenate(outs, axis=1)
    owned_pages, owned_scales, owned_ids = send_pages(keys, new_values, page_owner)
    partial_sum = jnp.dot(
        attended,
        lax.all_gather(w_out, "decode", axis=1, tiled=True),
        preferred_element_type=jnp.float32,
    )
    partial_sum = partial_sum.astype(jnp.bfloat16).astype(jnp.float32)
    summed = lax.psum_scatter(
        partial_sum.astype(jnp.bfloat16), "tensor", scatter_dimension=0, tiled=True
    )
    attn_out = summed[None]
    return (attn_out, owned_pages, owned_scales, owned_ids)


def solution(mesh):
    in_specs = (
        P("decode", "tensor", None),
        P(),
        P("decode", "tensor"),
        P("decode", "tensor"),
        P("decode", "tensor"),
        P("tensor", "decode"),
        P("decode", "tensor", None, None),
        P("decode", "tensor", None, None),
        P("decode"),
        P("decode", None),
    )
    out_specs = (
        P("decode", "tensor", None),
        P("decode", None, None, None, "tensor"),
        P("decode", None, None, "tensor"),
        P("decode", None),
    )
    return jax.shard_map(body, mesh=mesh, in_specs=in_specs, out_specs=out_specs, check_vma=False)
```

profile of v0, /device:TPU:1, one launch (start us, length us, event | category | flops | bytes accessed | tf_op | source)
XLA Modules:
  0.0 534.4 jit_solution(7493976893463310805)
XLA Ops:
  7.2 0.0 all-gather.10.cloned.1.call-start
  7.2 0.7 all-gather.10.cloned.1.call-update
  7.9 0.0 all-gather.6.cloned.1.call-start
  7.9 1.5 fusion.9
  9.5 2.5 fusion.11
  12.0 0.0 all-gather.6.cloned.1.call-update
  12.0 0.0 all-gather.12.cloned.1.call-start
  12.1 0.7 all-gather.12.cloned.1.call-update
  12.8 0.0 all-gather.8.cloned.1.call-start
  12.8 0.5 all-gather.8.cloned.1.call-update
  13.3 0.0 all-gather.14.cloned.1.call-start
  13.4 0.5 all-gather.14.cloned.1.call-update
  13.9 0.0 reduce-scatter.2.cloned.1.call-start
  14.7 0.5 multiply_cosine_fusion.1
  15.2 47.4 %all-gather.10.cloned.1.call-done = bf16[8192,128]{1,0:T(8,128)(2,1)} async-done(((bf16[512,128]{1,0:T(8,128)(2,1)}), bf16[8192,128]{1,0:T(8,128)(2,1)}) %all-gather.10.cloned.1.call-update) | async-done | bytes 2097168 | tf_op jit(solution)/shard_map/all_gather | solution.py:116
  62.6 92.4 %all-gather.6.cloned.1.call-done = bf16[512,8192]{1,0:T(8,128)(2,1)} async-done(((bf16[64,8192]{1,0:T(8,128)(2,1)}), bf16[512,8192]{1,0:T(8,128)(2,1)}) %all-gather.6.cloned.1.call-update) | async-done | bytes 8388624 | tf_op jit(solution)/shard_map/all_gather | solution.py:101
  155.0 6.9 %convolution_bitcast_fusion = f32[512,1,128]{0,2,1:T(8,128)S(1)} fusion(bf16[512,8192]{1,0:T(8,128)(2,1)} %all-gather.6.cloned.1.call-done, bf16[8192,128]{1,0:T(8,128)(2,1)} %all-gather.10.cloned.1.call-done), kind=kOutput, calls=%fused_computation.32 | convolution fusion | flops 1073741824 | bytes 10747904 | tf_op jit(solution)/shard_map/dot_general | solution.py:113
  161.9 0.6 fusion.32
  162.4 0.6 copy-done
  163.0 0.0 copy-done.2
  163.1 0.1 copy.25
  163.2 41.9 %all-gather.12.cloned.1.call-done = bf16[8192,128]{1,0:T(8,128)(2,1)} async-done(((bf16[512,128]{1,0:T(8,128)(2,1)}), bf16[8192,128]{1,0:T(8,128)(2,1)}) %all-gather.12.cloned.1.call-update) | async-done | bytes 2097168 | tf_op jit(solution)/shard_map/all_gather | solution.py:117
  205.1 6.3 %convolution_convert_fusion.2 = bf16[512,128]{1,0:T(8,128)(2,1)S(1)} fusion(bf16[512,8192]{1,0:T(8,128)(2,1)} %all-gather.6.cloned.1.call-done, bf16[8192,128]{1,0:T(8,128)(2,1)} %all-gather.12.cloned.1.call-done), kind=kOutput, calls=%fused_computation.37 | convolution fusion | flops 1073807360 | bytes 10616832 | tf_op jit(solution)/shard_map/dot_general | solution.py:113
  211.4 67.5 %all-gather.8.cloned.1.call-done = bf16[8192,512]{1,0:T(8,128)(2,1)} async-done(((bf16[512,512]{1,0:T(8,128)(2,1)}), bf16[8192,512]{1,0:T(8,128)(2,1)}) %all-gather.8.cloned.1.call-update) | async-done | bytes 8388624 | tf_op jit(solution)/shard_map/all_gather | solution.py:115
  278.9 9.6 %fusion.62 = f32[512,512]{0,1:T(8,128)S(1)} fusion(bf16[512,8192]{1,0:T(8,128)(2,1)} %all-gather.6.cloned.1.call-done, bf16[8192,512]{1,0:T(8,128)(2,1)} %all-gather.8.cloned.1.call-done), kind=kOutput, calls=%fused_computation.112 | convolution fusion | flops 4294967296 | bytes 17825792 | tf_op jit(solution)/shard_map/dot_general | solution.py:113
  288.5 0.2 subtract_convert_fusion
  288.7 10.9 %fusion.60 = (f32[512]{0:T(512)S(1)}, f32[512,8704]{1,0:T(8,128)}) fusion(bf16[512,128]{1,0:T(8,128)(2,1)S(1)} %copy.25, bf16[8192,128]{1,0:T(8,128)(2,1)S(1)} %bitcast.78, bf16[512,4,64]{0,2,1:T(8,128)(2,1)S(1)} %get-tuple-element.4, bf16[512,4,64]{0,2,1:T(8,128)(2,1)S(1)} %get-tuple-element.5, s32[8704]{0:T(1024)S(1)} %iota_add_fusion, ...), kind=kOutput, calls=%fused_computation.110 | convolution fusion | flops 1167851008 | bytes 20632576 | tf_op jit(solution)/shard_map/dot_general | solution.py:35
  299.6 8.6 %fusion.1 = f32[512]{0:T(512)S(1)} fusion(f32[512,8704]{1,0:T(8,128)} %get-tuple-element.17, f32[512]{0:T(512)S(1)} %get-tuple-element.16), kind=kLoop, calls=%fused_computation.15 | loop fusion | flops 8912384 | bytes 17829888 | tf_op jit(solution)/shard_map/reduce_sum | solution.py:39
  308.3 11.1 %fusion.59 = (f32[512]{0:T(512)S(1)}, f32[512,8704]{1,0:T(8,128)}) fusion(bf16[512,128]{1,0:T(8,128)(2,1)S(1)} %copy.25, bf16[8192,128]{1,0:T(8,128)(2,1)S(1)} %bitcast.79, bf16[512,4,64]{0,2,1:T(8,128)(2,1)S(1)} %get-tuple-element.4, bf16[512,4,64]{0,2,1:T(8,128)(2,1)S(1)} %get-tuple-element.5, s32[8704]{0:T(1024)S(1)} %iota_add_fusion, ...), kind=kOutput, calls=%fused_computation.109 | convolution fusion | flops 1167851008 | bytes 20632576 | tf_op jit(solution)/shard_map/dot_general | solution.py:35
  319.4 8.5 %fusion.2 = f32[512]{0:T(512)S(1)} fusion(f32[512,8704]{1,0:T(8,128)} %get-tuple-element.15, f32[512]{0:T(512)S(1)} %get-tuple-element.14), kind=kLoop, calls=%fused_computation.16 | loop fusion | flops 8912384 | bytes 17829888 | tf_op jit(solution)/shard_map/reduce_sum | solution.py:39
  327.9 11.3 %fusion.58 = (f32[512]{0:T(512)S(1)}, f32[512,8704]{1,0:T(8,128)}) fusion(bf16[512,128]{1,0:T(8,128)(2,1)S(1)} %copy.25, bf16[8192,128]{1,0:T(8,128)(2,1)S(1)} %bitcast.80, bf16[512,4,64]{0,2,1:T(8,128)(2,1)S(1)} %get-tuple-element.4, bf16[512,4,64]{0,2,1:T(8,128)(2,1)S(1)} %get-tuple-element.5, s32[8704]{0:T(1024)S(1)} %iota_add_fusion, ...), kind=kOutput, calls=%fused_computation.108 | convolution fusion | flops 1167851008 | bytes 20632576 | tf_op jit(solution)/shard_map/dot_general | solution.py:35
  339.2 8.9 %fusion.3 = f32[512]{0:T(512)S(1)} fusion(f32[512,8704]{1,0:T(8,128)} %get-tuple-element.13, f32[512]{0:T(512)S(1)} %get-tuple-element.12), kind=kLoop, calls=%fused_computation.17 | loop fusion | flops 8912384 | bytes 17829888 | tf_op jit(solution)/shard_map/reduce_sum | solution.py:39
  348.1 10.6 %fusion.57 = (f32[512]{0:T(512)S(1)}, f32[512,8704]{1,0:T(8,128)}) fusion(bf16[512,128]{1,0:T(8,128)(2,1)S(1)} %copy.25, bf16[8192,128]{1,0:T(8,128)(2,1)} %bitcast.77, bf16[512,4,64]{0,2,1:T(8,128)(2,1)S(1)} %get-tuple-element.5, bf16[512,4,64]{0,2,1:T(8,128)(2,1)S(1)} %get-tuple-element.4, s32[8704]{0:T(1024)S(1)} %iota_add_fusion, ...), kind=kOutput, calls=%fused_computation.107 | convolution fusion | flops 1167851008 | bytes 20632576 | tf_op jit(solution)/shard_map/dot_general | solution.py:35
  358.7 8.6 %fusion.4 = f32[512]{0:T(512)S(1)} fusion(f32[512,8704]{1,0:T(8,128)} %get-tuple-element.11, f32[512]{0:T(512)S(1)} %get-tuple-element.10), kind=kLoop, calls=%fused_computation.18 | loop fusion | flops 8912384 | bytes 17829888 | tf_op jit(solution)/shard_map/reduce_sum | solution.py:39
  367.4 9.1 %fusion.16 = bf16[512,128]{0,1:T(8,128)(2,1)S(1)} fusion(f32[512,8704]{1,0:T(8,128)} %get-tuple-element.17, f32[512]{0:T(512)S(1)} %fusion.1, f32[512]{0:T(512)S(1)} %get-tuple-element.16, bf16[512,128]{1,0:T(8,128)(2,1)S(1)} %convolution_convert_fusion.2, bf16[8192,128]{1,0:T(8,128)(2,1)} %bitcast.81), kind=kOutput, calls=%fused_computation.36 | convolution fusion | flops 1158742016 | bytes 20189184 | tf_op jit(solution)/shard_map/dot_general | solution.py:41
  376.6 1.1 slice-done.3
  377.7 1.2 slice-done.4
  378.9 5.3 fusion.15
  384.2 8.9 %fusion.14 = bf16[512,128]{0,1:T(8,128)(2,1)S(1)} fusion(f32[512,8704]{1,0:T(8,128)} %get-tuple-element.13, f32[512]{0:T(512)S(1)} %fusion.3, f32[512]{0:T(512)S(1)} %get-tuple-element.12, bf16[512,128]{1,0:T(8,128)(2,1)S(1)} %convolution_convert_fusion.2, bf16[8192,128]{1,0:T(8,128)(2,1)} %bitcast.83), kind=kOutput, calls=%fused_computation.34 | convolution fusion | flops 1158742016 | bytes 20189184 | tf_op jit(solution)/shard_map/dot_general | solution.py:41
  393.2 8.9 %fusion.13 = bf16[512,128]{0,1:T(8,128)(2,1)S(1)} fusion(f32[512,8704]{1,0:T(8,128)} %get-tuple-element.11, f32[512]{0:T(512)S(1)} %fusion.4, f32[512]{0:T(512)S(1)} %get-tuple-element.10, bf16[512,128]{1,0:T(8,128)(2,1)S(1)} %convolution_convert_fusion.2, bf16[8192,128]{1,0:T(8,128)(2,1)S(1)} %bitcast.84), kind=kOutput, calls=%fused_computation.33 | convolution fusion | flops 1158742016 | bytes 20189184 | tf_op jit(solution)/shard_map/dot_general | solution.py:41
  402.1 0.0 all-gather.14.cloned.1.call-done
  402.2 10.2 %convolution_convert_fusion.1 = bf16[512,8192]{1,0:T(8,128)(2,1)} fusion(bf16[512,8192]{1,0:T(8,128)(2,1)} %all-gather.14.cloned.1.call-done, bf16[512,128]{0,1:T(8,128)(2,1)S(1)} %fusion.13, bf16[512,128]{0,1:T(8,128)(2,1)S(1)} %fusion.14, bf16[512,128]{0,1:T(8,128)(2,1)S(1)} %fusion.15, bf16[512,128]{0,1:T(8,128)(2,1)S(1)} %fusion.16), kind=kOutput, calls=%fused_computation.19 | convolution fusion | flops 4301258752 | bytes 17301504 | tf_op jit(solution)/shard_map/dot_general | solution.py:131
  412.3 0.0 reduce-scatter.2.cloned.1.call-update
  412.4 0.6 copy-done.6
  413.0 0.2 convert_reduce_fusion.1
  413.2 0.1 select_reduce_fusion
  413.3 0.7 convert_element_type.170
  414.0 3.5 all-to-all-start.2
  417.5 0.1 copy.31
  417.6 0.1 fusion.17
  417.8 0.2 convolution_convert_fusion.3
  418.0 0.1 reshape.231
  418.1 0.1 fusion.18
  418.2 0.6 copy.28
  418.8 5.7 %all-to-all-done.2 = bf16[16,1,2]{2,1,0:T(2,128)(2,1)S(1)} async-done(((bf16[16,1,2]{2,1,0:T(2,128)(2,1)}), bf16[16,1,2]{2,1,0:T(2,128)(2,1)S(1)}, u32[]{:S(2)}, u32[]{:S(2)}) %all-to-all-start.2) | async-done | bytes 96 | tf_op jit(solution)/shard_map/all_to_all | solution.py:85
  424.5 3.8 all-to-all-start.1
  428.3 0.8 fusion.12
  429.1 1.8 copy.33
  430.9 4.5 all-to-all-done.1
  435.4 4.0 all-to-all-start
  439.5 0.6 reshape.234
  440.1 0.6 reshape.232
  440.7 85.4 %all-to-all-done = bf16[16,2,2,128,128]{4,3,2,1,0:T(8,128)(2,1)S(1)} async-done(((bf16[16,2,2,128,128]{4,3,2,1,0:T(8,128)(2,1)}), bf16[16,2,2,128,128]{4,3,2,1,0:T(8,128)(2,1)S(1)}, u32[]{:S(2)}, u32[]{:S(2)}) %all-to-all-start) | async-done | bytes 2097184 | tf_op jit(solution)/shard_map/all_to_all | solution.py:75
  526.1 1.3 copy.40
  (34 shorter events, 0.2 us)
Async XLA Ops:
  7.2 55.4 %all-gather.10.cloned.1.call-start = ((), (), s32[]{:S(2)}) async-start(), calls=%async_computation.6 | async-start | bytes 2228224 | tf_op jit(solution)/shard_map/all_gather | solution.py:116
  7.9 147.1 %all-gather.6.cloned.1.call-start = ((), (), s32[]{:S(2)}) async-start(), calls=%async_computation.4 | async-start | bytes 9437184 | tf_op jit(solution)/shard_map/all_gather | solution.py:101
  12.0 193.1 %all-gather.12.cloned.1.call-start = ((), (), s32[]{:S(2)}) async-start(), calls=%async_computation.7 | async-start | bytes 2228224 | tf_op jit(solution)/shard_map/all_gather | solution.py:117
  12.8 266.1 %all-gather.8.cloned.1.call-start = ((), (), s32[]{:S(2)}) async-start(), calls=%async_computation.5 | async-start | bytes 8912896 | tf_op jit(solution)/shard_map/all_gather | solution.py:115
  13.3 388.8 %all-gather.14.cloned.1.call-start = ((), (), s32[]{:S(2)}) async-start(), calls=%async_computation.8 | async-start | bytes 8912896 | tf_op jit(solution)/shard_map/all_gather | solution.py:133
  13.9 512.2 %reduce-scatter.2.cloned.1.call-start = ((), (), s32[]{:S(2)}) async-start(), calls=%async_computation.9 | async-start | bytes 9437184 | tf_op jit(solution)/shard_map/reduce_scatter | solution.py:137
  162.4 0.6 copy-start
  162.4 0.6 copy-start.2
  211.4 77.3 %copy-start.4 = (bf16[1,1,8192,128]{3,2,1,0:T(8,128)(2,1)S(1)}, bf16[1,1,8192,128]{3,2,1,0:T(8,128)(2,1)}, u32[]{:S(2)}) copy-start(bf16[1,1,8192,128]{3,2,1,0:T(8,128)(2,1)} %param.16) | copy-start | bytes 6291460
  358.7 17.8 %slice-start = ((s8[17825792]{0:T(1024)(128)(4,1)}), s8[1048576]{0:T(1024)(128)(4,1)S(1)}, s32[]{:S(2)}) async-start(s8[17825792]{0:T(1024)(128)(4,1)} %bitcast.67), calls=%async_computation.10 | async-start | bytes 2097152
  367.4 9.2 %slice-start.1 = ((s8[17825792]{0:T(1024)(128)(4,1)}), s8[4194304]{0:T(1024)(128)(4,1)S(1)}, s32[]{:S(2)}) async-start(s8[17825792]{0:T(1024)(128)(4,1)} %bitcast.67), calls=%async_computation.11 | async-start | bytes 8388608
  367.4 9.2 %slice-start.2 = ((s8[17825792]{0:T(1024)(128)(4,1)}), s8[4194304]{0:T(1024)(128)(4,1)S(1)}, s32[]{:S(2)}) async-start(s8[17825792]{0:T(1024)(128)(4,1)} %bitcast.67), calls=%async_computation.12 | async-start | bytes 8388608
  367.4 10.3 %slice-start.3 = ((s8[17825792]{0:T(1024)(128)(4,1)}), s8[4194304]{0:T(1024)(128)(4,1)S(1)}, s32[]{:S(2)}) async-start(s8[17825792]{0:T(1024)(128)(4,1)} %bitcast.67), calls=%async_computation.13 | async-start | bytes 8388608
  367.4 11.5 %slice-start.4 = ((s8[17825792]{0:T(1024)(128)(4,1)}), s8[4194304]{0:T(1024)(128)(4,1)S(1)}, s32[]{:S(2)}) async-start(s8[17825792]{0:T(1024)(128)(4,1)} %bitcast.67), calls=%async_computation.14 | async-start | bytes 8388608
  384.2 9.0 %copy-start.5 = (bf16[1,1,8192,128]{3,2,1,0:T(8,128)(2,1)S(1)}, bf16[1,1,8192,128]{3,2,1,0:T(8,128)(2,1)}, u32[]{:S(2)}) copy-start(bf16[1,1,8192,128]{3,2,1,0:T(8,128)(2,1)} %param.17) | copy-start | bytes 6291460
  412.3 0.7 copy-start.6
  412.3 5.2 copy-start.1
  412.3 5.2 copy-start.3
  414.0 10.6 %all-to-all-start.2 = ((bf16[16,1,2]{2,1,0:T(2,128)(2,1)}), bf16[16,1,2]{2,1,0:T(2,128)(2,1)S(1)}, u32[]{:S(2)}, u32[]{:S(2)}) async-start(bf16[16,1,2]{2,1,0:T(2,128)(2,1)} %convert_element_type.170), calls=%async_computation.3 | async-start | bytes 16384 | tf_op jit(solution)/shard_map/all_to_all | solution.py:85
  424.5 10.9 %all-to-all-start.1 = ((bf16[16,2,2]{1,2,0:T(2,128)(2,1)}), bf16[16,2,2]{1,2,0:T(2,128)(2,1)S(1)}, u32[]{:S(2)}, u32[]{:S(2)}) async-start(bf16[16,2,2]{1,2,0:T(2,128)(2,1)} %copy.28), calls=%async_computation.2 | async-start | bytes 16384 | tf_op jit(solution)/shard_map/all_to_all | solution.py:82
  435.4 90.7 %all-to-all-start = ((bf16[16,2,2,128,128]{4,3,2,1,0:T(8,128)(2,1)}), bf16[16,2,2,128,128]{4,3,2,1,0:T(8,128)(2,1)S(1)}, u32[]{:S(2)}, u32[]{:S(2)}) async-start(bf16[16,2,2,128,128]{4,3,2,1,0:T(8,128)(2,1)} %bitcast.70), calls=%async_computation.1 | async-start | bytes 4194304 | tf_op jit(solution)/shard_map/all_to_all | solution.py:75
Sparse Core Ops, SparseCore 0:
  10.4 52.0 all-gather.9
  64.8 90.1 all-gather.5
  157.4 47.6 all-gather.11
  207.4 71.4 all-gather.7
  281.0 77.8 all-gather.13
  412.5 107.5 reduce-scatter.1
where the time goes:
time: 540 us; the launch traced here: 534 us
  waiting for transfers between devices  347 us (64%)
  matrix products  110 us (20%)
  other arithmetic  40.7 us (8%)
  between operations  15.3 us (3%)
  starting transfers between devices  11.5 us (2%)
  local copies, waits for them, and re-layouts  9.59 us (2%)
    all_gather x1, waiting for transfers between devices, body(): gathered = lax.all_gather(normed, 'tensor', axis=0, tiled=True)  92.4 us
    all_to_all x1, waiting for transfers between devices, send_pages(): lax.all_to_all(placed.reshape(groups, CAP, 2, page, width), 'decode', spl...  85.4 us
    all_gather x1, waiting for transfers between devices, body(): q_raw = add_rows(lax.all_gather(w_query, 'decode', axis=0, tiled=True))  67.5 us
    all_gather x1, waiting for transfers between devices, body(): key_raw = add_rows(lax.all_gather(w_key, 'decode', axis=0, tiled=True))  47.4 us
    dot_general x4, matrix products, attend_head(): scores = jnp.dot(query, keys.T, preferred_element_type=jnp.float32) * factor  43.9 us
    all_gather x1, waiting for transfers between devices, body(): value_raw = add_rows(lax.all_gather(w_value, 'decode', axis=0, tiled=True))  41.9 us
    reduce_sum x4, other arithmetic, attend_head(): total = jnp.sum(expo, axis=1, keepdims=True)  34.7 us
    dot_general x4, matrix products, attend_head(): jnp.dot(weights, values, preferred_element_type=jnp.float32)  32.3 us
  transfers between devices with their start and end apart: 9, of which 7 were waited for; matrix products, arithmetic and copies ran while one was open for 27% of the time, Pallas kernels for 0%

commit v1 on v0

v1 whole, which is shorter than its diff:
```python
import functools
import math

import jax
import jax.numpy as jnp
from jax import lax
from jax.experimental import pallas as pl
from jax.experimental.pallas import tpu as pltpu
from jax.sharding import PartitionSpec as P

CAP = 2
THETA = 500000.0
EPS = 1e-05
BF = jnp.bfloat16
F32 = jnp.float32
MB = 2**20


def tensor_perm(move):
    pairs = []
    for z in range(2):
        for x in range(4):
            a, b = move(z, x)
            pairs.append((z * 4 + x, a * 4 + b % 4))
    return pairs


def decode_perm(move):
    pairs = []
    for z in range(2):
        for y in range(4):
            for c in range(2):
                a, b, e = move(z, y, c)
                pairs.append((z * 8 + y * 2 + c, a * 8 + (b % 4) * 2 + e))
    return pairs


X_UP = tensor_perm(lambda z, x: (z, x + 1))
X_DOWN = tensor_perm(lambda z, x: (z, x - 1))
Z_SWAP = tensor_perm(lambda z, x: (1 - z, x))
Y_UP = decode_perm(lambda z, y, c: (z, y + 1, c))
Y_DOWN = decode_perm(lambda z, y, c: (z, y - 1, c))
ZH_SWAP = decode_perm(lambda z, y, c: (1 - z, y, c))
CORE_SWAP = decode_perm(lambda z, y, c: (z, y, 1 - c))
X_GROUPS = [[0, 1, 2, 3], [4, 5, 6, 7]]


def to_t(value, pairs):
    return lax.ppermute(value, "tensor", pairs)


def to_d(value, pairs):
    return lax.ppermute(value, "decode", pairs)


def gather_rows(own, z, x):
    h = own.shape[0] // 2
    left = to_t(own, X_UP)
    right = to_t(own, X_DOWN)
    over = to_t(own, Z_SWAP)
    over_left_a = to_t(left[:h], Z_SWAP)
    over_right_b = to_t(right[h:], Z_SWAP)
    over_left_b = to_t(over[h:], X_UP)
    over_right_a = to_t(over[:h], X_DOWN)
    far_a = to_t(left[:h], X_UP)
    far_b = to_t(right[h:], X_DOWN)
    over_far_b = to_t(over_left_b, X_UP)
    over_far_a = to_t(over_right_a, X_DOWN)
    here, there = z * 4, (1 - z) * 4
    lo, hi, far = (x + 3) % 4, (x + 1) % 4, (x + 2) % 4
    return [
        (own, here + x, 0),
        (left, here + lo, 0),
        (right, here + hi, 0),
        (over, there + x, 0),
        (over_left_a, there + lo, 0),
        (over_left_b, there + lo, h),
        (over_right_a, there + hi, 0),
        (over_right_b, there + hi, h),
        (far_a, here + far, 0),
        (far_b, here + far, h),
        (over_far_a, there + far, 0),
        (over_far_b, there + far, h),
    ]


def gather_shards(own, zh, y, core):
    h = own.shape[0] // 2
    over = to_d(own, ZH_SWAP)
    low = to_d(own, Y_UP)
    high = to_d(own, Y_DOWN)
    over_low = to_d(over, Y_UP)
    over_high = to_d(over, Y_DOWN)
    far_a = to_d(low[:h], Y_UP)
    far_b = to_d(high[h:], Y_DOWN)
    over_far_a = to_d(over_low[:h], Y_UP)
    over_far_b = to_d(over_high[h:], Y_DOWN)
    here, there = zh * 8 + core, (1 - zh) * 8 + core
    lo, hi, far = (y + 3) % 4 * 2, (y + 1) % 4 * 2, (y + 2) % 4 * 2
    whole = [
        (own, here + y * 2),
        (over, there + y * 2),
        (low, here + lo),
        (high, here + hi),
        (over_low, there + lo),
        (over_high, there + hi),
    ]
    halves = [
        (far_a, far_b, here + far),
        (over_far_a, over_far_b, there + far),
    ]
    flip = 1 - 2 * core
    whole = whole + [(to_d(a, CORE_SWAP), i + flip) for a, i in whole]
    halves = halves + [
        (to_d(a, CORE_SWAP), to_d(b, CORE_SWAP), i + flip) for a, b, i in halves
    ]
    return whole, halves


def hbm():
    return pl.BlockSpec(memory_space=pl.ANY)


def vmem():
    return pl.BlockSpec(memory_space=pltpu.VMEM)


def smem():
    return pl.BlockSpec(memory_space=pltpu.SMEM)


def load_shards(refs, place, sems):
    for i in range(12):
        pltpu.make_async_copy(refs[i], place(i, None), sems.at[i]).start()
    for i in range(4):
        for half in range(2):
            ref = refs[12 + 2 * i + half]
            pltpu.make_async_copy(ref, place(12 + i, half), sems.at[12 + i]).start()


def flat_shards(whole, halves):
    arrays = [a for a, _ in whole] + [a for p in halves for a in p[:2]]
    index = jnp.stack([i for _, i in whole] + [p[2] for p in halves]).astype(jnp.int32)
    return arrays, index


def project_kernel(n_rows, rot_scale, x_at, w_at, cos_ref, sin_ref, *refs):
    xs, ws = refs[:n_rows], refs[n_rows : n_rows + 20]
    q_ref, k_ref, v_ref, xv, wv, acc, xsem, wsem = refs[n_rows + 20 :]
    copies = []
    for i, ref in enumerate(xs):
        for part in range(ref.shape[0] // 32):
            to = pl.multiple_of(x_at[2 * i + part], 32)
            copies.append(
                pltpu.make_async_copy(
                    ref.at[pl.ds(part * 32, 32), :],
                    xv.at[pl.ds(to, 32), :],
                    xsem.at[2 * i + part],
                )
            )
    for copy in copies:
        copy.start()
    depth = ws[0].shape[0]

    def place(i, half):
        base = pl.multiple_of(w_at[i] * depth, depth)
        if half is None:
            return wv.at[pl.ds(base, depth), :]
        return wv.at[pl.ds(base + half * (depth // 2), depth // 2), :]

    load_shards(ws, place, wsem)
    for copy in copies:
        copy.wait()

    def step(i, carry):
        base = pl.multiple_of(w_at[i] * depth, depth)
        part = wv.at[pl.ds(base, depth), :]
        pltpu.make_async_copy(part, part, wsem.at[i]).wait()
        term = jnp.dot(xv[:, pl.ds(base, depth)], part[...], preferred_element_type=F32)

        @pl.when(i == 0)
        def _():
            acc[...] = term

        @pl.when(i > 0)
        def _():
            acc[...] += term

        return carry

    lax.fori_loop(0, 16, step, 0)
    cos, sin = cos_ref[...], sin_ref[...]
    heads = q_ref.shape[0]

    def rotated(j):
        part = acc[:, j * 128 : (j + 1) * 128]
        return part * cos + pltpu.roll(part, 64, 1) * sin

    for j in range(heads):
        q_ref[j] = (rotated(j) * rot_scale).astype(BF)
    keys = rotated(heads).astype(BF)
    values = acc[:, (heads + 1) * 128 :].astype(BF)
    half = keys.shape[0] // 2
    for s in range(half // 32):
        for r in range(2):
            rows = slice(r * half + s * 32, r * half + s * 32 + 32)
            to = slice(s * 64 + r * 32, s * 64 + r * 32 + 32)
            k_ref[to, :] = keys[rows]
            v_ref[to, :] = values[rows]


def project(pieces, whole, halves, cosine, sine, span):
    arrays = [a for a, _, _ in pieces]
    width = arrays[0].shape[1]
    at = []
    for a, source, offset in pieces:
        for part in range(2):
            first = offset + part * 32
            at.append(source * 32 + (first // 32 % 2) * (span // 2))
    ws, index = flat_shards(whole, halves)
    cols = ws[0].shape[1]
    heads = cols // 128 - 2
    scale = math.log2(math.e) / math.sqrt(128)
    n = len(arrays)
    return pl.pallas_call(
        functools.partial(project_kernel, n, scale),
        in_specs=[smem(), smem(), vmem(), vmem()] + [hbm()] * (n + 20),
        out_specs=[vmem()] * 3,
        out_shape=[
            jax.ShapeDtypeStruct((heads, span, 128), BF),
            jax.ShapeDtypeStruct((span, 128), BF),
            jax.ShapeDtypeStruct((span, 128), BF),
        ],
        scratch_shapes=[
            pltpu.VMEM((span, width), BF),
            pltpu.VMEM((width, cols), BF),
            pltpu.VMEM((span, cols), F32),
            pltpu.SemaphoreType.DMA((2 * n,)),
            pltpu.SemaphoreType.DMA((16,)),
        ],
        compiler_params=pltpu.CompilerParams(vmem_limit_bytes=40 * MB),
        cost_estimate=pl.CostEstimate(
            flops=2 * span * width * cols, bytes_accessed=24 * MB, transcendentals=0
        ),
        name="project",
    )(jnp.stack(at).astype(jnp.int32), index, cosine, sine, *arrays, *ws)


def attend_kernel(chunk, block, live_ref, q_ref, k_ref, v_ref, kn_ref, vn_ref, o_ref):
    live = live_ref[0]
    q = q_ref[0]

    def update(state, keys, values, allowed):
        s = lax.dot_general(q, keys, (((1,), (1,)), ((), ())), preferred_element_type=F32)
        if allowed is not None:
            s = jnp.where(allowed(s.shape), s, -1e30)
        top = jnp.max(s, axis=1, keepdims=True)
        if state is not None:
            top = jnp.maximum(state[0], top)
        p = jnp.exp2(s - top)
        total = sum(p[:, c * 128 : (c + 1) * 128] for c in range(p.shape[1] // 128))
        out = jnp.dot(p.astype(BF), values, preferred_element_type=F32)
        if state is None:
            return top, total, out
        keep = jnp.exp2(state[0] - top)
        return top, state[1] * keep + total, state[2] * keep + out

    def cached(j, state, allowed=None):
        at = pl.ds(pl.multiple_of(j * block, block), block)
        return update(state, k_ref[at, :], v_ref[at, :], allowed)

    def new_allowed(shape):
        i = lax.broadcasted_iota(jnp.int32, shape, 0)
        row = i // 32 * 64 + chunk * 32 + i % 32
        return lax.broadcasted_iota(jnp.int32, shape, 1) <= row

    full = live // block
    state = update(None, kn_ref[...], vn_ref[...], new_allowed)
    state = lax.fori_loop(0, full, cached, state)
    left = live - full * block

    def last(state):
        return cached(
            full, state, lambda shape: lax.broadcasted_iota(jnp.int32, shape, 1) < left
        )

    top, total, out = lax.cond(left > 0, last, lambda s: s, state)
    o_ref[...] = (out / jnp.sum(total, axis=1, keepdims=True)).astype(BF)


def attend(chunk, q, cache_k, cache_v, keys, values, live):
    heads, span, width = q.shape
    rows = span // 2
    prefix = cache_k.shape[0]
    block = 2048
    return pl.pallas_call(
        functools.partial(attend_kernel, chunk, block),
        grid=(heads,),
        in_specs=[
            smem(),
            pl.BlockSpec((1, rows, width), lambda i: (i, chunk, 0)),
            vmem(),
            vmem(),
            vmem(),
            vmem(),
        ],
        out_specs=pl.BlockSpec((rows, width), lambda i: (0, i)),
        out_shape=jax.ShapeDtypeStruct((rows, heads * width), BF),
        compiler_params=pltpu.CompilerParams(vmem_limit_bytes=40 * MB),
        cost_estimate=pl.CostEstimate(
            flops=4 * heads * rows * (prefix + span) * width,
            bytes_accessed=4 * prefix * width,
            transcendentals=heads * rows * (prefix + span),
        ),
        name="attend",
    )(live, q, cache_k, cache_v, keys, values)


def output_kernel(x_at, w_at, z_at, a0, a1, a2, a3, a4, *refs):
    ws = refs[:20]
    send_ref, keep_ref, xv, wv, xsem, wsem = refs[20:]
    width = a0.shape[1]
    half = a3.shape[0]
    copies = []
    for i, (ref, row) in enumerate(((a0, 0), (a1, 0), (a2, 0), (a3, 0), (a4, half))):
        to = pl.multiple_of(x_at[i] * width, width)
        copies.append(
            pltpu.make_async_copy(
                ref, xv.at[pl.ds(row, ref.shape[0]), pl.ds(to, width)], xsem.at[i]
            )
        )
    for copy in copies:
        copy.start()
    depth, cols = ws[0].shape

    def place(i, part):
        to = pl.multiple_of(w_at[i] * cols, cols)
        if part is None:
            return wv.at[:, pl.ds(to, cols)]
        return wv.at[pl.ds(part * (depth // 2), depth // 2), pl.ds(to, cols)]

    load_shards(ws, place, wsem)
    for copy in copies:
        copy.wait()
    for i in range(16):
        part = place(i, None)
        pltpu.make_async_copy(part, part, wsem.at[i]).wait()
    theirs = pl.multiple_of((1 - z_at[0]) * half, half)
    mine = pl.multiple_of(z_at[0] * half, half)

    def step(i, carry):
        at = pl.ds(pl.multiple_of(i * 512, 512), 512)
        w = wv[:, at]
        send_ref[:, at] = jnp.dot(
            xv[pl.ds(theirs, half), :], w, preferred_element_type=F32
        ).astype(BF)
        keep_ref[:, at] = jnp.dot(xv[pl.ds(mine, half), :], w, preferred_element_type=F32)
        return carry

    lax.fori_loop(0, wv.shape[1] // 512, step, 0)


def output(attended, whole, halves, z, x):
    half = attended.shape[0] // 2
    left = to_t(attended, X_UP)
    right = to_t(attended, X_DOWN)
    far_a = to_t(left[:half], X_UP)
    far_b = to_t(right[half:], X_DOWN)
    far = (x + 2) % 4
    at = jnp.stack([x, (x + 3) % 4, (x + 1) % 4, far, far]).astype(jnp.int32)
    ws, index = flat_shards(whole, halves)
    depth, cols = ws[0].shape
    return pl.pallas_call(
        output_kernel,
        in_specs=[smem()] * 3 + [hbm()] * 25,
        out_specs=[vmem()] * 2,
        out_shape=[
            jax.ShapeDtypeStruct((half, 16 * cols), BF),
            jax.ShapeDtypeStruct((half, 16 * cols), F32),
        ],
        scratch_shapes=[
            pltpu.VMEM((2 * half, depth), BF),
            pltpu.VMEM((depth, 16 * cols), BF),
            pltpu.SemaphoreType.DMA((5,)),
            pltpu.SemaphoreType.DMA((16,)),
        ],
        compiler_params=pltpu.CompilerParams(vmem_limit_bytes=40 * MB),
        cost_estimate=pl.CostEstimate(
            flops=4 * half * depth * 16 * cols, bytes_accessed=11 * MB, transcendentals=0
        ),
        name="output",
    )(at, index, z[None].astype(jnp.int32), attended, left, right, far_a, far_b, *ws)


def place_kernel(pages, w_at, page_of, *refs):
    ws = refs[:20]
    out_ref, scale_ref, wv, wsem = refs[20:]
    depth, cols = ws[0].shape
    page = depth // pages

    def place(i, part):
        base = pl.multiple_of(w_at[i] * depth, depth)
        if part is None:
            return wv.at[pl.ds(base, depth), :]
        return wv.at[pl.ds(base + part * (depth // 2), depth // 2), :]

    load_shards(ws, place, wsem)
    for i in range(16):
        part = place(i, None)
        pltpu.make_async_copy(part, part, wsem.at[i]).wait()

    def slot(s, carry):
        number = page_of[s]

        @pl.when(number < 0)
        def _():
            out_ref[s] = jnp.zeros(out_ref.shape[1:], BF)
            scale_ref[s] = jnp.zeros(scale_ref.shape[1:], F32)

        @pl.when(number >= 0)
        def _():
            at = pl.multiple_of(s // CAP * depth + number * page, page)
            rows = wv[pl.ds(at, page), :].astype(F32)
            for c in range(2):
                part = rows[:, c * 128 : (c + 1) * 128]
                most = jnp.max(jnp.max(jnp.abs(part), axis=0, keepdims=True), axis=1, keepdims=True)
                scale = (most + 1e-06).astype(BF).astype(F32)
                out_ref[s, c] = (part / scale).astype(BF)
                scale_ref[s, c : c + 1, :] = jnp.broadcast_to(scale, (1, 128))

        return carry

    lax.fori_loop(0, out_ref.shape[0], slot, 0)


def place_pages(keys, values, owners, zh, y, core, d):
    groups, count = owners.shape
    span = keys.shape[0]
    order = jnp.arange(count, dtype=jnp.int32)
    same = owners[:, :, None] == owners[:, None, :]
    rank = jnp.sum((same & (order[None, :] < order[:, None])[None]).astype(jnp.int32), axis=2)
    mine = (owners == d)[:, None, :] & (rank[:, None, :] == jnp.arange(CAP)[None, :, None])
    ids = jnp.max(jnp.where(mine, order[None, None, :], -1), axis=2).reshape(groups * CAP)
    whole, halves = gather_shards(jnp.concatenate([keys, values], axis=1), zh, y, core)
    ws, index = flat_shards(whole, halves)
    pages, scales = pl.pallas_call(
        functools.partial(place_kernel, count),
        in_specs=[smem()] * 2 + [hbm()] * 20,
        out_specs=[vmem()] * 2,
        out_shape=[
            jax.ShapeDtypeStruct((groups * CAP, 2, span // count, 128), BF),
            jax.ShapeDtypeStruct((groups * CAP, 2, 128), F32),
        ],
        scratch_shapes=[
            pltpu.VMEM((groups * span, 256), BF),
            pltpu.SemaphoreType.DMA((16,)),
        ],
        compiler_params=pltpu.CompilerParams(vmem_limit_bytes=24 * MB),
        cost_estimate=pl.CostEstimate(
            flops=4 * MB, bytes_accessed=8 * MB, transcendentals=0
        ),
        name="place",
    )(index, ids, *ws)
    return pages[None], scales[None, :, :, :1].astype(BF), ids[None]


def rope_tables(positions, width):
    half = width // 2
    steps = jnp.arange(half, dtype=F32) * (2.0 / width)
    freqs = jnp.exp(-math.log(THETA) * steps)
    angles = positions.astype(F32)[:, None] * freqs[None, :]
    cosine, sine = jnp.cos(angles), jnp.sin(angles)
    return (
        jnp.concatenate([cosine, cosine], axis=1),
        jnp.concatenate([-sine, sine], axis=1),
    )


def body(
    hidden_in, norm_gain, w_query, w_key, w_value, w_out, cache_k, cache_v, prefix_len, page_owner
):
    t, d = lax.axis_index("tensor"), lax.axis_index("decode")
    z, x = t // 4, t % 4
    zh, y, core = d // 8, d // 2 % 4, d % 2
    span = hidden_in.shape[1] * 8
    width = cache_k.shape[-1]
    owners = lax.all_gather(page_owner, "decode", axis=0, tiled=True)
    rows = hidden_in[0].astype(F32)
    mean_sq = jnp.mean(rows * rows, axis=1, keepdims=True)
    normed = (rows * lax.rsqrt(mean_sq + EPS) * norm_gain).astype(BF)
    weights = gather_shards(
        jnp.concatenate([w_query, w_key, w_value], axis=1), zh, y, core
    )
    pieces = gather_rows(normed, z, x)
    i = jnp.arange(span, dtype=jnp.int32)
    true_row = i % (span // 2) // 32 * 64 + i // (span // 2) * 32 + i % 32
    cosine, sine = rope_tables(prefix_len[0] + true_row, width)
    queries, keys, values = project(pieces, *weights, cosine, sine, span)
    depth, cols = w_out.shape
    quarters = w_out.reshape(depth, 4, cols // 4).transpose(1, 0, 2)
    quarters = lax.all_to_all(
        quarters, "tensor", 0, 0, axis_index_groups=X_GROUPS, tiled=True
    )
    out_weights = gather_shards(quarters.reshape(4 * depth, cols // 4), zh, y, core)
    parts = []
    for chunk in range(2):
        attended = attend(chunk, queries, cache_k[0, 0], cache_v[0, 0], keys, values, prefix_len)
        send, keep = output(attended, *out_weights, z, x)
        summed = (keep + to_t(send, Z_SWAP).astype(F32)).astype(BF)
        back = lax.all_to_all(
            summed, "tensor", 0, 0, axis_index_groups=X_GROUPS, tiled=True
        )
        back = back.reshape(4, 32, 16, cols // 4).transpose(1, 2, 0, 3)
        parts.append(back.reshape(32, 16 * cols))
    attn_out = jnp.concatenate(parts, axis=0)[None]
    placed = place_pages(keys, values, owners, zh, y, core, d)
    return (attn_out, *placed)


def solution(mesh):
    in_specs = (
        P("decode", "tensor", None),
        P(),
        P("decode", "tensor"),
        P("decode", "tensor"),
        P("decode", "tensor"),
        P("tensor", "decode"),
        P("decode", "tensor", None, None),
        P("decode", "tensor", None, None),
        P("decode"),
        P("decode", None),
    )
    out_specs = (
        P("decode", "tensor", None),
        P("decode", None, None, None, "tensor"),
        P("decode", None, None, "tensor"),
        P("decode", None),
    )
    return jax.shard_map(body, mesh=mesh, in_specs=in_specs, out_specs=out_specs, check_vma=False)
```

time: 540 us -> 362 us (0.67)
  waiting for transfers between devices: 347 us -> 54.9 us
  starting transfers between devices: 11.5 us -> 123 us
  matrix products: 110 us -> 0 us
  Pallas kernels: 0 us -> 64.4 us
  local copies, waits for them, and re-layouts: 9.59 us -> 57.1 us
  blocking collectives: 0 us -> 45.8 us
  other arithmetic: 40.7 us -> 7.21 us
  between operations: 15.3 us -> 2.64 us
    all_gather x5 -> x0, waiting for transfers between devices: 249 us -> none  [the longest x1 92.4 us: body(): gathered = lax.all_gather(normed, 'tensor', axis=0, tiled=True)]
    ppermute x0 -> x78, starting transfers between devices: none -> 114 us  [the longest x57 84.8 us: to_d(): return lax.ppermute(value, 'decode', pairs)]
    dot_general x14 -> x0, matrix products: 110 us -> none  [the longest x4 43.9 us: attend_head(): scores = jnp.dot(query, keys.T, preferred_element_type=jnp.float32) * factor]
    all_to_all x3 -> x2, waiting for transfers between devices: 95.6 us -> 4.36 us  [body(): lax.all_to_all(summed, 'tensor', 0, 0, axis_index_groups=X_GROUPS, tiled=...]
    pallas_call x0 -> x6, Pallas kernels: none -> 64.4 us  [the longest x2 28.8 us: attend(): pl.pallas_call(functools.partial(attend_kernel, chunk, block), grid=(head...]
    ppermute x0 -> x78, waiting for transfers between devices: none -> 50.5 us  [the longest x57 35.6 us: to_d(): return lax.ppermute(value, 'decode', pairs)]
    unnamed x26 -> x167, local copies, waits for them, and re-layouts: 6.74 us -> 42.5 us
    reduce_sum x6 -> x1, other arithmetic: 35 us -> 0.09 us  [place_pages(): jnp.sum((same & (order[None, :] < order[:, None])[None]).astype(jnp.int32...]
  transfers between devices with their start and end apart: 9 -> 80, of which waited for: 7 -> 13; matrix products, arithmetic and copies ran while one was open for 27% -> 6% of each run, Pallas kernels for 0% -> 18%
where the time goes in v1:
time: 362 us; the launch traced here: 355 us
  starting transfers between devices  123 us (34%)
  Pallas kernels  64.4 us (18%)
  local copies, waits for them, and re-layouts  57.1 us (16%)
  waiting for transfers between devices  54.9 us (15%)
  blocking collectives  45.8 us (13%)
  other arithmetic  7.21 us (2%)
    ppermute x57, starting transfers between devices, to_d(): return lax.ppermute(value, 'decode', pairs)  84.8 us
    unnamed x167, local copies, waits for them, and re-layouts  42.5 us
    ppermute x57, waiting for transfers between devices, to_d(): return lax.ppermute(value, 'decode', pairs)  35.6 us
    ppermute x21, starting transfers between devices, to_t(): return lax.ppermute(value, 'tensor', pairs)  29.6 us
    pallas_call x2, Pallas kernels, attend(): pl.pallas_call(functools.partial(attend_kernel, chunk, block), grid=(head...  28.8 us
    all_to_all x1, blocking collectives, body(): lax.all_to_all(quarters, 'tensor', 0, 0, axis_index_groups=X_GROUPS, tile...  24.8 us
    all_gather x1, blocking collectives, body(): owners = lax.all_gather(page_owner, 'decode', axis=0, tiled=True)  21 us
    pallas_call x1, Pallas kernels, project(): pl.pallas_call(functools.partial(project_kernel, n, scale), in_specs=[sme...  16.1 us
  transfers between devices with their start and end apart: 80, of which 13 were waited for; matrix products, arithmetic and copies ran while one was open for 6% of the time, Pallas kernels for 18%

profile of v1, /device:TPU:1, one launch (start us, length us, event | category | flops | bytes accessed | tf_op | source)
XLA Modules:
  0.0 354.8 jit_solution(3354144190268777353)
XLA Ops:
  0.7 1.2 constant_dynamic-update-slice_fusion.2
  3.8 4.5 %collective-permute-start.11 = (bf16[512,768]{1,0:T(8,128)(2,1)S(1)}, bf16[512,768]{1,0:T(8,128)(2,1)S(1)}, u32[]{:S(2)}, u32[]{:S(2)}) collective-permute-start(bf16[512,768]{1,0:T(8,128)(2,1)S(1)} %constant_dynamic-update-slice_fusion.refs_12_), channel_id=1, source_target_pairs={{0,8},{1,9},{2,10},{3,11},{4,12},{5,13},{6,14},{7,15},{8,0},{9,1},... | collective-permute-start | bytes 2359304 | tf_op jit(solution)/shard_map/ppermute | solution.py:53
  8.3 1.3 collective-permute-start.12
  10.2 1.3 collective-permute-start
  11.5 1.4 collective-permute-start.13
  12.9 1.7 collective-permute-start.16
  14.7 10.9 %collective-permute-done.11.refs_13_ = bf16[512,768]{1,0:T(8,128)(2,1)S(1)} collective-permute-done((bf16[512,768]{1,0:T(8,128)(2,1)S(1)}, bf16[512,768]{1,0:T(8,128)(2,1)S(1)}, u32[]{:S(2)}, u32[]{:S(2)}) %collective-permute-start.11) | collective-permute-done | bytes 786464 | tf_op jit(solution)/shard_map/ppermute | solution.py:53
  25.5 2.5 collective-permute-start.1
  28.8 24.8 %all_to_all.23 = bf16[4,512,128]{2,1,0:T(8,128)(2,1)S(1)} all-to-all(bf16[4,512,128]{2,1,0:T(8,128)(2,1)S(1)} %bitcast_bitcast_fusion), channel_id=1, replica_groups={{0,16,32,48},{64,80,96,112},{1,17,33,49},{65,81,97,113},{2,18,34,50},{6..., dimensions={0} | all-to-all | bytes 1048576 | tf_op jit(solution)/shard_map/all_to_all | solution.py:501
  53.6 2.6 collective-permute-start.34
  57.0 1.3 collective-permute-start.35
  58.3 1.5 collective-permute-start.36
  59.9 5.1 %collective-permute-done.34.refs_1_ = bf16[2048,128]{1,0:T(8,128)(2,1)S(1)} collective-permute-done((bf16[2048,128]{1,0:T(8,128)(2,1)S(1)}, bf16[2048,128]{1,0:T(8,128)(2,1)S(1)}, u32[]{:S(2)}, u32[]{:S(2)}) %collective-permute-start.34) | collective-permute-done | bytes 524320 | tf_op jit(solution)/shard_map/ppermute | solution.py:53
  65.1 1.3 collective-permute-start.22
  66.4 1.6 collective-permute-done.35.refs_2_
  68.0 1.4 collective-permute-start.23
  69.4 2.6 collective-permute-start.38
  73.0 4.6 %collective-permute-done.22.refs_24_ = bf16[256,768]{1,0:T(8,128)(2,1)S(1)} collective-permute-done((bf16[256,768]{1,0:T(8,128)(2,1)S(1)}, bf16[256,768]{1,0:T(8,128)(2,1)S(1)}, u32[]{:S(2)}, u32[]{:S(2)}) %collective-permute-start.22) | collective-permute-done | bytes 393248 | tf_op jit(solution)/shard_map/ppermute | solution.py:53
  77.5 3.8 %collective-permute-start.4 = (bf16[32,8192]{1,0:T(8,128)(2,1)S(1)}, bf16[32,8192]{1,0:T(8,128)(2,1)}, u32[]{:S(2)}, u32[]{:S(2)}) collective-permute-start(bf16[32,8192]{1,0:T(8,128)(2,1)S(1)} %get-tuple-element.23), channel_id=1, source_target_pairs={{0,16},{16,32},{32,48},{48,0},{64,80},{80,96},{96,112},{112,64},{1... | collective-permute-start | bytes 1572872 | tf_op jit(solution)/shard_map/ppermute | solution.py:49
  82.0 6.9 %collective-permute-done.37.refs_4_ = bf16[2048,128]{1,0:T(8,128)(2,1)S(1)} collective-permute-done((bf16[2048,128]{1,0:T(8,128)(2,1)S(1)}, bf16[2048,128]{1,0:T(8,128)(2,1)S(1)}, u32[]{:S(2)}, u32[]{:S(2)}) %collective-permute-start.37) | collective-permute-done | bytes 524320 | tf_op jit(solution)/shard_map/ppermute | solution.py:53
  89.3 3.8 %collective-permute-start.7 = (bf16[32,8192]{1,0:T(8,128)(2,1)S(1)}, bf16[32,8192]{1,0:T(8,128)(2,1)S(1)}, u32[]{:S(2)}, u32[]{:S(2)}) collective-permute-start(bf16[32,8192]{1,0:T(8,128)(2,1)S(1)} %slice.87), channel_id=1, source_target_pairs={{0,16},{16,32},{32,48},{48,0},{64,80},{80,96},{96,112},{112,64},{1... | collective-permute-start | bytes 1572872 | tf_op jit(solution)/shard_map/ppermute | solution.py:49
  93.3 2.6 collective-permute-start.15
  95.9 3.0 collective-permute-done.6.refs_7_
  98.9 5.2 %collective-permute-start.17 = (bf16[512,768]{1,0:T(8,128)(2,1)S(1)}, bf16[512,768]{1,0:T(8,128)(2,1)S(1)}, u32[]{:S(2)}, u32[]{:S(2)}) collective-permute-start(bf16[512,768]{1,0:T(8,128)(2,1)S(1)} %collective-permute-done.11.refs_13_), channel_id=1, source_target_pairs={{0,1},{1,0},{2,3},{3,2},{4,5},{5,4},{6,7},{7,6},{8,9},{9,8},{10,11... | collective-permute-start | bytes 2359304 | tf_op jit(solution)/shard_map/ppermute | solution.py:53
  104.9 1.9 collective-permute-start.18
  107.6 1.5 collective-permute-start.19
  109.7 4.8 %collective-permute-start.26 = (bf16[256,768]{1,0:T(8,128)(2,1)S(1)}, bf16[256,768]{1,0:T(8,128)(2,1)S(1)}, u32[]{:S(2)}, u32[]{:S(2)}) collective-permute-start(bf16[256,768]{1,0:T(8,128)(2,1)S(1)} %collective-permute-done.22.refs_24_), channel_id=1, source_target_pairs={{0,1},{1,0},{2,3},{3,2},{4,5},{5,4},{6,7},{7,6},{8,9},{9,8},{10,11... | collective-permute-start | bytes 1179656 | tf_op jit(solution)/shard_map/ppermute | solution.py:53
  115.4 2.5 collective-permute-start.9
  119.0 1.2 slice.94
  120.2 3.6 %collective-permute-start.25 = (bf16[256,768]{1,0:T(8,128)(2,1)S(1)}, bf16[256,768]{1,0:T(8,128)(2,1)}, u32[]{:S(2)}, u32[]{:S(2)}) collective-permute-start(bf16[256,768]{1,0:T(8,128)(2,1)S(1)} %slice.94), channel_id=1, source_target_pairs={{0,6},{1,7},{2,0},{3,1},{4,2},{5,3},{6,4},{7,5},{8,14},{9,15},{10,... | collective-permute-start | bytes 1179656 | tf_op jit(solution)/shard_map/ppermute | solution.py:53
  126.9 5.0 %collective-permute-done.24.refs_26_ = bf16[256,768]{1,0:T(8,128)(2,1)} collective-permute-done((bf16[256,768]{1,0:T(8,128)(2,1)S(1)}, bf16[256,768]{1,0:T(8,128)(2,1)}, u32[]{:S(2)}, u32[]{:S(2)}) %collective-permute-start.24) | collective-permute-done | bytes 393248 | tf_op jit(solution)/shard_map/ppermute | solution.py:53
  137.2 8.8 %collective-permute-done.10.refs_11_ = bf16[32,8192]{1,0:T(8,128)(2,1)} collective-permute-done((bf16[32,8192]{1,0:T(8,128)(2,1)}, bf16[32,8192]{1,0:T(8,128)(2,1)}, u32[]{:S(2)}, u32[]{:S(2)}) %collective-permute-start.10) | collective-permute-done | bytes 524320 | tf_op jit(solution)/shard_map/ppermute | solution.py:49
  146.1 1.7 collective-permute-start.39
  158.8 16.1 %project.1 = (bf16[4,512,128]{2,1,0:T(8,128)(2,1)S(1)}, bf16[512,128]{1,0:T(8,128)(2,1)S(1)}, bf16[512,128]{1,0:T(8,128)(2,1)S(1)}) custom-call(s32[24]{0:T(128)S(1)} %stack.221.x_at, s32[16]{0:T(128)S(1)} %stack.99.w_at, f32[512,128]{1,0:T(8,128)S(1)} %get-tuple-element.27.cos_ref, f32[512,128]{1,0:T(8,128)S(1)} %get-tuple-element.28.sin_ref, ...), custom_call_target="tpu_custom_call" | custom-call | flops 6442450944 | bytes 25165824 | tf_op jit(solution)/shard_map/project/pallas_call | solution.py:225
  174.9 2.8 collective-permute-start.46
  177.8 14.7 %attend.3.a0 = bf16[256,512]{1,0:T(8,128)(2,1)} custom-call(s32[1]{0:T(128)} %copy.56.live_ref, bf16[4,512,128]{2,1,0:T(8,128)(2,1)S(1)} %get-tuple-element.13.q_ref, bf16[8192,128]{1,0:T(8,128)(2,1)S(1)} %bitcast.82, bf16[8192,128]{1,0:T(8,128)(2,1)S(1)} %bitcast.84, bf16[512,128]{1,0:T(8,128)(2,1)S(1)} %get-tuple-element.14.kn_ref, ...), custom_call_target="tpu_custom_call" | custom-call | flops 4563402752 | bytes 4194304 | tf_op jit(solution)/shard_map/attend/pallas_call | solution.py:296
  193.5 4.1 %collective-permute-start.48 = (bf16[1024,128]{1,0:T(8,128)(2,1)}, bf16[1024,128]{1,0:T(8,128)(2,1)}, u32[]{:S(2)}, u32[]{:S(2)}) collective-permute-start(bf16[1024,128]{1,0:T(8,128)(2,1)} %slice.100), channel_id=1, source_target_pairs={{0,6},{1,7},{2,0},{3,1},{4,2},{5,3},{6,4},{7,5},{8,14},{9,15},{10,... | collective-permute-start | bytes 786440 | tf_op jit(solution)/shard_map/ppermute | solution.py:53
  199.2 2.7 collective-permute-start.55
  204.5 3.0 collective-permute-done.54.a1
  207.5 1.2 collective-permute-start.51
  208.7 8.6 %collective-permute-start.52 = (bf16[1024,128]{1,0:T(8,128)(2,1)}, bf16[1024,128]{1,0:T(8,128)(2,1)S(1)}, u32[]{:S(2)}, u32[]{:S(2)}) collective-permute-start(bf16[1024,128]{1,0:T(8,128)(2,1)} %collective-permute-done.48.refs_15_), channel_id=1, source_target_pairs={{0,1},{1,0},{2,3},{3,2},{4,5},{5,4},{6,7},{7,6},{8,9},{9,8},{10,11... | collective-permute-start | bytes 786440 | tf_op jit(solution)/shard_map/ppermute | solution.py:53
  218.2 1.6 copy-done.42
  219.8 1.6 copy-done.44
  222.4 14.1 %attend.2.a0 = bf16[256,512]{1,0:T(8,128)(2,1)S(1)} custom-call(s32[1]{0:T(128)} %copy.56.live_ref, bf16[4,512,128]{2,1,0:T(8,128)(2,1)S(1)} %copy-done.70, bf16[8192,128]{1,0:T(8,128)(2,1)S(1)} %bitcast.83, bf16[8192,128]{1,0:T(8,128)(2,1)S(1)} %bitcast.85, bf16[512,128]{1,0:T(8,128)(2,1)S(1)} %copy-done.40, bf16[512,128]{1,0:T(8,128)(2,1)S(1)} %get-tuple-element.15.vn_ref), custom_call_target="tpu_custom_call" | custom-call | flops 4563402752 | bytes 4194304 | tf_op jit(solution)/shard_map/attend/pallas_call | solution.py:296
  238.5 3.5 collective-permute-start.57
  243.3 2.7 collective-permute-start.31
  246.0 7.5 %collective-permute-start.59 = (bf16[512,256]{1,0:T(8,128)(2,1)}, bf16[512,256]{1,0:T(8,128)(2,1)}, u32[]{:S(2)}, u32[]{:S(2)}) collective-permute-start(bf16[512,256]{1,0:T(8,128)(2,1)} %constant_dynamic-update-slice_fusion.3.refs_0_), channel_id=1, source_target_pairs={{0,8},{1,9},{2,10},{3,11},{4,12},{5,13},{6,14},{7,15},{8,0},{9,1},... | collective-permute-start | bytes 786440 | tf_op jit(solution)/shard_map/ppermute | solution.py:53
  253.5 7.4 %output.3 = (bf16[128,2048]{1,0:T(8,128)(2,1)}, f32[128,2048]{1,0:T(8,128)S(1)}) custom-call(s32[5]{0:T(128)S(1)} %stack.82.x_at, s32[16]{0:T(128)S(1)} %stack.99.w_at, s32[1]{0:T(128)} %bitcast.20.z_at, bf16[256,512]{1,0:T(8,128)(2,1)} %attend.3.a0, bf16[256,512]{1,0:T(8,128)(2,1)} %collective-permute-done.54.a1, ...), custom_call_target="tpu_custom_call" | custom-call | flops 2147483648 | bytes 11534336 | tf_op jit(solution)/shard_map/output/pallas_call | solution.py:373
  262.0 2.7 collective-permute-start.33
  264.8 2.7 collective-permute-start.61
  267.5 2.7 collective-permute-start.63
  270.1 7.4 %output.2 = (bf16[128,2048]{1,0:T(8,128)(2,1)}, f32[128,2048]{1,0:T(8,128)S(1)}) custom-call(s32[5]{0:T(128)S(1)} %stack.82.x_at, s32[16]{0:T(128)S(1)} %stack.99.w_at, s32[1]{0:T(128)} %bitcast.20.z_at, bf16[256,512]{1,0:T(8,128)(2,1)S(1)} %attend.2.a0, bf16[256,512]{1,0:T(8,128)(2,1)S(1)} %collective-permute-done.30.a1, ...), custom_call_target="tpu_custom_call" | custom-call | flops 2147483648 | bytes 11534336 | tf_op jit(solution)/shard_map/output/pallas_call | solution.py:373
  278.5 1.5 collective-permute-start.53
  279.9 21.0 %all-gather = s32[16,1,4]{2,1,0:T(1,128)S(1)} all-gather(s32[1,1,4]{2,1,0:T(1,128)S(1)} %bitcast.92), channel_id=1, replica_groups=mesh['tensor'=8,'decode'=16] {'decode'}, dimensions={0}, use_global_device_ids=true | all-gather | bytes 272 | tf_op jit(solution)/shard_map/all_gather | solution.py:487
  304.5 2.7 collective-permute-start.71
  309.1 2.3 add_convert_fusion
  311.4 4.1 %all-to-all-start.2 = ((bf16[4,32,2048]{2,1,0:T(8,128)(2,1)}), bf16[4,32,2048]{2,1,0:T(8,128)(2,1)}, u32[]{:S(2)}, u32[]{:S(2)}) async-start(bf16[4,32,2048]{2,1,0:T(8,128)(2,1)} %bitcast.46), calls=%async_computation.2 | async-start | bytes 1048576 | tf_op jit(solution)/shard_map/all_to_all | solution.py:510
  316.1 1.9 add_convert_fusion.1
  318.2 2.7 collective-permute-start.73
  320.9 4.4 %all-to-all-done.2 = bf16[4,32,2048]{2,1,0:T(8,128)(2,1)} async-done(((bf16[4,32,2048]{2,1,0:T(8,128)(2,1)}), bf16[4,32,2048]{2,1,0:T(8,128)(2,1)}, u32[]{:S(2)}, u32[]{:S(2)}) %all-to-all-start.2) | async-done | bytes 524320 | tf_op jit(solution)/shard_map/all_to_all | solution.py:510
  325.2 4.1 %all-to-all-start.1 = ((bf16[4,32,2048]{2,1,0:T(8,128)(2,1)}), bf16[4,32,2048]{2,1,0:T(8,128)(2,1)}, u32[]{:S(2)}, u32[]{:S(2)}) async-start(bf16[4,32,2048]{2,1,0:T(8,128)(2,1)} %bitcast.90), calls=%async_computation.1 | async-start | bytes 1048576 | tf_op jit(solution)/shard_map/all_to_all | solution.py:510
  344.1 4.9 %place.1 = (bf16[32,2,128,128]{3,2,1,0:T(8,128)(2,1)}, f32[32,2,128]{2,1,0:T(2,128)S(1)}) custom-call(s32[16]{0:T(128)S(1)} %stack.99.w_at, s32[32]{0:T(128)S(1)} %reshape.134.page_of, bf16[512,256]{1,0:T(8,128)(2,1)} %constant_dynamic-update-slice_fusion.3.refs_0_, bf16[512,256]{1,0:T(8,128)(2,1)} %collective-permute-done.59.refs_1_, ...), custom_call_target="tpu_custom_call" | custom-call | flops 4194304 | bytes 8388608 | tf_op jit(solution)/shard_map/place/pallas_call | solution.py:446
  349.6 1.1 copy.47
  351.5 1.1 copy.46
  (320 shorter events, 65.5 us)
Async XLA Ops:
  3.8 21.8 %collective-permute-start.11 = (bf16[512,768]{1,0:T(8,128)(2,1)S(1)}, bf16[512,768]{1,0:T(8,128)(2,1)S(1)}, u32[]{:S(2)}, u32[]{:S(2)}) collective-permute-start(bf16[512,768]{1,0:T(8,128)(2,1)S(1)} %constant_dynamic-update-slice_fusion.refs_12_), channel_id=1, source_target_pairs={{0,8},{1,9},{2,10},{3,11},{4,12},{5,13},{6,14},{7,15},{8,0},{9,1},... | collective-permute-start | bytes 2359304 | tf_op jit(solution)/shard_map/ppermute | solution.py:53
  8.3 19.8 %collective-permute-start.12 = (bf16[512,768]{1,0:T(8,128)(2,1)S(1)}, bf16[512,768]{1,0:T(8,128)(2,1)S(1)}, u32[]{:S(2)}, u32[]{:S(2)}) collective-permute-start(bf16[512,768]{1,0:T(8,128)(2,1)S(1)} %constant_dynamic-update-slice_fusion.refs_12_), channel_id=1, source_target_pairs={{0,2},{1,3},{2,4},{3,5},{4,6},{5,7},{6,0},{7,1},{8,10},{9,11},{10,... | collective-permute-start | bytes 2359304 | tf_op jit(solution)/shard_map/ppermute | solution.py:53
  10.2 48.1 %collective-permute-start = (bf16[64,8192]{1,0:T(8,128)(2,1)S(1)}, bf16[64,8192]{1,0:T(8,128)(2,1)S(1)}, u32[]{:S(2)}, u32[]{:S(2)}) collective-permute-start(bf16[64,8192]{1,0:T(8,128)(2,1)S(1)} %fusion.2.refs_0_), channel_id=1, source_target_pairs={{0,16},{16,32},{32,48},{48,0},{64,80},{80,96},{96,112},{112,64},{1... | collective-permute-start | bytes 3145736 | tf_op jit(solution)/shard_map/ppermute | solution.py:49
  11.5 42.1 %collective-permute-start.13 = (bf16[512,768]{1,0:T(8,128)(2,1)S(1)}, bf16[512,768]{1,0:T(8,128)(2,1)S(1)}, u32[]{:S(2)}, u32[]{:S(2)}) collective-permute-start(bf16[512,768]{1,0:T(8,128)(2,1)S(1)} %constant_dynamic-update-slice_fusion.refs_12_), channel_id=1, source_target_pairs={{0,6},{1,7},{2,0},{3,1},{4,2},{5,3},{6,4},{7,5},{8,14},{9,15},{10,... | collective-permute-start | bytes 2359304 | tf_op jit(solution)/shard_map/ppermute | solution.py:53
  12.9 43.2 %collective-permute-start.16 = (bf16[512,768]{1,0:T(8,128)(2,1)S(1)}, bf16[512,768]{1,0:T(8,128)(2,1)S(1)}, u32[]{:S(2)}, u32[]{:S(2)}) collective-permute-start(bf16[512,768]{1,0:T(8,128)(2,1)S(1)} %constant_dynamic-update-slice_fusion.refs_12_), channel_id=1, source_target_pairs={{0,1},{1,0},{2,3},{3,2},{4,5},{5,4},{6,7},{7,6},{8,9},{9,8},{10,11... | collective-permute-start | bytes 2359304 | tf_op jit(solution)/shard_map/ppermute | solution.py:53
  25.5 43.9 %collective-permute-start.1 = (bf16[64,8192]{1,0:T(8,128)(2,1)S(1)}, bf16[64,8192]{1,0:T(8,128)(2,1)S(1)}, u32[]{:S(2)}, u32[]{:S(2)}) collective-permute-start(bf16[64,8192]{1,0:T(8,128)(2,1)S(1)} %fusion.2.refs_0_), channel_id=1, source_target_pairs={{0,48},{16,0},{32,16},{48,32},{64,112},{80,64},{96,80},{112,96},{1... | collective-permute-start | bytes 3145736 | tf_op jit(solution)/shard_map/ppermute | solution.py:49
  28.0 44.1 %collective-permute-start.2 = (bf16[64,8192]{1,0:T(8,128)(2,1)S(1)}, bf16[64,8192]{1,0:T(8,128)(2,1)S(1)}, u32[]{:S(2)}, u32[]{:S(2)}) collective-permute-start(bf16[64,8192]{1,0:T(8,128)(2,1)S(1)} %fusion.2.refs_0_), channel_id=1, source_target_pairs={{0,64},{16,80},{32,96},{48,112},{64,0},{80,16},{96,32},{112,48},{1... | collective-permute-start | bytes 3145736 | tf_op jit(solution)/shard_map/ppermute | solution.py:49
  53.6 11.5 %collective-permute-start.34 = (bf16[2048,128]{1,0:T(8,128)(2,1)S(1)}, bf16[2048,128]{1,0:T(8,128)(2,1)S(1)}, u32[]{:S(2)}, u32[]{:S(2)}) collective-permute-start(bf16[2048,128]{1,0:T(8,128)(2,1)S(1)} %bitcast.76), channel_id=1, source_target_pairs={{0,8},{1,9},{2,10},{3,11},{4,12},{5,13},{6,14},{7,15},{8,0},{9,1},... | collective-permute-start | bytes 1572872 | tf_op jit(solution)/shard_map/ppermute | solution.py:53
  65.1 12.5 %collective-permute-start.22 = (bf16[256,768]{1,0:T(8,128)(2,1)S(1)}, bf16[256,768]{1,0:T(8,128)(2,1)S(1)}, u32[]{:S(2)}, u32[]{:S(2)}) collective-permute-start(bf16[256,768]{1,0:T(8,128)(2,1)S(1)} %slice.91), channel_id=1, source_target_pairs={{0,2},{1,3},{2,4},{3,5},{4,6},{5,7},{6,0},{7,1},{8,10},{9,11},{10,... | collective-permute-start | bytes 1179656 | tf_op jit(solution)/shard_map/ppermute | solution.py:53
  68.0 13.4 %collective-permute-start.23 = (bf16[256,768]{1,0:T(8,128)(2,1)S(1)}, bf16[256,768]{1,0:T(8,128)(2,1)S(1)}, u32[]{:S(2)}, u32[]{:S(2)}) collective-permute-start(bf16[256,768]{1,0:T(8,128)(2,1)S(1)} %slice.92), channel_id=1, source_target_pairs={{0,6},{1,7},{2,0},{3,1},{4,2},{5,3},{6,4},{7,5},{8,14},{9,15},{10,... | collective-permute-start | bytes 1179656 | tf_op jit(solution)/shard_map/ppermute | solution.py:53
  69.4 19.5 %collective-permute-start.37 = (bf16[2048,128]{1,0:T(8,128)(2,1)S(1)}, bf16[2048,128]{1,0:T(8,128)(2,1)S(1)}, u32[]{:S(2)}, u32[]{:S(2)}) collective-permute-start(bf16[2048,128]{1,0:T(8,128)(2,1)S(1)} %collective-permute-done.34.refs_1_), channel_id=1, source_target_pairs={{0,2},{1,3},{2,4},{3,5},{4,6},{5,7},{6,0},{7,1},{8,10},{9,11},{10,... | collective-permute-start | bytes 1572872 | tf_op jit(solution)/shard_map/ppermute | solution.py:53
  69.4 19.8 %collective-permute-start.38 = (bf16[2048,128]{1,0:T(8,128)(2,1)S(1)}, bf16[2048,128]{1,0:T(8,128)(2,1)S(1)}, u32[]{:S(2)}, u32[]{:S(2)}) collective-permute-start(bf16[2048,128]{1,0:T(8,128)(2,1)S(1)} %collective-permute-done.34.refs_1_), channel_id=1, source_target_pairs={{0,6},{1,7},{2,0},{3,1},{4,2},{5,3},{6,4},{7,5},{8,14},{9,15},{10,... | collective-permute-start | bytes 1572872 | tf_op jit(solution)/shard_map/ppermute | solution.py:53
  72.1 21.0 %collective-permute-start.3 = (bf16[32,8192]{1,0:T(8,128)(2,1)S(1)}, bf16[32,8192]{1,0:T(8,128)(2,1)S(1)}, u32[]{:S(2)}, u32[]{:S(2)}) collective-permute-start(bf16[32,8192]{1,0:T(8,128)(2,1)S(1)} %slice.87), channel_id=1, source_target_pairs={{0,64},{16,80},{32,96},{48,112},{64,0},{80,16},{96,32},{112,48},{1... | collective-permute-start | bytes 1572872 | tf_op jit(solution)/shard_map/ppermute | solution.py:49
  77.5 15.7 %collective-permute-start.4 = (bf16[32,8192]{1,0:T(8,128)(2,1)S(1)}, bf16[32,8192]{1,0:T(8,128)(2,1)}, u32[]{:S(2)}, u32[]{:S(2)}) collective-permute-start(bf16[32,8192]{1,0:T(8,128)(2,1)S(1)} %get-tuple-element.23), channel_id=1, source_target_pairs={{0,16},{16,32},{32,48},{48,0},{64,80},{80,96},{96,112},{112,64},{1... | collective-permute-start | bytes 1572872 | tf_op jit(solution)/shard_map/ppermute | solution.py:49
  81.4 12.0 %collective-permute-start.5 = (bf16[32,8192]{1,0:T(8,128)(2,1)S(1)}, bf16[32,8192]{1,0:T(8,128)(2,1)S(1)}, u32[]{:S(2)}, u32[]{:S(2)}) collective-permute-start(bf16[32,8192]{1,0:T(8,128)(2,1)S(1)} %get-tuple-element.22), channel_id=1, source_target_pairs={{0,48},{16,0},{32,16},{48,32},{64,112},{80,64},{96,80},{112,96},{1... | collective-permute-start | bytes 1572872 | tf_op jit(solution)/shard_map/ppermute | solution.py:49
  89.3 14.8 %collective-permute-start.7 = (bf16[32,8192]{1,0:T(8,128)(2,1)S(1)}, bf16[32,8192]{1,0:T(8,128)(2,1)S(1)}, u32[]{:S(2)}, u32[]{:S(2)}) collective-permute-start(bf16[32,8192]{1,0:T(8,128)(2,1)S(1)} %slice.87), channel_id=1, source_target_pairs={{0,16},{16,32},{32,48},{48,0},{64,80},{80,96},{96,112},{112,64},{1... | collective-permute-start | bytes 1572872 | tf_op jit(solution)/shard_map/ppermute | solution.py:49
  93.1 13.7 %collective-permute-start.8 = (bf16[32,8192]{1,0:T(8,128)(2,1)S(1)}, bf16[32,8192]{1,0:T(8,128)(2,1)S(1)}, u32[]{:S(2)}, u32[]{:S(2)}) collective-permute-start(bf16[32,8192]{1,0:T(8,128)(2,1)S(1)} %slice.90), channel_id=1, source_target_pairs={{0,48},{16,0},{32,16},{48,32},{64,112},{80,64},{96,80},{112,96},{1... | collective-permute-start | bytes 1572872 | tf_op jit(solution)/shard_map/ppermute | solution.py:49
  93.2 16.5 %collective-permute-start.14 = (bf16[512,768]{1,0:T(8,128)(2,1)S(1)}, bf16[512,768]{1,0:T(8,128)(2,1)}, u32[]{:S(2)}, u32[]{:S(2)}) collective-permute-start(bf16[512,768]{1,0:T(8,128)(2,1)S(1)} %collective-permute-done.11.refs_13_), channel_id=1, source_target_pairs={{0,2},{1,3},{2,4},{3,5},{4,6},{5,7},{6,0},{7,1},{8,10},{9,11},{10,... | collective-permute-start | bytes 2359304 | tf_op jit(solution)/shard_map/ppermute | solution.py:53
  93.3 21.2 %collective-permute-start.15 = (bf16[512,768]{1,0:T(8,128)(2,1)S(1)}, bf16[512,768]{1,0:T(8,128)(2,1)}, u32[]{:S(2)}, u32[]{:S(2)}) collective-permute-start(bf16[512,768]{1,0:T(8,128)(2,1)S(1)} %collective-permute-done.11.refs_13_), channel_id=1, source_target_pairs={{0,6},{1,7},{2,0},{3,1},{4,2},{5,3},{6,4},{7,5},{8,14},{9,15},{10,... | collective-permute-start | bytes 2359304 | tf_op jit(solution)/shard_map/ppermute | solution.py:53
  98.9 15.6 %collective-permute-start.17 = (bf16[512,768]{1,0:T(8,128)(2,1)S(1)}, bf16[512,768]{1,0:T(8,128)(2,1)S(1)}, u32[]{:S(2)}, u32[]{:S(2)}) collective-permute-start(bf16[512,768]{1,0:T(8,128)(2,1)S(1)} %collective-permute-done.11.refs_13_), channel_id=1, source_target_pairs={{0,1},{1,0},{2,3},{3,2},{4,5},{5,4},{6,7},{7,6},{8,9},{9,8},{10,11... | collective-permute-start | bytes 2359304 | tf_op jit(solution)/shard_map/ppermute | solution.py:53
  104.9 13.9 %collective-permute-start.18 = (bf16[512,768]{1,0:T(8,128)(2,1)S(1)}, bf16[512,768]{1,0:T(8,128)(2,1)S(1)}, u32[]{:S(2)}, u32[]{:S(2)}) collective-permute-start(bf16[512,768]{1,0:T(8,128)(2,1)S(1)} %collective-permute-done.12.refs_14_), channel_id=1, source_target_pairs={{0,1},{1,0},{2,3},{3,2},{4,5},{5,4},{6,7},{7,6},{8,9},{9,8},{10,11... | collective-permute-start | bytes 2359304 | tf_op jit(solution)/shard_map/ppermute | solution.py:53
  107.6 12.6 %collective-permute-start.19 = (bf16[512,768]{1,0:T(8,128)(2,1)S(1)}, bf16[512,768]{1,0:T(8,128)(2,1)S(1)}, u32[]{:S(2)}, u32[]{:S(2)}) collective-permute-start(bf16[512,768]{1,0:T(8,128)(2,1)S(1)} %collective-permute-done.13.refs_15_), channel_id=1, source_target_pairs={{0,1},{1,0},{2,3},{3,2},{4,5},{5,4},{6,7},{7,6},{8,9},{9,8},{10,11... | collective-permute-start | bytes 2359304 | tf_op jit(solution)/shard_map/ppermute | solution.py:53
  109.7 14.2 %collective-permute-start.26 = (bf16[256,768]{1,0:T(8,128)(2,1)S(1)}, bf16[256,768]{1,0:T(8,128)(2,1)S(1)}, u32[]{:S(2)}, u32[]{:S(2)}) collective-permute-start(bf16[256,768]{1,0:T(8,128)(2,1)S(1)} %collective-permute-done.22.refs_24_), channel_id=1, source_target_pairs={{0,1},{1,0},{2,3},{3,2},{4,5},{5,4},{6,7},{7,6},{8,9},{9,8},{10,11... | collective-permute-start | bytes 1179656 | tf_op jit(solution)/shard_map/ppermute | solution.py:53
  115.4 17.8 %collective-permute-start.9 = (bf16[32,8192]{1,0:T(8,128)(2,1)S(1)}, bf16[32,8192]{1,0:T(8,128)(2,1)S(1)}, u32[]{:S(2)}, u32[]{:S(2)}) collective-permute-start(bf16[32,8192]{1,0:T(8,128)(2,1)S(1)} %collective-permute-done.5.refs_6_), channel_id=1, source_target_pairs={{0,48},{16,0},{32,16},{48,32},{64,112},{80,64},{96,80},{112,96},{1... | collective-permute-start | bytes 1572872 | tf_op jit(solution)/shard_map/ppermute | solution.py:49
  118.9 13.0 %collective-permute-start.24 = (bf16[256,768]{1,0:T(8,128)(2,1)S(1)}, bf16[256,768]{1,0:T(8,128)(2,1)}, u32[]{:S(2)}, u32[]{:S(2)}) collective-permute-start(bf16[256,768]{1,0:T(8,128)(2,1)S(1)} %slice.93), channel_id=1, source_target_pairs={{0,2},{1,3},{2,4},{3,5},{4,6},{5,7},{6,0},{7,1},{8,10},{9,11},{10,... | collective-permute-start | bytes 1179656 | tf_op jit(solution)/shard_map/ppermute | solution.py:53
  120.2 11.8 %collective-permute-start.25 = (bf16[256,768]{1,0:T(8,128)(2,1)S(1)}, bf16[256,768]{1,0:T(8,128)(2,1)}, u32[]{:S(2)}, u32[]{:S(2)}) collective-permute-start(bf16[256,768]{1,0:T(8,128)(2,1)S(1)} %slice.94), channel_id=1, source_target_pairs={{0,6},{1,7},{2,0},{3,1},{4,2},{5,3},{6,4},{7,5},{8,14},{9,15},{10,... | collective-permute-start | bytes 1179656 | tf_op jit(solution)/shard_map/ppermute | solution.py:53
  124.6 23.1 %collective-permute-start.20 = (bf16[512,768]{1,0:T(8,128)(2,1)}, bf16[512,768]{1,0:T(8,128)(2,1)}, u32[]{:S(2)}, u32[]{:S(2)}) collective-permute-start(bf16[512,768]{1,0:T(8,128)(2,1)} %collective-permute-done.14.refs_16_), channel_id=1, source_target_pairs={{0,1},{1,0},{2,3},{3,2},{4,5},{5,4},{6,7},{7,6},{8,9},{9,8},{10,11... | collective-permute-start | bytes 2359304 | tf_op jit(solution)/shard_map/ppermute | solution.py:53
  126.2 21.6 %collective-permute-start.21 = (bf16[512,768]{1,0:T(8,128)(2,1)}, bf16[512,768]{1,0:T(8,128)(2,1)}, u32[]{:S(2)}, u32[]{:S(2)}) collective-permute-start(bf16[512,768]{1,0:T(8,128)(2,1)} %collective-permute-done.15.refs_17_), channel_id=1, source_target_pairs={{0,1},{1,0},{2,3},{3,2},{4,5},{5,4},{6,7},{7,6},{8,9},{9,8},{10,11... | collective-permute-start | bytes 2359304 | tf_op jit(solution)/shard_map/ppermute | solution.py:53
  131.9 14.2 %collective-permute-start.10 = (bf16[32,8192]{1,0:T(8,128)(2,1)}, bf16[32,8192]{1,0:T(8,128)(2,1)}, u32[]{:S(2)}, u32[]{:S(2)}) collective-permute-start(bf16[32,8192]{1,0:T(8,128)(2,1)} %collective-permute-done.4.refs_5_), channel_id=1, source_target_pairs={{0,16},{16,32},{32,48},{48,0},{64,80},{80,96},{96,112},{112,64},{1... | collective-permute-start | bytes 1572872 | tf_op jit(solution)/shard_map/ppermute | solution.py:49
  132.1 15.8 %collective-permute-start.28 = (bf16[256,768]{1,0:T(8,128)(2,1)}, bf16[256,768]{1,0:T(8,128)(2,1)}, u32[]{:S(2)}, u32[]{:S(2)}) collective-permute-start(bf16[256,768]{1,0:T(8,128)(2,1)} %collective-permute-done.24.refs_26_), channel_id=1, source_target_pairs={{0,1},{1,0},{2,3},{3,2},{4,5},{5,4},{6,7},{7,6},{8,9},{9,8},{10,11... | collective-permute-start | bytes 1179656 | tf_op jit(solution)/shard_map/ppermute | solution.py:53
  134.0 14.4 %collective-permute-start.29 = (bf16[256,768]{1,0:T(8,128)(2,1)}, bf16[256,768]{1,0:T(8,128)(2,1)}, u32[]{:S(2)}, u32[]{:S(2)}) collective-permute-start(bf16[256,768]{1,0:T(8,128)(2,1)} %collective-permute-done.25.refs_27_), channel_id=1, source_target_pairs={{0,1},{1,0},{2,3},{3,2},{4,5},{5,4},{6,7},{7,6},{8,9},{9,8},{10,11... | collective-permute-start | bytes 1179656 | tf_op jit(solution)/shard_map/ppermute | solution.py:53
  146.1 28.8 %collective-permute-start.39 = (bf16[2048,128]{1,0:T(8,128)(2,1)S(1)}, bf16[2048,128]{1,0:T(8,128)(2,1)S(1)}, u32[]{:S(2)}, u32[]{:S(2)}) collective-permute-start(bf16[2048,128]{1,0:T(8,128)(2,1)S(1)} %bitcast.79), channel_id=1, source_target_pairs={{0,1},{1,0},{2,3},{3,2},{4,5},{5,4},{6,7},{7,6},{8,9},{9,8},{10,11... | collective-permute-start | bytes 1572872 | tf_op jit(solution)/shard_map/ppermute | solution.py:53
  147.7 44.7 %collective-permute-start.45 = (bf16[1024,128]{1,0:T(8,128)(2,1)S(1)}, bf16[1024,128]{1,0:T(8,128)(2,1)S(1)}, u32[]{:S(2)}, u32[]{:S(2)}) collective-permute-start(bf16[1024,128]{1,0:T(8,128)(2,1)S(1)} %slice.97), channel_id=1, source_target_pairs={{0,2},{1,3},{2,4},{3,5},{4,6},{5,7},{6,0},{7,1},{8,10},{9,11},{10,... | collective-permute-start | bytes 786440 | tf_op jit(solution)/shard_map/ppermute | solution.py:53
  147.8 44.9 %collective-permute-start.40 = (bf16[2048,128]{1,0:T(8,128)(2,1)S(1)}, bf16[2048,128]{1,0:T(8,128)(2,1)S(1)}, u32[]{:S(2)}, u32[]{:S(2)}) collective-permute-start(bf16[2048,128]{1,0:T(8,128)(2,1)S(1)} %copy-done.2), channel_id=1, source_target_pairs={{0,1},{1,0},{2,3},{3,2},{4,5},{5,4},{6,7},{7,6},{8,9},{9,8},{10,11... | collective-permute-start | bytes 1572872 | tf_op jit(solution)/shard_map/ppermute | solution.py:53
  147.9 49.8 %collective-permute-start.41 = (bf16[2048,128]{1,0:T(8,128)(2,1)S(1)}, bf16[2048,128]{1,0:T(8,128)(2,1)S(1)}, u32[]{:S(2)}, u32[]{:S(2)}) collective-permute-start(bf16[2048,128]{1,0:T(8,128)(2,1)S(1)} %collective-permute-done.35.refs_2_), channel_id=1, source_target_pairs={{0,1},{1,0},{2,3},{3,2},{4,5},{5,4},{6,7},{7,6},{8,9},{9,8},{10,11... | collective-permute-start | bytes 1572872 | tf_op jit(solution)/shard_map/ppermute | solution.py:53
  148.4 50.1 %collective-permute-start.42 = (bf16[2048,128]{1,0:T(8,128)(2,1)S(1)}, bf16[2048,128]{1,0:T(8,128)(2,1)S(1)}, u32[]{:S(2)}, u32[]{:S(2)}) collective-permute-start(bf16[2048,128]{1,0:T(8,128)(2,1)S(1)} %collective-permute-done.36.refs_3_), channel_id=1, source_target_pairs={{0,1},{1,0},{2,3},{3,2},{4,5},{5,4},{6,7},{7,6},{8,9},{9,8},{10,11... | collective-permute-start | bytes 1572872 | tf_op jit(solution)/shard_map/ppermute | solution.py:53
  174.9 17.7 %collective-permute-start.46 = (bf16[1024,128]{1,0:T(8,128)(2,1)S(1)}, bf16[1024,128]{1,0:T(8,128)(2,1)S(1)}, u32[]{:S(2)}, u32[]{:S(2)}) collective-permute-start(bf16[1024,128]{1,0:T(8,128)(2,1)S(1)} %slice.98), channel_id=1, source_target_pairs={{0,6},{1,7},{2,0},{3,1},{4,2},{5,3},{6,4},{7,5},{8,14},{9,15},{10,... | collective-permute-start | bytes 786440 | tf_op jit(solution)/shard_map/ppermute | solution.py:53
  192.6 11.1 %collective-permute-start.47 = (bf16[1024,128]{1,0:T(8,128)(2,1)}, bf16[1024,128]{1,0:T(8,128)(2,1)}, u32[]{:S(2)}, u32[]{:S(2)}) collective-permute-start(bf16[1024,128]{1,0:T(8,128)(2,1)} %slice.99), channel_id=1, source_target_pairs={{0,2},{1,3},{2,4},{3,5},{4,6},{5,7},{6,0},{7,1},{8,10},{9,11},{10,... | collective-permute-start | bytes 786440 | tf_op jit(solution)/shard_map/ppermute | solution.py:53
  202.0 36.3 %collective-permute-start.50 = (bf16[1024,128]{1,0:T(8,128)(2,1)}, bf16[1024,128]{1,0:T(8,128)(2,1)S(1)}, u32[]{:S(2)}, u32[]{:S(2)}) collective-permute-start(bf16[1024,128]{1,0:T(8,128)(2,1)} %copy-done.12), channel_id=1, source_target_pairs={{0,1},{1,0},{2,3},{3,2},{4,5},{5,4},{6,7},{7,6},{8,9},{9,8},{10,11... | collective-permute-start | bytes 786440 | tf_op jit(solution)/shard_map/ppermute | solution.py:53
  203.7 39.6 %collective-permute-start.43 = (bf16[2048,128]{1,0:T(8,128)(2,1)S(1)}, bf16[2048,128]{1,0:T(8,128)(2,1)S(1)}, u32[]{:S(2)}, u32[]{:S(2)}) collective-permute-start(bf16[2048,128]{1,0:T(8,128)(2,1)S(1)} %collective-permute-done.37.refs_4_), channel_id=1, source_target_pairs={{0,1},{1,0},{2,3},{3,2},{4,5},{5,4},{6,7},{7,6},{8,9},{9,8},{10,11... | collective-permute-start | bytes 1572872 | tf_op jit(solution)/shard_map/ppermute | solution.py:53
  204.4 41.6 %collective-permute-start.44 = (bf16[2048,128]{1,0:T(8,128)(2,1)S(1)}, bf16[2048,128]{1,0:T(8,128)(2,1)S(1)}, u32[]{:S(2)}, u32[]{:S(2)}) collective-permute-start(bf16[2048,128]{1,0:T(8,128)(2,1)S(1)} %collective-permute-done.38.refs_5_), channel_id=1, source_target_pairs={{0,1},{1,0},{2,3},{3,2},{4,5},{5,4},{6,7},{7,6},{8,9},{9,8},{10,11... | collective-permute-start | bytes 1572872 | tf_op jit(solution)/shard_map/ppermute | solution.py:53
  207.5 31.0 %collective-permute-start.51 = (bf16[1024,128]{1,0:T(8,128)(2,1)}, bf16[1024,128]{1,0:T(8,128)(2,1)S(1)}, u32[]{:S(2)}, u32[]{:S(2)}) collective-permute-start(bf16[1024,128]{1,0:T(8,128)(2,1)} %collective-permute-done.47.refs_14_), channel_id=1, source_target_pairs={{0,1},{1,0},{2,3},{3,2},{4,5},{5,4},{6,7},{7,6},{8,9},{9,8},{10,11... | collective-permute-start | bytes 786440 | tf_op jit(solution)/shard_map/ppermute | solution.py:53
  208.7 34.6 %collective-permute-start.52 = (bf16[1024,128]{1,0:T(8,128)(2,1)}, bf16[1024,128]{1,0:T(8,128)(2,1)S(1)}, u32[]{:S(2)}, u32[]{:S(2)}) collective-permute-start(bf16[1024,128]{1,0:T(8,128)(2,1)} %collective-permute-done.48.refs_15_), channel_id=1, source_target_pairs={{0,1},{1,0},{2,3},{3,2},{4,5},{5,4},{6,7},{7,6},{8,9},{9,8},{10,11... | collective-permute-start | bytes 786440 | tf_op jit(solution)/shard_map/ppermute | solution.py:53
  238.4 15.1 %collective-permute-start.56 = (bf16[128,512]{1,0:T(8,128)(2,1)S(1)}, bf16[128,512]{1,0:T(8,128)(2,1)S(1)}, u32[]{:S(2)}, u32[]{:S(2)}) collective-permute-start(bf16[128,512]{1,0:T(8,128)(2,1)S(1)} %slice.101), channel_id=1, source_target_pairs={{0,16},{16,32},{32,48},{48,0},{64,80},{80,96},{96,112},{112,64},{1... | collective-permute-start | bytes 393224 | tf_op jit(solution)/shard_map/ppermute | solution.py:49
  238.5 15.0 %collective-permute-start.57 = (bf16[128,512]{1,0:T(8,128)(2,1)S(1)}, bf16[128,512]{1,0:T(8,128)(2,1)S(1)}, u32[]{:S(2)}, u32[]{:S(2)}) collective-permute-start(bf16[128,512]{1,0:T(8,128)(2,1)S(1)} %slice.102), channel_id=1, source_target_pairs={{0,48},{16,0},{32,16},{48,32},{64,112},{80,64},{96,80},{112,96},{1... | collective-permute-start | bytes 393224 | tf_op jit(solution)/shard_map/ppermute | solution.py:49
  243.3 18.6 %collective-permute-start.30 = (bf16[256,512]{1,0:T(8,128)(2,1)S(1)}, bf16[256,512]{1,0:T(8,128)(2,1)S(1)}, u32[]{:S(2)}, u32[]{:S(2)}) collective-permute-start(bf16[256,512]{1,0:T(8,128)(2,1)S(1)} %attend.2.a0), channel_id=1, source_target_pairs={{0,16},{16,32},{32,48},{48,0},{64,80},{80,96},{96,112},{112,64},{1... | collective-permute-start | bytes 786440 | tf_op jit(solution)/shard_map/ppermute | solution.py:49
  243.3 18.7 %collective-permute-start.31 = (bf16[256,512]{1,0:T(8,128)(2,1)S(1)}, bf16[256,512]{1,0:T(8,128)(2,1)S(1)}, u32[]{:S(2)}, u32[]{:S(2)}) collective-permute-start(bf16[256,512]{1,0:T(8,128)(2,1)S(1)} %attend.2.a0), channel_id=1, source_target_pairs={{0,48},{16,0},{32,16},{48,32},{64,112},{80,64},{96,80},{112,96},{1... | collective-permute-start | bytes 786440 | tf_op jit(solution)/shard_map/ppermute | solution.py:49
  246.0 18.8 %collective-permute-start.59 = (bf16[512,256]{1,0:T(8,128)(2,1)}, bf16[512,256]{1,0:T(8,128)(2,1)}, u32[]{:S(2)}, u32[]{:S(2)}) collective-permute-start(bf16[512,256]{1,0:T(8,128)(2,1)} %constant_dynamic-update-slice_fusion.3.refs_0_), channel_id=1, source_target_pairs={{0,8},{1,9},{2,10},{3,11},{4,12},{5,13},{6,14},{7,15},{8,0},{9,1},... | collective-permute-start | bytes 786440 | tf_op jit(solution)/shard_map/ppermute | solution.py:53
  261.9 46.3 %collective-permute-start.58 = (bf16[128,2048]{1,0:T(8,128)(2,1)}, bf16[128,2048]{1,0:T(8,128)(2,1)}, u32[]{:S(2)}, u32[]{:S(2)}) collective-permute-start(bf16[128,2048]{1,0:T(8,128)(2,1)} %get-tuple-element.19), channel_id=1, source_target_pairs={{0,64},{16,80},{32,96},{48,112},{64,0},{80,16},{96,32},{112,48},{1... | collective-permute-start | bytes 1572872 | tf_op jit(solution)/shard_map/ppermute | solution.py:49
  264.8 13.7 %collective-permute-start.60 = (bf16[512,256]{1,0:T(8,128)(2,1)}, bf16[512,256]{1,0:T(8,128)(2,1)}, u32[]{:S(2)}, u32[]{:S(2)}) collective-permute-start(bf16[512,256]{1,0:T(8,128)(2,1)} %constant_dynamic-update-slice_fusion.3.refs_0_), channel_id=1, source_target_pairs={{0,2},{1,3},{2,4},{3,5},{4,6},{5,7},{6,0},{7,1},{8,10},{9,11},{10,... | collective-permute-start | bytes 786440 | tf_op jit(solution)/shard_map/ppermute | solution.py:53
  264.8 37.3 %collective-permute-start.61 = (bf16[512,256]{1,0:T(8,128)(2,1)}, bf16[512,256]{1,0:T(8,128)(2,1)}, u32[]{:S(2)}, u32[]{:S(2)}) collective-permute-start(bf16[512,256]{1,0:T(8,128)(2,1)} %constant_dynamic-update-slice_fusion.3.refs_0_), channel_id=1, source_target_pairs={{0,6},{1,7},{2,0},{3,1},{4,2},{5,3},{6,4},{7,5},{8,14},{9,15},{10,... | collective-permute-start | bytes 786440 | tf_op jit(solution)/shard_map/ppermute | solution.py:53
  267.4 35.8 %collective-permute-start.62 = (bf16[512,256]{1,0:T(8,128)(2,1)}, bf16[512,256]{1,0:T(8,128)(2,1)}, u32[]{:S(2)}, u32[]{:S(2)}) collective-permute-start(bf16[512,256]{1,0:T(8,128)(2,1)} %collective-permute-done.59.refs_1_), channel_id=1, source_target_pairs={{0,2},{1,3},{2,4},{3,5},{4,6},{5,7},{6,0},{7,1},{8,10},{9,11},{10,... | collective-permute-start | bytes 786440 | tf_op jit(solution)/shard_map/ppermute | solution.py:53
  267.5 37.1 %collective-permute-start.63 = (bf16[512,256]{1,0:T(8,128)(2,1)}, bf16[512,256]{1,0:T(8,128)(2,1)}, u32[]{:S(2)}, u32[]{:S(2)}) collective-permute-start(bf16[512,256]{1,0:T(8,128)(2,1)} %collective-permute-done.59.refs_1_), channel_id=1, source_target_pairs={{0,6},{1,7},{2,0},{3,1},{4,2},{5,3},{6,4},{7,5},{8,14},{9,15},{10,... | collective-permute-start | bytes 786440 | tf_op jit(solution)/shard_map/ppermute | solution.py:53
  278.5 37.1 %collective-permute-start.53 = (bf16[128,2048]{1,0:T(8,128)(2,1)}, bf16[128,2048]{1,0:T(8,128)(2,1)}, u32[]{:S(2)}, u32[]{:S(2)}) collective-permute-start(bf16[128,2048]{1,0:T(8,128)(2,1)} %get-tuple-element.17), channel_id=1, source_target_pairs={{0,64},{16,80},{32,96},{48,112},{64,0},{80,16},{96,32},{112,48},{1... | collective-permute-start | bytes 1572872 | tf_op jit(solution)/shard_map/ppermute | solution.py:49
  302.1 13.4 %collective-permute-start.64 = (bf16[512,256]{1,0:T(8,128)(2,1)}, bf16[512,256]{1,0:T(8,128)(2,1)S(1)}, u32[]{:S(2)}, u32[]{:S(2)}) collective-permute-start(bf16[512,256]{1,0:T(8,128)(2,1)} %constant_dynamic-update-slice_fusion.3.refs_0_), channel_id=1, source_target_pairs={{0,1},{1,0},{2,3},{3,2},{4,5},{5,4},{6,7},{7,6},{8,9},{9,8},{10,11... | collective-permute-start | bytes 786440 | tf_op jit(solution)/shard_map/ppermute | solution.py:53
  303.3 14.8 %collective-permute-start.70 = (bf16[256,256]{1,0:T(8,128)(2,1)S(1)}, bf16[256,256]{1,0:T(8,128)(2,1)S(1)}, u32[]{:S(2)}, u32[]{:S(2)}) collective-permute-start(bf16[256,256]{1,0:T(8,128)(2,1)S(1)} %slice.103), channel_id=1, source_target_pairs={{0,2},{1,3},{2,4},{3,5},{4,6},{5,7},{6,0},{7,1},{8,10},{9,11},{10,... | collective-permute-start | bytes 393224 | tf_op jit(solution)/shard_map/ppermute | solution.py:53
  304.5 13.7 %collective-permute-start.71 = (bf16[256,256]{1,0:T(8,128)(2,1)S(1)}, bf16[256,256]{1,0:T(8,128)(2,1)S(1)}, u32[]{:S(2)}, u32[]{:S(2)}) collective-permute-start(bf16[256,256]{1,0:T(8,128)(2,1)S(1)} %slice.104), channel_id=1, source_target_pairs={{0,6},{1,7},{2,0},{3,1},{4,2},{5,3},{6,4},{7,5},{8,14},{9,15},{10,... | collective-permute-start | bytes 393224 | tf_op jit(solution)/shard_map/ppermute | solution.py:53
  311.4 13.8 %all-to-all-start.2 = ((bf16[4,32,2048]{2,1,0:T(8,128)(2,1)}), bf16[4,32,2048]{2,1,0:T(8,128)(2,1)}, u32[]{:S(2)}, u32[]{:S(2)}) async-start(bf16[4,32,2048]{2,1,0:T(8,128)(2,1)} %bitcast.46), calls=%async_computation.2 | async-start | bytes 1048576 | tf_op jit(solution)/shard_map/all_to_all | solution.py:510
  315.5 13.8 %collective-permute-start.66 = (bf16[512,256]{1,0:T(8,128)(2,1)}, bf16[512,256]{1,0:T(8,128)(2,1)S(1)}, u32[]{:S(2)}, u32[]{:S(2)}) collective-permute-start(bf16[512,256]{1,0:T(8,128)(2,1)} %collective-permute-done.60.refs_2_), channel_id=1, source_target_pairs={{0,1},{1,0},{2,3},{3,2},{4,5},{5,4},{6,7},{7,6},{8,9},{9,8},{10,11... | collective-permute-start | bytes 786440 | tf_op jit(solution)/shard_map/ppermute | solution.py:53
  315.6 14.6 %collective-permute-start.67 = (bf16[512,256]{1,0:T(8,128)(2,1)}, bf16[512,256]{1,0:T(8,128)(2,1)S(1)}, u32[]{:S(2)}, u32[]{:S(2)}) collective-permute-start(bf16[512,256]{1,0:T(8,128)(2,1)} %collective-permute-done.61.refs_3_), channel_id=1, source_target_pairs={{0,1},{1,0},{2,3},{3,2},{4,5},{5,4},{6,7},{7,6},{8,9},{9,8},{10,11... | collective-permute-start | bytes 786440 | tf_op jit(solution)/shard_map/ppermute | solution.py:53
  318.1 12.3 %collective-permute-start.74 = (bf16[256,256]{1,0:T(8,128)(2,1)S(1)}, bf16[256,256]{1,0:T(8,128)(2,1)S(1)}, u32[]{:S(2)}, u32[]{:S(2)}) collective-permute-start(bf16[256,256]{1,0:T(8,128)(2,1)S(1)} %collective-permute-done.70.refs_12_), channel_id=1, source_target_pairs={{0,1},{1,0},{2,3},{3,2},{4,5},{5,4},{6,7},{7,6},{8,9},{9,8},{10,11... | collective-permute-start | bytes 393224 | tf_op jit(solution)/shard_map/ppermute | solution.py:53
  318.2 13.3 %collective-permute-start.72 = (bf16[256,256]{1,0:T(8,128)(2,1)S(1)}, bf16[256,256]{1,0:T(8,128)(2,1)S(1)}, u32[]{:S(2)}, u32[]{:S(2)}) collective-permute-start(bf16[256,256]{1,0:T(8,128)(2,1)S(1)} %slice.105), channel_id=1, source_target_pairs={{0,2},{1,3},{2,4},{3,5},{4,6},{5,7},{6,0},{7,1},{8,10},{9,11},{10,... | collective-permute-start | bytes 393224 | tf_op jit(solution)/shard_map/ppermute | solution.py:53
  318.2 14.0 %collective-permute-start.73 = (bf16[256,256]{1,0:T(8,128)(2,1)S(1)}, bf16[256,256]{1,0:T(8,128)(2,1)S(1)}, u32[]{:S(2)}, u32[]{:S(2)}) collective-permute-start(bf16[256,256]{1,0:T(8,128)(2,1)S(1)} %slice.106), channel_id=1, source_target_pairs={{0,6},{1,7},{2,0},{3,1},{4,2},{5,3},{6,4},{7,5},{8,14},{9,15},{10,... | collective-permute-start | bytes 393224 | tf_op jit(solution)/shard_map/ppermute | solution.py:53
  325.2 26.3 %all-to-all-start.1 = ((bf16[4,32,2048]{2,1,0:T(8,128)(2,1)}), bf16[4,32,2048]{2,1,0:T(8,128)(2,1)}, u32[]{:S(2)}, u32[]{:S(2)}) async-start(bf16[4,32,2048]{2,1,0:T(8,128)(2,1)} %bitcast.90), calls=%async_computation.1 | async-start | bytes 1048576 | tf_op jit(solution)/shard_map/all_to_all | solution.py:510
  (97 other events, 1447.7 us)

commit v2 on v0

v2 whole, which is shorter than its diff:
```python
import functools
import math

import jax
import jax.numpy as jnp
from jax import lax
from jax.experimental import pallas as pl
from jax.experimental.pallas import tpu as pltpu
from jax.sharding import PartitionSpec as P

CAP = 2
THETA = 500000.0
EPS = 1e-05
BF = jnp.bfloat16
F32 = jnp.float32
MB = 2**20


def tensor_perm(move):
    pairs = []
    for z in range(2):
        for x in range(4):
            a, b = move(z, x)
            pairs.append((z * 4 + x, a * 4 + b % 4))
    return pairs


def decode_perm(move):
    pairs = []
    for z in range(2):
        for y in range(4):
            for c in range(2):
                a, b, e = move(z, y, c)
                pairs.append((z * 8 + y * 2 + c, a * 8 + (b % 4) * 2 + e))
    return pairs


X_UP = tensor_perm(lambda z, x: (z, x + 1))
X_DOWN = tensor_perm(lambda z, x: (z, x - 1))
Z_SWAP = tensor_perm(lambda z, x: (1 - z, x))
Y_UP = decode_perm(lambda z, y, c: (z, y + 1, c))
Y_DOWN = decode_perm(lambda z, y, c: (z, y - 1, c))
ZH_SWAP = decode_perm(lambda z, y, c: (1 - z, y, c))
CORE_SWAP = decode_perm(lambda z, y, c: (z, y, 1 - c))
X_FAR = tensor_perm(lambda z, x: (z, x + 2))


def to_t(value, pairs):
    return lax.ppermute(value, "tensor", pairs)


def to_d(value, pairs):
    return lax.ppermute(value, "decode", pairs)


def after(value, *others):
    return lax.optimization_barrier((value, *others))[0]


def together(*values):
    return lax.optimization_barrier(values)


def gather_inputs(rows, w, out, tables):
    h = w.shape[0] // 2
    low, high = to_d(w, Y_UP), to_d(w, Y_DOWN)
    left, right, over = to_t(rows, X_UP), to_t(rows, X_DOWN), to_t(rows, Z_SWAP)
    low, high, left, right, over = together(low, high, left, right, over)
    w_over = to_d(after(w, low), ZH_SWAP)
    far_low = to_d(low, Y_UP)
    far = to_t(left, X_UP)
    over_right = to_t(over, X_DOWN)
    far, over_right, w_over, far_low, out, *tables = together(
        far, over_right, w_over, far_low, out, *tables
    )
    over_left = to_t(after(over, far), X_UP)
    over_far = to_t(over_right, X_DOWN)
    over_low, over_high = to_d(w_over, Y_UP), to_d(w_over, Y_DOWN)
    over_left, over_far, over_low, over_high = together(over_left, over_far, over_low, over_high)
    far_a, far_b = to_d(over_low[:h], Y_UP), to_d(over_high[h:], Y_DOWN)
    return (
        [rows, left, right, far, over, over_left, over_right, over_far],
        [w, low, high, far_low, w_over, over_low, over_high],
        [far_a, far_b],
        tables,
        out,
    )


def row_sources(z, x):
    here, there = z * 4, (1 - z) * 4
    lo, hi, end = (x + 3) % 4, (x + 1) % 4, (x + 2) % 4
    return jnp.stack([first + at for first in (here, there) for at in (x, lo, hi, end)])


def shard_sources(zh, y):
    here, there = zh * 4, (1 - zh) * 4
    lo, hi, end = (y + 3) % 4, (y + 1) % 4, (y + 2) % 4
    return jnp.stack([first + at for first in (here, there) for at in (y, lo, hi, end)])


def stack_out(pieces, x):
    depth, wide = pieces[0].shape

    def kernel(x_ref, a0, a1, a2, a3, o_ref):
        for i, ref in enumerate((a0, a1, a2, a3)):
            to = pl.multiple_of((x_ref[0] + i) % 4 * depth, depth)
            o_ref[pl.ds(to, depth), :] = ref[...]

    return pl.pallas_call(
        kernel,
        in_specs=[smem()] + [vmem()] * 4,
        out_specs=vmem(),
        out_shape=jax.ShapeDtypeStruct((4 * depth, wide), BF),
        name="stack",
    )(x[None].astype(jnp.int32), *pieces)


def hbm():
    return pl.BlockSpec(memory_space=pltpu.HBM)


def vmem():
    return pl.BlockSpec(memory_space=pltpu.VMEM)


def smem():
    return pl.BlockSpec(memory_space=pltpu.SMEM)


def prepare_kernel(at_ref, h_ref, gain_ref, wq, wk, wv, wo, keep_ref, send_ref, w_ref, *parts):
    q_cols, k_cols = wq.shape[1], wk.shape[1]
    w_ref[:, :q_cols] = wq[...]
    w_ref[:, q_cols : q_cols + k_cols] = wk[...]
    w_ref[:, q_cols + k_cols :] = wv[...]
    rows, width = h_ref.shape
    depth = wq.shape[0]
    even_core = at_ref[0] == 0
    wide = wo.shape[1] // 4
    for j, part in enumerate(parts):
        to = pl.multiple_of((at_ref[1] + j) % 4 * wide, wide)
        part[...] = wo[:, pl.ds(to, wide)]

    def step(i, carry):
        at = pl.ds(pl.multiple_of(i * 16, 16), 16)
        h = h_ref[at, :].astype(F32)
        mean_sq = jnp.sum(h * h, axis=1, keepdims=True) / width
        normed = (h * lax.rsqrt(mean_sq + EPS) * gain_ref[...]).astype(BF)
        for k in range(width // (2 * depth)):
            even = normed[:, 2 * k * depth : (2 * k + 1) * depth]
            odd = normed[:, (2 * k + 1) * depth : (2 * k + 2) * depth]
            keep_ref[at, k * depth : (k + 1) * depth] = jnp.where(even_core, even, odd)
            send_ref[at, k * depth : (k + 1) * depth] = jnp.where(even_core, odd, even)
        return carry

    lax.fori_loop(0, rows // 16, step, 0)


def prepare(hidden, gain, w_query, w_key, w_value, w_out, core, x):
    rows, width = hidden.shape
    depth = w_query.shape[0]
    cols = w_query.shape[1] + 2 * w_key.shape[1]
    return pl.pallas_call(
        prepare_kernel,
        in_specs=[smem()] + [vmem()] * 6,
        out_specs=[vmem()] * 7,
        out_shape=[
            jax.ShapeDtypeStruct((rows, width // 2), BF),
            jax.ShapeDtypeStruct((rows, width // 2), BF),
            jax.ShapeDtypeStruct((depth, cols), BF),
        ]
        + [jax.ShapeDtypeStruct((w_out.shape[0], w_out.shape[1] // 4), BF)] * 4,
        compiler_params=pltpu.CompilerParams(vmem_limit_bytes=60 * MB),
        name="prepare",
    )(jnp.stack([core, x]).astype(jnp.int32), hidden, gain[None], w_query, w_key, w_value, w_out)


def project_kernel(x_at, w_at, *refs):
    xs, ws = refs[:8], refs[8:15]
    keep_ref, send_ref, xv, wv, xsem, wsem = refs[15:]
    span, cols = keep_ref.shape
    depth = ws[0].shape[0]
    half = xv.shape[1] // 2
    columns = []
    for g in range(2):
        columns.append(pl.ds(pl.multiple_of(w_at[4 * g] // 4 * half, half), half))
        for i, ref in enumerate(xs):
            for part in range(4):
                to = pl.multiple_of(x_at[i] * 32 + part * (span // 2), 32)
                pltpu.make_async_copy(
                    ref.at[pl.ds(part * 32, 32), columns[g]],
                    xv.at[pl.ds(to, 32), columns[g]],
                    xsem.at[g],
                ).start()
        for i in range(4 * g, min(4 * g + 4, 7)):
            to = pl.multiple_of(w_at[i] * depth, depth)
            pltpu.make_async_copy(ws[i], wv.at[pl.ds(to, depth), :], wsem.at[g]).start()
    missing = pl.multiple_of(w_at[7] * depth, depth)
    wv[pl.ds(missing, depth), :] = jnp.zeros((depth, cols), BF)
    for g in range(2):
        arrived = xv.at[:, columns[g]]
        pltpu.make_async_copy(arrived, arrived, xsem.at[g]).wait()
        arrived = wv.at[pl.ds(0, (4 - g) * depth), :]
        pltpu.make_async_copy(arrived, arrived, wsem.at[g]).wait()

        def step(i, carry, g=g):
            at = pl.ds(pl.multiple_of(i * 256, 256), 256)
            for p, ref in enumerate((keep_ref, send_ref)):
                term = jnp.dot(
                    xv[p * span : (p + 1) * span, columns[g]],
                    wv[columns[g], at],
                    preferred_element_type=F32,
                )
                ref[:, at] = term if g == 0 else ref[:, at] + term
            return carry

        lax.fori_loop(0, cols // 256, step, 0)


def project(rows, x_at, shards, w_at):
    span, width = rows[0].shape[0] * 4, rows[0].shape[1]
    cols = shards[0].shape[1]
    return pl.pallas_call(
        project_kernel,
        in_specs=[smem()] * 2 + [hbm()] * 15,
        out_specs=[vmem()] * 2,
        out_shape=[jax.ShapeDtypeStruct((span, cols), F32)] * 2,
        scratch_shapes=[
            pltpu.VMEM((2 * span, width), BF),
            pltpu.VMEM((width, cols), BF),
            pltpu.SemaphoreType.DMA((2,)),
            pltpu.SemaphoreType.DMA((2,)),
        ],
        compiler_params=pltpu.CompilerParams(vmem_limit_bytes=60 * MB),
        cost_estimate=pl.CostEstimate(
            flops=4 * span * width * cols, bytes_accessed=18 * MB, transcendentals=0
        ),
        name="project",
    )(x_at, w_at, *rows, *shards)


def project_last_kernel(prompt, x_at, w_at, *refs):
    xs = refs[:8]
    wa_ref, wb_ref, before_ref, o_ref, xv, xsem = refs[8:]
    span = o_ref.shape[0]
    depth = 2 * wa_ref.shape[0]
    columns = pl.ds(pl.multiple_of(w_at[7] * depth, depth), depth)
    for i, ref in enumerate(xs):
        for part in range(2):
            to = pl.multiple_of(x_at[i] * 32 + part * (span // 2), 32)
            pltpu.make_async_copy(
                ref.at[pl.ds(prompt * 64 + part * 32, 32), columns],
                xv.at[pl.ds(to, 32), :],
                xsem,
            ).start()
    pltpu.make_async_copy(xv, xv, xsem).wait()
    a = jnp.dot(xv[:, : depth // 2], wa_ref[...], preferred_element_type=F32)
    b = jnp.dot(xv[:, depth // 2 :], wb_ref[...], preferred_element_type=F32)
    o_ref[...] = before_ref[...] + a + b


def project_last(prompt, rows, x_at, halves, w_at, before):
    span, cols = before.shape
    depth = 2 * halves[0].shape[0]
    return pl.pallas_call(
        functools.partial(project_last_kernel, prompt),
        in_specs=[smem()] * 2 + [hbm()] * 8 + [vmem()] * 3,
        out_specs=vmem(),
        out_shape=jax.ShapeDtypeStruct((span, cols), F32),
        scratch_shapes=[pltpu.VMEM((span, depth), BF), pltpu.SemaphoreType.DMA],
        compiler_params=pltpu.CompilerParams(vmem_limit_bytes=40 * MB),
        cost_estimate=pl.CostEstimate(
            flops=2 * span * depth * cols, bytes_accessed=5 * MB, transcendentals=0
        ),
        name="project_last",
    )(x_at, w_at, *rows, *halves, before)


def rotate_kernel(rot_scale, a_ref, b_ref, cos_ref, sin_ref, q_ref, k_ref, v_ref):
    cos, sin = cos_ref[...], sin_ref[...]
    heads = q_ref.shape[0]

    def total(j):
        at = slice(j * 128, (j + 1) * 128)
        return a_ref[:, at] + b_ref[:, at]

    def rotated(j):
        part = total(j)
        return part * cos + pltpu.roll(part, 64, 1) * sin

    for j in range(heads):
        q_ref[j] = (rotated(j) * rot_scale).astype(BF)
    keys = rotated(heads).astype(BF)
    values = total(heads + 1).astype(BF)
    half = keys.shape[0] // 2
    for s in range(half // 32):
        for r in range(2):
            rows = slice(r * half + s * 32, r * half + s * 32 + 32)
            to = slice(s * 64 + r * 32, s * 64 + r * 32 + 32)
            k_ref[to, :] = keys[rows]
            v_ref[to, :] = values[rows]


def rotate(own, got, cosine, sine):
    span, cols = own.shape
    heads = cols // 128 - 2
    scale = math.log2(math.e) / math.sqrt(128)
    return pl.pallas_call(
        functools.partial(rotate_kernel, scale),
        in_specs=[vmem()] * 4,
        out_specs=[vmem()] * 3,
        out_shape=[
            jax.ShapeDtypeStruct((heads, span, 128), BF),
            jax.ShapeDtypeStruct((span, 128), BF),
            jax.ShapeDtypeStruct((span, 128), BF),
        ],
        compiler_params=pltpu.CompilerParams(vmem_limit_bytes=60 * MB),
        name="rotate",
    )(own, got, cosine, sine)


def attend_kernel(chunk, block, live_ref, q_ref, k_hbm, v_hbm, kn_ref, vn_ref, o_ref, k_ref, v_ref, sems):
    live = live_ref[0]
    blocks = k_ref.shape[0] // block
    head = pl.program_id(0)

    def loads(j):
        at = pl.ds(pl.multiple_of(j * block, block), block)
        return (
            pltpu.make_async_copy(k_hbm.at[at, :], k_ref.at[at, :], sems.at[0, j]),
            pltpu.make_async_copy(v_hbm.at[at, :], v_ref.at[at, :], sems.at[1, j]),
        )

    @pl.when(head == 0)
    def _():
        for j in range(blocks):
            for load in loads(j):
                load.start()

    q = q_ref[0]
    full = live // block
    left = live - full * block

    def scores(keys, allowed):
        s = lax.dot_general(q, keys, (((1,), (1,)), ((), ())), preferred_element_type=F32)
        return s if allowed is None else jnp.where(allowed(s.shape), s, -1e30)

    def lanes(op, values):
        return functools.reduce(
            op, [values[:, c * 128 : (c + 1) * 128] for c in range(values.shape[1] // 128)]
        )

    def weigh(s, top, values):
        p = jnp.exp2(s - top)
        return lanes(jnp.add, p), jnp.dot(p.astype(BF), values, preferred_element_type=F32)

    def part(j):
        at = pl.ds(pl.multiple_of(j * block, block), block)
        return k_ref[at, :], v_ref[at, :]

    def arrive(j):
        @pl.when(head == 0)
        def _():
            for load in loads(j):
                load.wait()

    def part_allowed(shape):
        return lax.broadcasted_iota(jnp.int32, shape, 1) < left

    def new_allowed(shape):
        i = lax.broadcasted_iota(jnp.int32, shape, 0)
        row = i // 32 * 64 + chunk * 32 + i % 32
        return lax.broadcasted_iota(jnp.int32, shape, 1) <= row

    def every(one, state, await_block):
        def body(j, state):
            await_block(j)
            return one(state, *part(j), None)

        state = lax.fori_loop(1, full, body, state)

        def rest(j, carry):
            await_block(j)
            return carry

        lax.fori_loop(full, blocks, rest, 0)
        state = lax.cond(
            left > 0, lambda st: one(st, *part(full), part_allowed), lambda st: st, state
        )
        return one(state, kn_ref[...], vn_ref[...], new_allowed)

    def finish(total, out):
        o_ref[...] = (out / jnp.sum(total, axis=1, keepdims=True)).astype(BF)

    arrive(0)
    keys, values = part(0)
    s = scores(keys, None)
    first_top = jnp.max(s, axis=1, keepdims=True)
    first = weigh(s, first_top, values)

    def fixed(state, keys, values, allowed):
        most, total, out = state
        s = scores(keys, allowed)
        more, term = weigh(s, first_top, values)
        return jnp.maximum(most, lanes(jnp.maximum, s)), total + more, out + term

    start = jnp.broadcast_to(first_top, (q.shape[0], 128))
    most, total, out = every(fixed, (start, *first), arrive)
    finish(total, out)

    @pl.when(jnp.max(most - first_top) > 40.0)
    def _():
        def running(state, keys, values, allowed):
            top, total, out = state
            s = scores(keys, allowed)
            new_top = jnp.maximum(top, jnp.max(s, axis=1, keepdims=True))
            more, term = weigh(s, new_top, values)
            keep = jnp.exp2(top - new_top)
            return new_top, total * keep + more, out * keep + term

        _, total, out = every(running, (first_top, *first), lambda j: None)
        finish(total, out)


def attend(chunk, q, cache_k, cache_v, keys, values, live):
    heads, span, width = q.shape
    rows = span // 2
    prefix = cache_k.shape[0]
    block = 2048
    return pl.pallas_call(
        functools.partial(attend_kernel, chunk, block),
        grid=(heads,),
        in_specs=[
            smem(),
            pl.BlockSpec((1, rows, width), lambda i: (i, chunk, 0)),
            hbm(),
            hbm(),
            vmem(),
            vmem(),
        ],
        out_specs=pl.BlockSpec((rows, width), lambda i: (0, i)),
        out_shape=jax.ShapeDtypeStruct((rows, heads * width), BF),
        scratch_shapes=[
            pltpu.VMEM((prefix, width), BF),
            pltpu.VMEM((prefix, width), BF),
            pltpu.SemaphoreType.DMA((2, prefix // block)),
        ],
        compiler_params=pltpu.CompilerParams(vmem_limit_bytes=60 * MB),
        cost_estimate=pl.CostEstimate(
            flops=4 * heads * rows * (prefix + span) * width,
            bytes_accessed=4 * prefix * width,
            transcendentals=heads * rows * (prefix + span),
        ),
        name="attend",
    )(live, q, cache_k, cache_v, keys, values)


def output_kernel(x_at, a0, a1, a2, a3, w_ref, o_ref, xv, wv, xsem, wsem):
    shards, depth, cols = w_ref.shape
    width = a0.shape[1]
    copies = []
    for i, ref in enumerate((a0, a1, a2, a3)):
        to = pl.multiple_of(x_at[i] * width, width)
        copies.append(pltpu.make_async_copy(ref, xv.at[:, pl.ds(to, width)], xsem.at[i]))
    for copy in copies:
        copy.start()
    loads = []
    for i in range(shards // 4):
        group = pl.ds(4 * i, 4)
        loads.append(pltpu.make_async_copy(w_ref.at[group], wv.at[group], wsem.at[i]))
    for load in loads:
        load.start()
    for copy in copies:
        copy.wait()
    for i, load in enumerate(loads):
        load.wait()
        w = jnp.concatenate([wv[j] for j in range(4 * i, 4 * i + 4)], axis=1)
        o_ref[:, 4 * i * cols : 4 * (i + 1) * cols] = jnp.dot(
            xv[...], w, preferred_element_type=F32
        ).astype(BF)


def output(pieces, weights, x):
    rows, width = pieces[0].shape
    x_at = jnp.stack([x, (x + 3) % 4, (x + 1) % 4, (x + 2) % 4]).astype(jnp.int32)
    shards, depth, cols = weights.shape
    return pl.pallas_call(
        output_kernel,
        in_specs=[smem()] + [hbm()] * 5,
        out_specs=vmem(),
        out_shape=jax.ShapeDtypeStruct((rows, shards * cols), BF),
        scratch_shapes=[
            pltpu.VMEM((rows, 4 * width), BF),
            pltpu.VMEM((shards, depth, cols), BF),
            pltpu.SemaphoreType.DMA((4,)),
            pltpu.SemaphoreType.DMA((4,)),
        ],
        compiler_params=pltpu.CompilerParams(vmem_limit_bytes=60 * MB),
        cost_estimate=pl.CostEstimate(
            flops=2 * rows * depth * shards * cols, bytes_accessed=11 * MB, transcendentals=0
        ),
        name="output",
    )(x_at, *pieces, weights)


def finish_kernel(*refs):
    o_ref = refs[-1]
    for r, ref in enumerate(refs[:-1]):
        for x in range(4):
            total = ref[x].astype(F32) + ref[4 + x].astype(F32)
            total = total.astype(BF)
            for d in range(16):
                to = d * 512 + x * 128
                o_ref[r * 32 : r * 32 + 32, to : to + 128] = total[:, d * 128 : d * 128 + 128]


def finish(parts):
    rows = parts[0].shape[1] * len(parts)
    return pl.pallas_call(
        finish_kernel,
        in_specs=[vmem()] * len(parts),
        out_specs=vmem(),
        out_shape=jax.ShapeDtypeStruct((rows, parts[0].shape[2] * 4), BF),
        compiler_params=pltpu.CompilerParams(vmem_limit_bytes=60 * MB),
        name="finish",
    )(*parts)


def place_kernel(pages, page_of, kv_ref, out_ref, scale_ref):
    page = out_ref.shape[2]

    def slot(s, carry):
        number = page_of[s]

        @pl.when(number < 0)
        def _():
            out_ref[s] = jnp.zeros(out_ref.shape[1:], BF)
            scale_ref[s] = jnp.zeros(scale_ref.shape[1:], F32)

        @pl.when(number >= 0)
        def _():
            at = pl.multiple_of(number * page, page)
            rows = kv_ref[s // CAP, pl.ds(at, page), :].astype(F32)
            for c in range(2):
                part = rows[:, c * 128 : (c + 1) * 128]
                most = jnp.max(jnp.max(jnp.abs(part), axis=0, keepdims=True), axis=1, keepdims=True)
                scale = (most + 1e-06).astype(BF).astype(F32)
                out_ref[s, c] = (part / scale).astype(BF)
                scale_ref[s, c : c + 1, :] = jnp.broadcast_to(scale, (1, 128))

        return carry

    lax.fori_loop(0, out_ref.shape[0], slot, 0)


def gather_pages(keys, values, page_owner):
    count = page_owner.shape[1]
    span = keys.shape[0]
    owner_rows = jnp.pad(page_owner.astype(BF), ((0, 15), (0, 256 - count)))
    sent = jnp.concatenate([jnp.concatenate([keys, values], axis=1), owner_rows], axis=0)
    return lax.all_gather(sent, "decode", axis=0)


def place_pages(got, count, d):
    groups, span = got.shape[0], got.shape[1] - 16
    owners = got[:, span, :count].astype(jnp.int32)
    order = jnp.arange(count, dtype=jnp.int32)
    same = owners[:, :, None] == owners[:, None, :]
    rank = jnp.sum((same & (order[None, :] < order[:, None])[None]).astype(jnp.int32), axis=2)
    mine = (owners == d)[:, None, :] & (rank[:, None, :] == jnp.arange(CAP)[None, :, None])
    ids = jnp.max(jnp.where(mine, order[None, None, :], -1), axis=2).reshape(groups * CAP)
    pages, scales = pl.pallas_call(
        functools.partial(place_kernel, count),
        in_specs=[smem(), vmem()],
        out_specs=[vmem()] * 2,
        out_shape=[
            jax.ShapeDtypeStruct((groups * CAP, 2, span // count, 128), BF),
            jax.ShapeDtypeStruct((groups * CAP, 2, 128), F32),
        ],
        compiler_params=pltpu.CompilerParams(vmem_limit_bytes=60 * MB),
        cost_estimate=pl.CostEstimate(
            flops=4 * MB, bytes_accessed=8 * MB, transcendentals=0
        ),
        name="place",
    )(ids, got)
    return pages[None], scales[None, :, :, :1].astype(BF), ids[None]


def rope_tables(positions, width):
    half = width // 2
    steps = jnp.arange(half, dtype=F32) * (2.0 / width)
    freqs = jnp.exp(-math.log(THETA) * steps)
    angles = positions.astype(F32)[:, None] * freqs[None, :]
    cosine, sine = jnp.cos(angles), jnp.sin(angles)
    return (
        jnp.concatenate([cosine, cosine], axis=1),
        jnp.concatenate([-sine, sine], axis=1),
    )


def body(
    hidden_in, norm_gain, w_query, w_key, w_value, w_out, cache_k, cache_v, prefix_len, page_owner
):
    t, d = lax.axis_index("tensor"), lax.axis_index("decode")
    z, x = t // 4, t % 4
    zh, y, core = d // 8, d // 2 % 4, d % 2
    span = hidden_in.shape[1] * 8
    width = cache_k.shape[-1]
    i = jnp.arange(span, dtype=jnp.int32)
    true_row = i % (span // 2) // 32 * 64 + i // (span // 2) * 32 + i % 32
    tables = rope_tables(prefix_len[0] + true_row, width)
    keep, send, w, *quarters = prepare(
        hidden_in[0], norm_gain, w_query, w_key, w_value, w_out, core, x
    )
    moves = (X_UP, X_FAR, X_DOWN)
    quarters = [quarters[0]] + [to_t(a, pairs) for a, pairs in zip(quarters[1:], moves)]
    chip_rows = jnp.concatenate([keep, to_d(send, CORE_SWAP)], axis=0)
    chip_rows, *quarters = together(chip_rows, *quarters)
    out = stack_out([quarters[i] for i in (0, 3, 2, 1)], x)
    rows, shards, last, (cosine, sine), out = gather_inputs(chip_rows, w, out, tables)
    out_weights = lax.all_gather(out, "decode", axis=0)
    x_at = row_sources(z, x).astype(jnp.int32)
    w_at = shard_sources(zh, y).astype(jnp.int32)
    own, other = project(rows, x_at, shards, w_at)
    other = project_last(1, rows, x_at, last, w_at, other)
    own = project_last(0, rows, x_at, last, w_at, after(own, other))
    queries, keys, values = rotate(own, to_d(other, CORE_SWAP), cosine, sine)

    def attend_chunk(chunk, queries):
        return attend(chunk, queries, cache_k[0, 0], cache_v[0, 0], keys, values, prefix_len)

    def spread(attended):
        return [attended] + [to_t(attended, pairs) for pairs in (X_UP, X_DOWN, X_FAR)]

    def back(partial):
        got = lax.all_to_all(partial, "tensor", 0, 0, tiled=True)
        return got.reshape(8, 32, partial.shape[1])

    got = gather_pages(keys, values, page_owner)
    first = attend_chunk(0, queries)
    first_pieces = spread(first)
    second = attend_chunk(1, after(queries, first))
    first_pieces[0] = after(first_pieces[0], second)
    second_pieces = spread(second)
    first_partial = output(first_pieces, out_weights, x)
    first_partial, *second_pieces = together(first_partial, *second_pieces)
    first_back = back(first_partial)
    second_partial = output(second_pieces, out_weights, x)
    placed = place_pages(after(got, second_partial), page_owner.shape[1], d)
    first_back = after(first_back, second_partial)
    second_back = back(after(second_partial, first_back))
    second_back = after(second_back, placed[0])
    attn_out = finish([first_back, second_back])[None]
    return (attn_out, *placed)


def solution(mesh):
    in_specs = (
        P("decode", "tensor", None),
        P(),
        P("decode", "tensor"),
        P("decode", "tensor"),
        P("decode", "tensor"),
        P("tensor", "decode"),
        P("decode", "tensor", None, None),
        P("decode", "tensor", None, None),
        P("decode"),
        P("decode", None),
    )
    out_specs = (
        P("decode", "tensor", None),
        P("decode", None, None, None, "tensor"),
        P("decode", None, None, "tensor"),
        P("decode", None),
    )
    return jax.shard_map(body, mesh=mesh, in_specs=in_specs, out_specs=out_specs, check_vma=False)
```

time: 540 us -> 245 us (0.45)
  the two profiles are of different devices: /device:TPU:1 before, /device:TPU:24 now
where the time goes in v2:
time: 245 us; the launch traced here: 244 us
  Pallas kernels  88.3 us (36%)
  waiting for transfers between devices  75.9 us (31%)
  starting transfers between devices  44.7 us (18%)
  between operations  15.1 us (6%)
  local copies, waits for them, and re-layouts  12 us (5%)
  other arithmetic  7.8 us (3%)
    ppermute x10, waiting for transfers between devices, to_d(): return lax.ppermute(value, 'decode', pairs)  53.5 us
    pallas_call x2, Pallas kernels, attend(): pl.pallas_call(functools.partial(attend_kernel, chunk, block), grid=(head...  37.8 us
    ppermute x16, starting transfers between devices, to_t(): return lax.ppermute(value, 'tensor', pairs)  25.2 us
    pallas_call x2, Pallas kernels, output(): pl.pallas_call(output_kernel, in_specs=[smem()] + [hbm()] * 5, out_specs=...  15.2 us
    pallas_call x1, Pallas kernels, project(): pl.pallas_call(project_kernel, in_specs=[smem()] * 2 + [hbm()] * 15, out_...  14.3 us
    all_to_all x2, waiting for transfers between devices, back(): got = lax.all_to_all(partial, 'tensor', 0, 0, tiled=True)  12.1 us
    ppermute x10, starting transfers between devices, to_d(): return lax.ppermute(value, 'decode', pairs)  10.4 us
    ppermute x16, waiting for transfers between devices, to_t(): return lax.ppermute(value, 'tensor', pairs)  10.3 us
  transfers between devices with their start and end apart: 30, of which 15 were waited for; matrix products, arithmetic and copies ran while one was open for 6% of the time, Pallas kernels for 33%

profile of v2, /device:TPU:24, one launch (start us, length us, event | category | flops | bytes accessed | tf_op | source)
XLA Modules:
  0.0 243.8 jit_solution(8420852339160285464)
XLA Ops:
  7.2 0.7 pad_add_fusion.1.at_ref
  7.9 4.1 %prepare.1 = (bf16[64,4096]{1,0:T(8,128)(2,1)}, bf16[64,4096]{1,0:T(8,128)(2,1)}, bf16[512,768]{1,0:T(8,128)(2,1)}, bf16[512,128]{1,0:T(8,128)(2,1)}, bf16[512,1...) custom-call(s32[2]{0:T(128)} %pad_add_fusion.1.at_ref, bf16[64,8192]{1,0:T(8,128)(2,1)} %bitcast.44, ...), custom_call_target="tpu_custom_call" | custom-call | tf_op jit(solution)/shard_map/prepare/pallas_call | solution.py:163
  12.0 1.6 collective-permute-start.1
  13.5 2.7 %collective-permute-start.2 = (bf16[512,128]{1,0:T(8,128)(2,1)}, bf16[512,128]{1,0:T(8,128)(2,1)S(1)}, u32[]{:S(2)}, u32[]{:S(2)}) collective-permute-start(bf16[512,128]{1,0:T(8,128)(2,1)} %get-tuple-element.57), channel_id=1, source_target_pairs={{0,32},{16,48},{32,0},{48,16},{64,96},{80,112},{96,64},{112,80},{1... | collective-permute-start | bytes 393224 | tf_op jit(solution)/shard_map/ppermute | solution.py:49
  16.3 1.4 collective-permute-start.3
  17.7 1.1 pad_maximum_fusion.refs_0_
  19.3 3.8 %collective-permute-done.2.a2 = bf16[512,128]{1,0:T(8,128)(2,1)S(1)} collective-permute-done((bf16[512,128]{1,0:T(8,128)(2,1)}, bf16[512,128]{1,0:T(8,128)(2,1)S(1)}, u32[]{:S(2)}, u32[]{:S(2)}) %collective-permute-start.2) | collective-permute-done | bytes 131104 | tf_op jit(solution)/shard_map/ppermute | solution.py:49
  23.1 1.3 collective-permute-start.6
  24.4 2.0 collective-permute-start.7
  26.4 1.9 collective-permute-start.8
  28.6 1.8 collective-permute-start.5
  30.4 16.5 %collective-permute-done.4.refs_9_ = bf16[512,768]{1,0:T(8,128)(2,1)} collective-permute-done((bf16[512,768]{1,0:T(8,128)(2,1)}, bf16[512,768]{1,0:T(8,128)(2,1)}, u32[]{:S(2)}, u32[]{:S(2)}) %collective-permute-start.4) | collective-permute-done | bytes 786464 | tf_op jit(solution)/shard_map/ppermute | solution.py:53
  46.9 1.1 collective-permute-done.5.refs_10_
  48.0 1.1 collective-permute-done.6.refs_1_
  49.1 1.7 collective-permute-done.8.refs_4_
  50.8 1.3 collective-permute-start.10
  52.1 0.7 collective-permute-start.9
  52.9 3.7 %collective-permute-start.11 = (bf16[512,768]{1,0:T(8,128)(2,1)}, bf16[512,768]{1,0:T(8,128)(2,1)}, u32[]{:S(2)}, u32[]{:S(2)}) collective-permute-start(bf16[512,768]{1,0:T(8,128)(2,1)} %get-tuple-element.65.refs_8_), channel_id=1, source_target_pairs={{0,8},{1,9},{2,10},{3,11},{4,12},{5,13},{6,14},{7,15},{8,0},{9,1},... | collective-permute-start | bytes 2359304 | tf_op jit(solution)/shard_map/ppermute | solution.py:53
  57.5 1.0 fusion.2
  58.5 1.1 pad_maximum_fusion.1
  59.6 1.9 stack.107
  61.5 10.7 %collective-permute-done.11.refs_12_ = bf16[512,768]{1,0:T(8,128)(2,1)} collective-permute-done((bf16[512,768]{1,0:T(8,128)(2,1)}, bf16[512,768]{1,0:T(8,128)(2,1)}, u32[]{:S(2)}, u32[]{:S(2)}) %collective-permute-start.11) | collective-permute-done | bytes 786464 | tf_op jit(solution)/shard_map/ppermute | solution.py:53
  72.2 1.5 collective-permute-done.12.refs_11_
  73.7 0.9 collective-permute-done.10.refs_6_
  74.6 2.1 collective-permute-done.9.refs_3_
  76.8 3.2 %collective-permute-start.14 = (bf16[128,4096]{1,0:T(8,128)(2,1)}, bf16[128,4096]{1,0:T(8,128)(2,1)}, u32[]{:S(2)}, u32[]{:S(2)}) collective-permute-start(bf16[128,4096]{1,0:T(8,128)(2,1)} %collective-permute-done.10.refs_6_), channel_id=1, source_target_pairs={{0,48},{16,0},{32,16},{48,32},{64,112},{80,64},{96,80},{112,96},{1... | collective-permute-start | bytes 3145736 | tf_op jit(solution)/shard_map/ppermute | solution.py:49
  80.3 1.8 collective-permute-start.16
  82.1 0.7 stack.104.w_at
  82.7 0.6 stack.95.x_at
  83.4 23.5 %collective-permute-done.15.refs_13_ = bf16[512,768]{1,0:T(8,128)(2,1)} collective-permute-done((bf16[512,768]{1,0:T(8,128)(2,1)}, bf16[512,768]{1,0:T(8,128)(2,1)}, u32[]{:S(2)}, u32[]{:S(2)}) %collective-permute-start.15) | collective-permute-done | bytes 786464 | tf_op jit(solution)/shard_map/ppermute | solution.py:53
  106.8 1.8 slice.13
  108.6 1.0 collective-permute-start.17
  109.6 1.8 slice.14
  111.4 1.2 collective-permute-start.18
  112.6 14.3 %project.1 = (f32[512,768]{1,0:T(8,128)}, f32[512,768]{1,0:T(8,128)}) custom-call(s32[8]{0:T(128)} %stack.95.x_at, s32[8]{0:T(128)} %stack.104.w_at, bf16[128,4096]{1,0:T(8,128)(2,1)} %copy-done, bf16[128,4096]{1,0:T(8,128)(2,1)} %copy-done.3, bf16[128,4096]{1,0:T(8,128)(2,1)} %copy-done.5, bf16[128,4096]{1,0:T(8,128)(2,1)} %collective-permute-done.9.refs_3_, ...), custom_call_target="tpu_custom_call" | custom-call | flops 6442450944 | bytes 18874368 | tf_op jit(solution)/shard_map/project/pallas_call | solution.py:223
  127.0 1.4 copy-done.8
  128.4 2.1 project_last.2
  130.8 2.1 project_last.3.a_ref
  133.0 1.1 copy-done.2
  134.3 3.2 %rotate.1 = (bf16[4,512,128]{2,1,0:T(8,128)(2,1)}, bf16[512,128]{1,0:T(8,128)(2,1)}, bf16[512,128]{1,0:T(8,128)(2,1)}) custom-call(f32[512,768]{1,0:T(8,128)} %copy-done.2, f32[512,768]{1,0:T(8,128)} %collective-permute-done.19.b_ref, f32[512,128]{1,0:T(8,128)} %get-tuple-element.83.cos_ref, f32[512,128]{1,0:T(8,128)} %get-tuple-element.84.sin_ref), custom_call_target="tpu_custom_call" | custom-call | tf_op jit(solution)/shard_map/rotate/pallas_call | solution.py:308
  137.5 1.7 fusion.1
  139.3 18.9 %attend.2.a0 = bf16[256,512]{1,0:T(8,128)(2,1)} custom-call(s32[1]{0:T(128)} %copy.36.live_ref, bf16[4,512,128]{2,1,0:T(8,128)(2,1)} %get-tuple-element.88.q_ref, bf16[8192,128]{1,0:T(8,128)(2,1)} %bitcast.49, bf16[8192,128]{1,0:T(8,128)(2,1)} %bitcast.51, bf16[512,128]{1,0:T(8,128)(2,1)} %get-tuple-element.86.kn_ref, bf16[512,128]{1,0:T(8,128)(2,1)} %get-tuple-element.87.vn_ref), custom_call_target="tpu_custom_call" | custom-call | flops 4563402752 | bytes 4194304 | tf_op jit(solution)/shard_map/attend/pallas_call | solution.py:430
  158.4 3.1 %collective-permute-start.21 = (bf16[256,512]{1,0:T(8,128)(2,1)}, bf16[256,512]{1,0:T(8,128)(2,1)S(1)}, u32[]{:S(2)}, u32[]{:S(2)}) collective-permute-start(bf16[256,512]{1,0:T(8,128)(2,1)} %attend.2.a0), channel_id=1, source_target_pairs={{0,48},{16,0},{32,16},{48,32},{64,112},{80,64},{96,80},{112,96},{1... | collective-permute-start | bytes 786440 | tf_op jit(solution)/shard_map/ppermute | solution.py:49
  161.5 18.9 %attend.3.a0 = bf16[256,512]{1,0:T(8,128)(2,1)} custom-call(s32[1]{0:T(128)} %copy.36.live_ref, bf16[4,512,128]{2,1,0:T(8,128)(2,1)} %get-tuple-element.88.q_ref, bf16[8192,128]{1,0:T(8,128)(2,1)} %bitcast.50, bf16[8192,128]{1,0:T(8,128)(2,1)} %bitcast.52, bf16[512,128]{1,0:T(8,128)(2,1)} %get-tuple-element.86.kn_ref, bf16[512,128]{1,0:T(8,128)(2,1)} %get-tuple-element.87.vn_ref), custom_call_target="tpu_custom_call" | custom-call | flops 4563402752 | bytes 4194304 | tf_op jit(solution)/shard_map/attend/pallas_call | solution.py:430
  180.4 1.0 collective-permute-start.23
  181.4 2.3 collective-permute-start.24
  183.7 2.3 collective-permute-start.25
  186.1 0.6 pad_add_fusion.x_at
  186.7 0.6 copy-done.16
  187.4 7.6 %output.2 = bf16[256,2048]{1,0:T(8,128)(2,1)} custom-call(s32[4]{0:T(128)} %pad_add_fusion.x_at, bf16[256,512]{1,0:T(8,128)(2,1)} %attend.2.a0, bf16[256,512]{1,0:T(8,128)(2,1)} %copy-done.14, bf16[256,512]{1,0:T(8,128)(2,1)} %copy-done.16, bf16[256,512]{1,0:T(8,128)(2,1)} %copy-done.17, bf16[16,2048,128]{2,1,0:T(8,128)(2,1)} %bitcast.36), custom_call_target="tpu_custom_call" | custom-call | flops 2147483648 | bytes 11534336 | tf_op jit(solution)/shard_map/output/pallas_call | solution.py:487
  195.3 5.4 %all-to-all-start = ((bf16[8,32,2048]{2,1,0:T(8,128)(2,1)}), bf16[8,32,2048]{2,1,0:T(8,128)(2,1)S(1)}, u32[]{:S(2)}, u32[]{:S(2)}) async-start(bf16[8,32,2048]{2,1,0:T(8,128)(2,1)} %bitcast.42), calls=%async_computation | async-start | bytes 2097152 | tf_op jit(solution)/shard_map/all_to_all | solution.py:636
  200.7 7.6 %output.3 = bf16[256,2048]{1,0:T(8,128)(2,1)} custom-call(s32[4]{0:T(128)} %pad_add_fusion.x_at, bf16[256,512]{1,0:T(8,128)(2,1)} %attend.3.a0, bf16[256,512]{1,0:T(8,128)(2,1)} %copy-done.13, bf16[256,512]{1,0:T(8,128)(2,1)} %copy-done.15, bf16[256,512]{1,0:T(8,128)(2,1)} %copy-done.18, bf16[16,2048,128]{2,1,0:T(8,128)(2,1)} %bitcast.37), custom_call_target="tpu_custom_call" | custom-call | flops 2147483648 | bytes 11534336 | tf_op jit(solution)/shard_map/output/pallas_call | solution.py:487
  208.4 5.9 %all-to-all-done.refs_0_ = bf16[8,32,2048]{2,1,0:T(8,128)(2,1)S(1)} async-done(((bf16[8,32,2048]{2,1,0:T(8,128)(2,1)}), bf16[8,32,2048]{2,1,0:T(8,128)(2,1)S(1)}, u32[]{:S(2)}, u32[]{:S(2)}) %all-to-all-start) | async-done | bytes 1048608 | tf_op jit(solution)/shard_map/all_to_all | solution.py:636
  214.3 3.6 %all-to-all-start.1 = ((bf16[8,32,2048]{2,1,0:T(8,128)(2,1)}), bf16[8,32,2048]{2,1,0:T(8,128)(2,1)S(1)}, u32[]{:S(2)}, u32[]{:S(2)}) async-start(bf16[8,32,2048]{2,1,0:T(8,128)(2,1)} %bitcast.41), calls=%async_computation.1 | async-start | bytes 2097152 | tf_op jit(solution)/shard_map/all_to_all | solution.py:636
  217.9 0.8 slice_convert_fusion.1
  218.8 0.8 broadcast_compare_fusion
  219.8 0.6 reshape.105.page_of
  220.4 0.6 broadcast_in_dim_reshape.3
  221.0 4.7 %place.1 = (bf16[32,2,128,128]{3,2,1,0:T(8,128)(2,1)}, f32[32,2,128]{2,1,0:T(2,128)}) custom-call(s32[32]{0:T(128)} %reshape.105.page_of, bf16[16,528,256]{2,1,0:T(8,128)(2,1)} %bitcast.40), custom_call_target="tpu_custom_call" | custom-call | flops 4194304 | bytes 8388608 | tf_op jit(solution)/shard_map/place/pallas_call | solution.py:572
  225.7 0.8 slice.22
  226.5 0.6 copy.34
  227.1 6.1 %all-to-all-done.1.refs_1_ = bf16[8,32,2048]{2,1,0:T(8,128)(2,1)S(1)} async-done(((bf16[8,32,2048]{2,1,0:T(8,128)(2,1)}), bf16[8,32,2048]{2,1,0:T(8,128)(2,1)S(1)}, u32[]{:S(2)}, u32[]{:S(2)}) %all-to-all-start.1) | async-done | bytes 1048608 | tf_op jit(solution)/shard_map/all_to_all | solution.py:636
  233.2 1.0 copy-done.12
  234.2 2.8 %finish.1 = bf16[64,8192]{1,0:T(8,128)(2,1)} custom-call(bf16[8,32,2048]{2,1,0:T(8,128)(2,1)} %copy-done.11, bf16[8,32,2048]{2,1,0:T(8,128)(2,1)} %copy-done.12), custom_call_target="tpu_custom_call" | custom-call | tf_op jit(solution)/shard_map/finish/pallas_call | solution.py:519
  (83 shorter events, 2.9 us)
Async XLA Ops:
  7.2 179.5 %all-gather.5.cloned.1.call-start = ((), (), s32[]{:S(2)}) async-start(), calls=%async_computation.2 | async-start | bytes 8912896 | tf_op jit(solution)/shard_map/all_gather | solution.py:621
  12.0 5.7 %collective-permute-start = (bf16[64,4096]{1,0:T(8,128)(2,1)}, bf16[64,4096]{1,0:T(8,128)(2,1)S(1)}, u32[]{:S(2)}, u32[]{:S(2)}) collective-permute-start(bf16[64,4096]{1,0:T(8,128)(2,1)} %get-tuple-element.54), channel_id=1, source_target_pairs={{0,1},{1,0},{2,3},{3,2},{4,5},{5,4},{6,7},{7,6},{8,9},{9,8},{10,11... | collective-permute-start | bytes 1572872 | tf_op jit(solution)/shard_map/ppermute | solution.py:53
  12.0 7.3 %collective-permute-start.1 = (bf16[512,128]{1,0:T(8,128)(2,1)}, bf16[512,128]{1,0:T(8,128)(2,1)S(1)}, u32[]{:S(2)}, u32[]{:S(2)}) collective-permute-start(bf16[512,128]{1,0:T(8,128)(2,1)} %get-tuple-element.56), channel_id=1, source_target_pairs={{0,16},{16,32},{32,48},{48,0},{64,80},{80,96},{96,112},{112,64},{1... | collective-permute-start | bytes 393224 | tf_op jit(solution)/shard_map/ppermute | solution.py:49
  13.5 9.6 %collective-permute-start.2 = (bf16[512,128]{1,0:T(8,128)(2,1)}, bf16[512,128]{1,0:T(8,128)(2,1)S(1)}, u32[]{:S(2)}, u32[]{:S(2)}) collective-permute-start(bf16[512,128]{1,0:T(8,128)(2,1)} %get-tuple-element.57), channel_id=1, source_target_pairs={{0,32},{16,48},{32,0},{48,16},{64,96},{80,112},{96,64},{112,80},{1... | collective-permute-start | bytes 393224 | tf_op jit(solution)/shard_map/ppermute | solution.py:49
  16.3 6.8 %collective-permute-start.3 = (bf16[512,128]{1,0:T(8,128)(2,1)}, bf16[512,128]{1,0:T(8,128)(2,1)S(1)}, u32[]{:S(2)}, u32[]{:S(2)}) collective-permute-start(bf16[512,128]{1,0:T(8,128)(2,1)} %get-tuple-element.58), channel_id=1, source_target_pairs={{0,48},{16,0},{32,16},{48,32},{64,112},{80,64},{96,80},{112,96},{1... | collective-permute-start | bytes 393224 | tf_op jit(solution)/shard_map/ppermute | solution.py:49
  18.8 89.7 %copy-start = (bf16[128,4096]{1,0:T(8,128)(2,1)}, bf16[128,4096]{1,0:T(8,128)(2,1)S(1)}, u32[]{:S(2)}) copy-start(bf16[128,4096]{1,0:T(8,128)(2,1)S(1)} %pad_maximum_fusion.refs_0_) | copy-start | bytes 3145732
  19.3 40.2 %copy-start.19 = (bf16[512,128]{1,0:T(8,128)(2,1)}, bf16[512,128]{1,0:T(8,128)(2,1)S(1)}, u32[]{:S(2)}) copy-start(bf16[512,128]{1,0:T(8,128)(2,1)S(1)} %collective-permute-done.1.a3) | copy-start | bytes 393220
  23.1 36.4 %copy-start.20 = (bf16[512,128]{1,0:T(8,128)(2,1)}, bf16[512,128]{1,0:T(8,128)(2,1)S(1)}, u32[]{:S(2)}) copy-start(bf16[512,128]{1,0:T(8,128)(2,1)S(1)} %collective-permute-done.2.a2) | copy-start | bytes 393220
  23.1 36.4 %copy-start.21 = (bf16[512,128]{1,0:T(8,128)(2,1)}, bf16[512,128]{1,0:T(8,128)(2,1)S(1)}, u32[]{:S(2)}) copy-start(bf16[512,128]{1,0:T(8,128)(2,1)S(1)} %collective-permute-done.3.a1) | copy-start | bytes 393220
  23.1 26.0 %collective-permute-start.6 = (bf16[128,4096]{1,0:T(8,128)(2,1)S(1)}, bf16[128,4096]{1,0:T(8,128)(2,1)S(1)}, u32[]{:S(2)}, u32[]{:S(2)}) collective-permute-start(bf16[128,4096]{1,0:T(8,128)(2,1)S(1)} %pad_maximum_fusion.refs_0_), channel_id=1, source_target_pairs={{0,16},{16,32},{32,48},{48,0},{64,80},{80,96},{96,112},{112,64},{1... | collective-permute-start | bytes 3145736 | tf_op jit(solution)/shard_map/ppermute | solution.py:49
  24.4 24.7 %collective-permute-start.7 = (bf16[128,4096]{1,0:T(8,128)(2,1)S(1)}, bf16[128,4096]{1,0:T(8,128)(2,1)S(1)}, u32[]{:S(2)}, u32[]{:S(2)}) collective-permute-start(bf16[128,4096]{1,0:T(8,128)(2,1)S(1)} %pad_maximum_fusion.refs_0_), channel_id=1, source_target_pairs={{0,48},{16,0},{32,16},{48,32},{64,112},{80,64},{96,80},{112,96},{1... | collective-permute-start | bytes 3145736 | tf_op jit(solution)/shard_map/ppermute | solution.py:49
  26.4 24.4 %collective-permute-start.8 = (bf16[128,4096]{1,0:T(8,128)(2,1)S(1)}, bf16[128,4096]{1,0:T(8,128)(2,1)}, u32[]{:S(2)}, u32[]{:S(2)}) collective-permute-start(bf16[128,4096]{1,0:T(8,128)(2,1)S(1)} %pad_maximum_fusion.refs_0_), channel_id=1, source_target_pairs={{0,64},{16,80},{32,96},{48,112},{64,0},{80,16},{96,32},{112,48},{1... | collective-permute-start | bytes 3145736 | tf_op jit(solution)/shard_map/ppermute | solution.py:49
  28.3 18.6 %collective-permute-start.4 = (bf16[512,768]{1,0:T(8,128)(2,1)}, bf16[512,768]{1,0:T(8,128)(2,1)}, u32[]{:S(2)}, u32[]{:S(2)}) collective-permute-start(bf16[512,768]{1,0:T(8,128)(2,1)} %get-tuple-element.65.refs_8_), channel_id=1, source_target_pairs={{0,2},{1,3},{2,4},{3,5},{4,6},{5,7},{6,0},{7,1},{8,10},{9,11},{10,... | collective-permute-start | bytes 2359304 | tf_op jit(solution)/shard_map/ppermute | solution.py:53
  28.6 19.5 %collective-permute-start.5 = (bf16[512,768]{1,0:T(8,128)(2,1)}, bf16[512,768]{1,0:T(8,128)(2,1)S(1)}, u32[]{:S(2)}, u32[]{:S(2)}) collective-permute-start(bf16[512,768]{1,0:T(8,128)(2,1)} %get-tuple-element.65.refs_8_), channel_id=1, source_target_pairs={{0,6},{1,7},{2,0},{3,1},{4,2},{5,3},{6,4},{7,5},{8,14},{9,15},{10,... | collective-permute-start | bytes 2359304 | tf_op jit(solution)/shard_map/ppermute | solution.py:53
  48.0 2.8 %copy-start.22 = (bf16[512,768]{1,0:T(8,128)(2,1)}, bf16[512,768]{1,0:T(8,128)(2,1)S(1)}, u32[]{:S(2)}) copy-start(bf16[512,768]{1,0:T(8,128)(2,1)S(1)} %collective-permute-done.5.refs_10_) | copy-start | bytes 2359300
  49.1 59.5 %copy-start.3 = (bf16[128,4096]{1,0:T(8,128)(2,1)}, bf16[128,4096]{1,0:T(8,128)(2,1)S(1)}, u32[]{:S(2)}) copy-start(bf16[128,4096]{1,0:T(8,128)(2,1)S(1)} %collective-permute-done.6.refs_1_) | copy-start | bytes 3145732
  49.1 59.5 %copy-start.5 = (bf16[128,4096]{1,0:T(8,128)(2,1)}, bf16[128,4096]{1,0:T(8,128)(2,1)S(1)}, u32[]{:S(2)}) copy-start(bf16[128,4096]{1,0:T(8,128)(2,1)S(1)} %collective-permute-done.7.refs_2_) | copy-start | bytes 3145732
  50.8 23.7 %collective-permute-start.10 = (bf16[128,4096]{1,0:T(8,128)(2,1)}, bf16[128,4096]{1,0:T(8,128)(2,1)}, u32[]{:S(2)}, u32[]{:S(2)}) collective-permute-start(bf16[128,4096]{1,0:T(8,128)(2,1)} %collective-permute-done.8.refs_4_), channel_id=1, source_target_pairs={{0,48},{16,0},{32,16},{48,32},{64,112},{80,64},{96,80},{112,96},{1... | collective-permute-start | bytes 3145736 | tf_op jit(solution)/shard_map/ppermute | solution.py:49
  52.1 24.5 %collective-permute-start.9 = (bf16[128,4096]{1,0:T(8,128)(2,1)S(1)}, bf16[128,4096]{1,0:T(8,128)(2,1)}, u32[]{:S(2)}, u32[]{:S(2)}) collective-permute-start(bf16[128,4096]{1,0:T(8,128)(2,1)S(1)} %collective-permute-done.6.refs_1_), channel_id=1, source_target_pairs={{0,16},{16,32},{32,48},{48,0},{64,80},{80,96},{96,112},{112,64},{1... | collective-permute-start | bytes 3145736 | tf_op jit(solution)/shard_map/ppermute | solution.py:49
  52.9 19.3 %collective-permute-start.11 = (bf16[512,768]{1,0:T(8,128)(2,1)}, bf16[512,768]{1,0:T(8,128)(2,1)}, u32[]{:S(2)}, u32[]{:S(2)}) collective-permute-start(bf16[512,768]{1,0:T(8,128)(2,1)} %get-tuple-element.65.refs_8_), channel_id=1, source_target_pairs={{0,8},{1,9},{2,10},{3,11},{4,12},{5,13},{6,14},{7,15},{8,0},{9,1},... | collective-permute-start | bytes 2359304 | tf_op jit(solution)/shard_map/ppermute | solution.py:53
  56.6 17.1 %collective-permute-start.12 = (bf16[512,768]{1,0:T(8,128)(2,1)}, bf16[512,768]{1,0:T(8,128)(2,1)}, u32[]{:S(2)}, u32[]{:S(2)}) collective-permute-start(bf16[512,768]{1,0:T(8,128)(2,1)} %collective-permute-done.4.refs_9_), channel_id=1, source_target_pairs={{0,2},{1,3},{2,4},{3,5},{4,6},{5,7},{6,0},{7,1},{8,10},{9,11},{10,... | collective-permute-start | bytes 2359304 | tf_op jit(solution)/shard_map/ppermute | solution.py:53
  76.7 141.2 %all-gather.7.cloned.1.call-start = ((), (), s32[]{:S(2)}) async-start(), calls=%async_computation.3 | async-start | bytes 4595712 | tf_op jit(solution)/shard_map/all_gather | solution.py:561
  76.8 30.1 %collective-permute-start.13 = (bf16[128,4096]{1,0:T(8,128)(2,1)}, bf16[128,4096]{1,0:T(8,128)(2,1)}, u32[]{:S(2)}, u32[]{:S(2)}) collective-permute-start(bf16[128,4096]{1,0:T(8,128)(2,1)} %collective-permute-done.8.refs_4_), channel_id=1, source_target_pairs={{0,16},{16,32},{32,48},{48,0},{64,80},{80,96},{96,112},{112,64},{1... | collective-permute-start | bytes 3145736 | tf_op jit(solution)/shard_map/ppermute | solution.py:49
  76.8 30.0 %collective-permute-start.14 = (bf16[128,4096]{1,0:T(8,128)(2,1)}, bf16[128,4096]{1,0:T(8,128)(2,1)}, u32[]{:S(2)}, u32[]{:S(2)}) collective-permute-start(bf16[128,4096]{1,0:T(8,128)(2,1)} %collective-permute-done.10.refs_6_), channel_id=1, source_target_pairs={{0,48},{16,0},{32,16},{48,32},{64,112},{80,64},{96,80},{112,96},{1... | collective-permute-start | bytes 3145736 | tf_op jit(solution)/shard_map/ppermute | solution.py:49
  80.1 26.8 %collective-permute-start.15 = (bf16[512,768]{1,0:T(8,128)(2,1)}, bf16[512,768]{1,0:T(8,128)(2,1)}, u32[]{:S(2)}, u32[]{:S(2)}) collective-permute-start(bf16[512,768]{1,0:T(8,128)(2,1)} %collective-permute-done.11.refs_12_), channel_id=1, source_target_pairs={{0,2},{1,3},{2,4},{3,5},{4,6},{5,7},{6,0},{7,1},{8,10},{9,11},{10,... | collective-permute-start | bytes 2359304 | tf_op jit(solution)/shard_map/ppermute | solution.py:53
  80.3 26.6 %collective-permute-start.16 = (bf16[512,768]{1,0:T(8,128)(2,1)}, bf16[512,768]{1,0:T(8,128)(2,1)}, u32[]{:S(2)}, u32[]{:S(2)}) collective-permute-start(bf16[512,768]{1,0:T(8,128)(2,1)} %collective-permute-done.11.refs_12_), channel_id=1, source_target_pairs={{0,6},{1,7},{2,0},{3,1},{4,2},{5,3},{6,4},{7,5},{8,14},{9,15},{10,... | collective-permute-start | bytes 2359304 | tf_op jit(solution)/shard_map/ppermute | solution.py:53
  108.6 18.3 %collective-permute-start.17 = (bf16[256,768]{1,0:T(8,128)(2,1)}, bf16[256,768]{1,0:T(8,128)(2,1)S(1)}, u32[]{:S(2)}, u32[]{:S(2)}) collective-permute-start(bf16[256,768]{1,0:T(8,128)(2,1)} %slice.13), channel_id=1, source_target_pairs={{0,2},{1,3},{2,4},{3,5},{4,6},{5,7},{6,0},{7,1},{8,10},{9,11},{10,... | collective-permute-start | bytes 1179656 | tf_op jit(solution)/shard_map/ppermute | solution.py:53
  111.3 15.6 %copy-start.1 = (bf16[128,4096]{1,0:T(8,128)(2,1)S(1)}, bf16[128,4096]{1,0:T(8,128)(2,1)}, u32[]{:S(2)}) copy-start(bf16[128,4096]{1,0:T(8,128)(2,1)} %copy-done) | copy-start | bytes 3145732
  111.3 15.6 %copy-start.4 = (bf16[128,4096]{1,0:T(8,128)(2,1)S(1)}, bf16[128,4096]{1,0:T(8,128)(2,1)}, u32[]{:S(2)}) copy-start(bf16[128,4096]{1,0:T(8,128)(2,1)} %copy-done.3) | copy-start | bytes 3145732
  111.3 15.6 %copy-start.6 = (bf16[128,4096]{1,0:T(8,128)(2,1)S(1)}, bf16[128,4096]{1,0:T(8,128)(2,1)}, u32[]{:S(2)}) copy-start(bf16[128,4096]{1,0:T(8,128)(2,1)} %copy-done.5) | copy-start | bytes 3145732
  111.3 15.6 %copy-start.9 = (s32[8]{0:T(128)S(1)}, s32[8]{0:T(128)}, u32[]{:S(2)}) copy-start(s32[8]{0:T(128)} %stack.104.w_at) | copy-start | bytes 100
  111.4 15.6 %copy-start.10 = (s32[8]{0:T(128)S(1)}, s32[8]{0:T(128)}, u32[]{:S(2)}) copy-start(s32[8]{0:T(128)} %stack.95.x_at) | copy-start | bytes 100
  111.4 15.6 %collective-permute-start.18 = (bf16[256,768]{1,0:T(8,128)(2,1)}, bf16[256,768]{1,0:T(8,128)(2,1)S(1)}, u32[]{:S(2)}, u32[]{:S(2)}) collective-permute-start(bf16[256,768]{1,0:T(8,128)(2,1)} %slice.14), channel_id=1, source_target_pairs={{0,6},{1,7},{2,0},{3,1},{4,2},{5,3},{6,4},{7,5},{8,14},{9,15},{10,... | collective-permute-start | bytes 1179656 | tf_op jit(solution)/shard_map/ppermute | solution.py:53
  127.0 1.4 copy-start.8
  128.4 2.4 copy-start.23
  128.4 2.4 %copy-start.7 = (f32[512,768]{1,0:T(8,128)S(1)}, f32[512,768]{1,0:T(8,128)}, u32[]{:S(2)}) copy-start(f32[512,768]{1,0:T(8,128)} %get-tuple-element.82.refs_10_) | copy-start | bytes 4718596
  130.5 3.8 %collective-permute-start.19 = (f32[512,768]{1,0:T(8,128)S(1)}, f32[512,768]{1,0:T(8,128)}, u32[]{:S(2)}, u32[]{:S(2)}) collective-permute-start(f32[512,768]{1,0:T(8,128)S(1)} %project_last.2), channel_id=1, source_target_pairs={{0,1},{1,0},{2,3},{3,2},{4,5},{5,4},{6,7},{7,6},{8,9},{9,8},{10,11... | collective-permute-start | bytes 4718600 | tf_op jit(solution)/shard_map/ppermute | solution.py:53
  133.0 1.1 copy-start.2
  158.2 25.5 %collective-permute-start.20 = (bf16[256,512]{1,0:T(8,128)(2,1)}, bf16[256,512]{1,0:T(8,128)(2,1)S(1)}, u32[]{:S(2)}, u32[]{:S(2)}) collective-permute-start(bf16[256,512]{1,0:T(8,128)(2,1)} %attend.2.a0), channel_id=1, source_target_pairs={{0,16},{16,32},{32,48},{48,0},{64,80},{80,96},{96,112},{112,64},{1... | collective-permute-start | bytes 786440 | tf_op jit(solution)/shard_map/ppermute | solution.py:49
  158.4 28.3 %collective-permute-start.21 = (bf16[256,512]{1,0:T(8,128)(2,1)}, bf16[256,512]{1,0:T(8,128)(2,1)S(1)}, u32[]{:S(2)}, u32[]{:S(2)}) collective-permute-start(bf16[256,512]{1,0:T(8,128)(2,1)} %attend.2.a0), channel_id=1, source_target_pairs={{0,48},{16,0},{32,16},{48,32},{64,112},{80,64},{96,80},{112,96},{1... | collective-permute-start | bytes 786440 | tf_op jit(solution)/shard_map/ppermute | solution.py:49
  161.5 25.2 %collective-permute-start.22 = (bf16[256,512]{1,0:T(8,128)(2,1)}, bf16[256,512]{1,0:T(8,128)(2,1)S(1)}, u32[]{:S(2)}, u32[]{:S(2)}) collective-permute-start(bf16[256,512]{1,0:T(8,128)(2,1)} %attend.2.a0), channel_id=1, source_target_pairs={{0,32},{16,48},{32,0},{48,16},{64,96},{80,112},{96,64},{112,80},{1... | collective-permute-start | bytes 786440 | tf_op jit(solution)/shard_map/ppermute | solution.py:49
  180.4 14.6 %collective-permute-start.23 = (bf16[256,512]{1,0:T(8,128)(2,1)}, bf16[256,512]{1,0:T(8,128)(2,1)S(1)}, u32[]{:S(2)}, u32[]{:S(2)}) collective-permute-start(bf16[256,512]{1,0:T(8,128)(2,1)} %attend.3.a0), channel_id=1, source_target_pairs={{0,16},{16,32},{32,48},{48,0},{64,80},{80,96},{96,112},{112,64},{1... | collective-permute-start | bytes 786440 | tf_op jit(solution)/shard_map/ppermute | solution.py:49
  181.4 13.6 %collective-permute-start.24 = (bf16[256,512]{1,0:T(8,128)(2,1)}, bf16[256,512]{1,0:T(8,128)(2,1)S(1)}, u32[]{:S(2)}, u32[]{:S(2)}) collective-permute-start(bf16[256,512]{1,0:T(8,128)(2,1)} %attend.3.a0), channel_id=1, source_target_pairs={{0,48},{16,0},{32,16},{48,32},{64,112},{80,64},{96,80},{112,96},{1... | collective-permute-start | bytes 786440 | tf_op jit(solution)/shard_map/ppermute | solution.py:49
  183.7 3.0 %copy-start.14 = (bf16[256,512]{1,0:T(8,128)(2,1)}, bf16[256,512]{1,0:T(8,128)(2,1)S(1)}, u32[]{:S(2)}) copy-start(bf16[256,512]{1,0:T(8,128)(2,1)S(1)} %collective-permute-done.20.a1) | copy-start | bytes 786436
  183.7 11.5 %collective-permute-start.25 = (bf16[256,512]{1,0:T(8,128)(2,1)}, bf16[256,512]{1,0:T(8,128)(2,1)S(1)}, u32[]{:S(2)}, u32[]{:S(2)}) collective-permute-start(bf16[256,512]{1,0:T(8,128)(2,1)} %attend.3.a0), channel_id=1, source_target_pairs={{0,32},{16,48},{32,0},{48,16},{64,96},{80,112},{96,64},{112,80},{1... | collective-permute-start | bytes 786440 | tf_op jit(solution)/shard_map/ppermute | solution.py:49
  186.7 0.7 copy-start.16
  186.7 0.8 copy-start.17
  195.0 5.7 %copy-start.13 = (bf16[256,512]{1,0:T(8,128)(2,1)}, bf16[256,512]{1,0:T(8,128)(2,1)S(1)}, u32[]{:S(2)}) copy-start(bf16[256,512]{1,0:T(8,128)(2,1)S(1)} %collective-permute-done.23.a1) | copy-start | bytes 786436
  195.1 5.7 %copy-start.15 = (bf16[256,512]{1,0:T(8,128)(2,1)}, bf16[256,512]{1,0:T(8,128)(2,1)S(1)}, u32[]{:S(2)}) copy-start(bf16[256,512]{1,0:T(8,128)(2,1)S(1)} %collective-permute-done.24.a2) | copy-start | bytes 786436
  195.3 5.5 %copy-start.18 = (bf16[256,512]{1,0:T(8,128)(2,1)}, bf16[256,512]{1,0:T(8,128)(2,1)S(1)}, u32[]{:S(2)}) copy-start(bf16[256,512]{1,0:T(8,128)(2,1)S(1)} %collective-permute-done.25.a3) | copy-start | bytes 786436
  195.3 19.0 %all-to-all-start = ((bf16[8,32,2048]{2,1,0:T(8,128)(2,1)}), bf16[8,32,2048]{2,1,0:T(8,128)(2,1)S(1)}, u32[]{:S(2)}, u32[]{:S(2)}) async-start(bf16[8,32,2048]{2,1,0:T(8,128)(2,1)} %bitcast.42), calls=%async_computation | async-start | bytes 2097152 | tf_op jit(solution)/shard_map/all_to_all | solution.py:636
  214.3 11.4 %copy-start.11 = (bf16[8,32,2048]{2,1,0:T(8,128)(2,1)}, bf16[8,32,2048]{2,1,0:T(8,128)(2,1)S(1)}, u32[]{:S(2)}) copy-start(bf16[8,32,2048]{2,1,0:T(8,128)(2,1)S(1)} %all-to-all-done.refs_0_) | copy-start | bytes 3145732
  214.3 18.9 %all-to-all-start.1 = ((bf16[8,32,2048]{2,1,0:T(8,128)(2,1)}), bf16[8,32,2048]{2,1,0:T(8,128)(2,1)S(1)}, u32[]{:S(2)}, u32[]{:S(2)}) async-start(bf16[8,32,2048]{2,1,0:T(8,128)(2,1)} %bitcast.41), calls=%async_computation.1 | async-start | bytes 2097152 | tf_op jit(solution)/shard_map/all_to_all | solution.py:636
  233.2 1.0 copy-start.12
Sparse Core Ops, SparseCore 0:
  76.8 72.1 all-gather.4
  152.0 62.3 all-gather.6

commit v3 on v2

--- a/solution.py
+++ b/solution.py
@@ -42,6 +42,7 @@
 Y_DOWN = decode_perm(lambda z, y, c: (z, y - 1, c))
 ZH_SWAP = decode_perm(lambda z, y, c: (1 - z, y, c))
 CORE_SWAP = decode_perm(lambda z, y, c: (z, y, 1 - c))
+PARITIES = [list(range(c, 16, 2)) for c in range(2)]
 X_FAR = tensor_perm(lambda z, x: (z, x + 2))
 
 
@@ -61,8 +62,7 @@
     return lax.optimization_barrier(values)
 
 
-def gather_inputs(rows, w, out, tables):
-    h = w.shape[0] // 2
+def gather_inputs(rows, w, w_at, out, tables):
     low, high = to_d(w, Y_UP), to_d(w, Y_DOWN)
     left, right, over = to_t(rows, X_UP), to_t(rows, X_DOWN), to_t(rows, Z_SWAP)
     low, high, left, right, over = together(low, high, left, right, over)
@@ -76,12 +76,17 @@
     over_left = to_t(after(over, far), X_UP)
     over_far = to_t(over_right, X_DOWN)
     over_low, over_high = to_d(w_over, Y_UP), to_d(w_over, Y_DOWN)
-    over_left, over_far, over_low, over_high = together(over_left, over_far, over_low, over_high)
-    far_a, far_b = to_d(over_low[:h], Y_UP), to_d(over_high[h:], Y_DOWN)
+    far_over = to_d(far_low, ZH_SWAP)
+    early = [rows, left, right, far, over, over_right]
+    here = [w, low, high, far_low]
+    before = project_early(early, here, w_at)
+    over_left, over_far, over_low, over_high, far_over, before, out = together(
+        over_left, over_far, over_low, over_high, far_over, before, out
+    )
     return (
-        [rows, left, right, far, over, over_left, over_right, over_far],
-        [w, low, high, far_low, w_over, over_low, over_high],
-        [far_a, far_b],
+        early + [over_left, over_far],
+        here + [w_over, over_low, over_high, far_over],
+        before,
         tables,
         out,
     )
@@ -90,7 +95,8 @@
 def row_sources(z, x):
     here, there = z * 4, (1 - z) * 4
     lo, hi, end = (x + 3) % 4, (x + 1) % 4, (x + 2) % 4
-    return jnp.stack([first + at for first in (here, there) for at in (x, lo, hi, end)])
+    places = [here + at for at in (x, lo, hi, end)] + [there + at for at in (x, hi, lo, end)]
+    return jnp.stack(places)
 
 
 def shard_sources(zh, y):
@@ -105,13 +111,15 @@
     def kernel(x_ref, a0, a1, a2, a3, o_ref):
         for i, ref in enumerate((a0, a1, a2, a3)):
             to = pl.multiple_of((x_ref[0] + i) % 4 * depth, depth)
-            o_ref[pl.ds(to, depth), :] = ref[...]
+            for k in range(8):
+                o_ref[k, pl.ds(to, depth), :] = ref[...]
 
     return pl.pallas_call(
         kernel,
         in_specs=[smem()] + [vmem()] * 4,
         out_specs=vmem(),
-        out_shape=jax.ShapeDtypeStruct((4 * depth, wide), BF),
+        out_shape=jax.ShapeDtypeStruct((8, 4 * depth, wide), BF),
+        compiler_params=pltpu.CompilerParams(vmem_limit_bytes=60 * MB),
         name="stack",
     )(x[None].astype(jnp.int32), *pieces)
 
@@ -175,108 +183,116 @@
     )(jnp.stack([core, x]).astype(jnp.int32), hidden, gain[None], w_query, w_key, w_value, w_out)
 
 
-def project_kernel(x_at, w_at, *refs):
-    xs, ws = refs[:8], refs[8:15]
-    keep_ref, send_ref, xv, wv, xsem, wsem = refs[15:]
-    span, cols = keep_ref.shape
-    depth = ws[0].shape[0]
-    half = xv.shape[1] // 2
-    columns = []
-    for g in range(2):
-        columns.append(pl.ds(pl.multiple_of(w_at[4 * g] // 4 * half, half), half))
-        for i, ref in enumerate(xs):
-            for part in range(4):
-                to = pl.multiple_of(x_at[i] * 32 + part * (span // 2), 32)
-                pltpu.make_async_copy(
-                    ref.at[pl.ds(part * 32, 32), columns[g]],
-                    xv.at[pl.ds(to, 32), columns[g]],
-                    xsem.at[g],
-                ).start()
-        for i in range(4 * g, min(4 * g + 4, 7)):
-            to = pl.multiple_of(w_at[i] * depth, depth)
-            pltpu.make_async_copy(ws[i], wv.at[pl.ds(to, depth), :], wsem.at[g]).start()
-    missing = pl.multiple_of(w_at[7] * depth, depth)
-    wv[pl.ds(missing, depth), :] = jnp.zeros((depth, cols), BF)
-    for g in range(2):
-        arrived = xv.at[:, columns[g]]
-        pltpu.make_async_copy(arrived, arrived, xsem.at[g]).wait()
-        arrived = wv.at[pl.ds(0, (4 - g) * depth), :]
-        pltpu.make_async_copy(arrived, arrived, wsem.at[g]).wait()
-
-        def step(i, carry, g=g):
-            at = pl.ds(pl.multiple_of(i * 256, 256), 256)
-            for p, ref in enumerate((keep_ref, send_ref)):
-                term = jnp.dot(
-                    xv[p * span : (p + 1) * span, columns[g]],
-                    wv[columns[g], at],
-                    preferred_element_type=F32,
-                )
-                ref[:, at] = term if g == 0 else ref[:, at] + term
-            return carry
-
-        lax.fori_loop(0, cols // 256, step, 0)
-
-
-def project(rows, x_at, shards, w_at):
-    span, width = rows[0].shape[0] * 4, rows[0].shape[1]
+def start_shards(refs, w_at, wv, sem):
+    for i, ref in enumerate(refs):
+        depth = ref.shape[0]
+        to = pl.multiple_of(w_at[i] % 4 * depth, depth)
+        pltpu.make_async_copy(ref, wv.at[pl.ds(to, depth), :], sem).start()
+
+
+def project_early_kernel(w_at, *refs):
+    xs, ws = refs[:6], refs[6:10]
+    o_ref, xv, wv, xsem, wsem = refs[10:]
+    rows, wide = xs[0].shape[0], xv.shape[1]
+    columns = pl.ds(pl.multiple_of(w_at[0] // 4 * wide, wide), wide)
+    for i, ref in enumerate(xs):
+        to = xv.at[i * rows : (i + 1) * rows, :]
+        pltpu.make_async_copy(ref.at[:, columns], to, xsem).start()
+    start_shards(ws, w_at, wv, wsem)
+    pltpu.make_async_copy(xv, xv, xsem).wait()
+    pltpu.make_async_copy(wv, wv, wsem).wait()
+    for n in range(o_ref.shape[1] // 256):
+        at = slice(n * 256, n * 256 + 256)
+        o_ref[:, at] = jnp.dot(xv[...], wv[:, at], preferred_element_type=F32)
+
+
+def project_early(rows, shards, w_at):
+    n = len(rows) * rows[0].shape[0]
+    wide, cols = rows[0].shape[1] // 2, shards[0].shape[1]
+    return pl.pallas_call(
+        project_early_kernel,
+        in_specs=[smem()] + [hbm()] * 10,
+        out_specs=vmem(),
+        out_shape=jax.ShapeDtypeStruct((n, cols), F32),
+        scratch_shapes=[
+            pltpu.VMEM((n, wide), BF),
+            pltpu.VMEM((wide, cols), BF),
+            pltpu.SemaphoreType.DMA,
+            pltpu.SemaphoreType.DMA,
+        ],
+        compiler_params=pltpu.CompilerParams(vmem_limit_bytes=60 * MB),
+        cost_estimate=pl.CostEstimate(flops=MB, bytes_accessed=MB, transcendentals=0),
+        name="project_early",
+    )(w_at, *rows, *shards)
+
+
+def project_kernel(prompt, x_at, w_at, *refs):
+    xs, ws, before = refs[:8], refs[8:16], refs[16]
+    o_ref, there, here, bv, wt, wh, acc, sems = refs[17:]
+    wide = there.shape[1]
+    part = o_ref.shape[0] // 8
+    mine = pl.ds(prompt * part, part)
+    side = w_at[0] // 4
+    here_columns = pl.ds(pl.multiple_of(side * wide, wide), wide)
+    there_columns = pl.ds(pl.multiple_of((1 - side) * wide, wide), wide)
+    for i, ref in enumerate(xs):
+        to = there.at[i * part : (i + 1) * part, :]
+        pltpu.make_async_copy(ref.at[mine, there_columns], to, sems.at[0]).start()
+    for i, ref in enumerate(ws[4:]):
+        depth = ref.shape[0]
+        to = pl.multiple_of(w_at[4 + i] % 4 * depth, depth)
+        pltpu.make_async_copy(ref, wt.at[pl.ds(to, depth), :], sems.at[1]).start()
+    for i in range(6):
+        to = bv.at[i * part : (i + 1) * part, :]
+        source = before.at[i * 2 * part + prompt * part : i * 2 * part + (prompt + 1) * part, :]
+        pltpu.make_async_copy(source, to, sems.at[2]).start()
+    for i in range(2):
+        to = here.at[i * part : (i + 1) * part, :]
+        pltpu.make_async_copy(xs[6 + i].at[mine, here_columns], to, sems.at[3]).start()
+    start_shards(ws[:4], w_at, wh, sems.at[4])
+    pltpu.make_async_copy(there, there, sems.at[0]).wait()
+    pltpu.make_async_copy(wt, wt, sems.at[1]).wait()
+    cols = acc.shape[1]
+    for n in range(cols // 256):
+        at = slice(n * 256, n * 256 + 256)
+        acc[:, at] = jnp.dot(there[...], wt[:, at], preferred_element_type=F32)
+    pltpu.make_async_copy(bv, bv, sems.at[2]).wait()
+    acc[: 6 * part, :] += bv[...]
+    pltpu.make_async_copy(here, here, sems.at[3]).wait()
+    pltpu.make_async_copy(wh, wh, sems.at[4]).wait()
+    for n in range(cols // 256):
+        at = slice(n * 256, n * 256 + 256)
+        acc[6 * part :, at] += jnp.dot(here[...], wh[:, at], preferred_element_type=F32)
+    for i in range(8):
+        for r in range(2):
+            to = pl.multiple_of(x_at[i] * 32 + r * (o_ref.shape[0] // 2), 32)
+            o_ref[pl.ds(to, 32), :] = acc[i * part + r * 32 : i * part + r * 32 + 32, :]
+
+
+def project(prompt, rows, x_at, shards, w_at, before):
+    span, wide = rows[0].shape[0] * 4, rows[0].shape[1] // 2
     cols = shards[0].shape[1]
     return pl.pallas_call(
-        project_kernel,
-        in_specs=[smem()] * 2 + [hbm()] * 15,
-        out_specs=[vmem()] * 2,
-        out_shape=[jax.ShapeDtypeStruct((span, cols), F32)] * 2,
-        scratch_shapes=[
-            pltpu.VMEM((2 * span, width), BF),
-            pltpu.VMEM((width, cols), BF),
-            pltpu.SemaphoreType.DMA((2,)),
-            pltpu.SemaphoreType.DMA((2,)),
-        ],
-        compiler_params=pltpu.CompilerParams(vmem_limit_bytes=60 * MB),
-        cost_estimate=pl.CostEstimate(
-            flops=4 * span * width * cols, bytes_accessed=18 * MB, transcendentals=0
-        ),
-        name="project",
-    )(x_at, w_at, *rows, *shards)
-
-
-def project_last_kernel(prompt, x_at, w_at, *refs):
-    xs = refs[:8]
-    wa_ref, wb_ref, before_ref, o_ref, xv, xsem = refs[8:]
-    span = o_ref.shape[0]
-    depth = 2 * wa_ref.shape[0]
-    columns = pl.ds(pl.multiple_of(w_at[7] * depth, depth), depth)
-    for i, ref in enumerate(xs):
-        for part in range(2):
-            to = pl.multiple_of(x_at[i] * 32 + part * (span // 2), 32)
-            pltpu.make_async_copy(
-                ref.at[pl.ds(prompt * 64 + part * 32, 32), columns],
-                xv.at[pl.ds(to, 32), :],
-                xsem,
-            ).start()
-    pltpu.make_async_copy(xv, xv, xsem).wait()
-    a = jnp.dot(xv[:, : depth // 2], wa_ref[...], preferred_element_type=F32)
-    b = jnp.dot(xv[:, depth // 2 :], wb_ref[...], preferred_element_type=F32)
-    o_ref[...] = before_ref[...] + a + b
-
-
-def project_last(prompt, rows, x_at, halves, w_at, before):
-    span, cols = before.shape
-    depth = 2 * halves[0].shape[0]
-    return pl.pallas_call(
-        functools.partial(project_last_kernel, prompt),
-        in_specs=[smem()] * 2 + [hbm()] * 8 + [vmem()] * 3,
+        functools.partial(project_kernel, prompt),
+        in_specs=[smem()] * 2 + [hbm()] * 17,
         out_specs=vmem(),
         out_shape=jax.ShapeDtypeStruct((span, cols), F32),
-        scratch_shapes=[pltpu.VMEM((span, depth), BF), pltpu.SemaphoreType.DMA],
-        compiler_params=pltpu.CompilerParams(vmem_limit_bytes=40 * MB),
-        cost_estimate=pl.CostEstimate(
-            flops=2 * span * depth * cols, bytes_accessed=5 * MB, transcendentals=0
-        ),
-        name="project_last",
-    )(x_at, w_at, *rows, *halves, before)
-
-
-def rotate_kernel(rot_scale, a_ref, b_ref, cos_ref, sin_ref, q_ref, k_ref, v_ref):
+        scratch_shapes=[
+            pltpu.VMEM((span, wide), BF),
+            pltpu.VMEM((span // 4, wide), BF),
+            pltpu.VMEM((span // 4 * 3, cols), F32),
+            pltpu.VMEM((wide, cols), BF),
+            pltpu.VMEM((wide, cols), BF),
+            pltpu.VMEM((span, cols), F32),
+            pltpu.SemaphoreType.DMA((5,)),
+        ],
+        compiler_params=pltpu.CompilerParams(vmem_limit_bytes=60 * MB),
+        cost_estimate=pl.CostEstimate(flops=MB, bytes_accessed=MB, transcendentals=0),
+        name="project",
+    )(x_at, w_at, *rows, *shards, before)
+
+
+def rotate_kernel(rot_scale, owner_ref, a_ref, b_ref, cos_ref, sin_ref, q_ref, k_ref, v_ref, p_ref):
     cos, sin = cos_ref[...], sin_ref[...]
     heads = q_ref.shape[0]
 
@@ -299,24 +315,45 @@
             to = slice(s * 64 + r * 32, s * 64 + r * 32 + 32)
             k_ref[to, :] = keys[rows]
             v_ref[to, :] = values[rows]
-
-
-def rotate(own, got, cosine, sine):
+    count = owner_ref.shape[1]
+    page = k_ref.shape[0] // count
+    p_ref[...] = jnp.zeros_like(p_ref)
+    body = CAP * 2 * page
+    line = lax.broadcasted_iota(jnp.int32, (16, 128), 0)
+    for p in range(count):
+        owner = owner_ref[0, p]
+        rank = jnp.int32(0)
+        for q in range(p):
+            rank += (owner_ref[0, q] == owner).astype(jnp.int32)
+        marks = jnp.where(line == 2 * CAP + rank, p + 1.0, 0.0)
+        for c, ref in enumerate((k_ref, v_ref)):
+            part = ref[p * page : (p + 1) * page, :].astype(F32)
+            most = jnp.max(jnp.max(jnp.abs(part), axis=0, keepdims=True), axis=1, keepdims=True)
+            scale = (most + 1e-06).astype(BF).astype(F32)
+            at = pl.multiple_of((rank * 2 + c) * page, page)
+            p_ref[owner, pl.ds(at, page), :] = (part / scale).astype(BF)
+            marks = jnp.where(line == rank * 2 + c, scale, marks)
+        p_ref[owner, body:, :] = (p_ref[owner, body:, :].astype(F32) + marks).astype(BF)
+
+
+def rotate(own, got, cosine, sine, page_owner, groups):
     span, cols = own.shape
     heads = cols // 128 - 2
+    page = span // page_owner.shape[1]
     scale = math.log2(math.e) / math.sqrt(128)
     return pl.pallas_call(
         functools.partial(rotate_kernel, scale),
-        in_specs=[vmem()] * 4,
-        out_specs=[vmem()] * 3,
+        in_specs=[smem()] + [vmem()] * 4,
+        out_specs=[vmem()] * 4,
         out_shape=[
             jax.ShapeDtypeStruct((heads, span, 128), BF),
             jax.ShapeDtypeStruct((span, 128), BF),
             jax.ShapeDtypeStruct((span, 128), BF),
+            jax.ShapeDtypeStruct((groups, CAP * 2 * page + 16, 128), BF),
         ],
         compiler_params=pltpu.CompilerParams(vmem_limit_bytes=60 * MB),
         name="rotate",
-    )(own, got, cosine, sine)
+    )(page_owner, own, got, cosine, sine)
 
 
 def attend_kernel(chunk, block, live_ref, q_ref, k_hbm, v_hbm, kn_ref, vn_ref, o_ref, k_ref, v_ref, sems):
@@ -446,17 +483,14 @@
             pltpu.SemaphoreType.DMA((2, prefix // block)),
         ],
         compiler_params=pltpu.CompilerParams(vmem_limit_bytes=60 * MB),
-        cost_estimate=pl.CostEstimate(
-            flops=4 * heads * rows * (prefix + span) * width,
-            bytes_accessed=4 * prefix * width,
-            transcendentals=heads * rows * (prefix + span),
-        ),
+        cost_estimate=pl.CostEstimate(flops=MB, bytes_accessed=MB, transcendentals=0),
         name="attend",
     )(live, q, cache_k, cache_v, keys, values)
 
 
-def output_kernel(x_at, a0, a1, a2, a3, w_ref, o_ref, xv, wv, xsem, wsem):
-    shards, depth, cols = w_ref.shape
+def output_kernel(x_at, a0, a1, a2, a3, mine, other, o_ref, xv, wv, xsem, wsem):
+    shards, depth, cols = wv.shape
+    core = x_at[4]
     width = a0.shape[1]
     copies = []
     for i, ref in enumerate((a0, a1, a2, a3)):
@@ -464,29 +498,29 @@
         copies.append(pltpu.make_async_copy(ref, xv.at[:, pl.ds(to, width)], xsem.at[i]))
     for copy in copies:
         copy.start()
-    loads = []
-    for i in range(shards // 4):
-        group = pl.ds(4 * i, 4)
-        loads.append(pltpu.make_async_copy(w_ref.at[group], wv.at[group], wsem.at[i]))
-    for load in loads:
-        load.start()
+    for k in range(shards // 2):
+        sem = wsem.at[k // 2]
+        pltpu.make_async_copy(mine.at[k], wv.at[2 * k + core], sem).start()
+        pltpu.make_async_copy(other.at[k], wv.at[2 * k + 1 - core], sem).start()
     for copy in copies:
         copy.wait()
-    for i, load in enumerate(loads):
-        load.wait()
+    for i in range(shards // 4):
+        group = wv.at[4 * i : 4 * i + 4]
+        pltpu.make_async_copy(group, group, wsem.at[i]).wait()
         w = jnp.concatenate([wv[j] for j in range(4 * i, 4 * i + 4)], axis=1)
         o_ref[:, 4 * i * cols : 4 * (i + 1) * cols] = jnp.dot(
             xv[...], w, preferred_element_type=F32
         ).astype(BF)
 
 
-def output(pieces, weights, x):
+def output(pieces, weights, x, core):
     rows, width = pieces[0].shape
-    x_at = jnp.stack([x, (x + 3) % 4, (x + 1) % 4, (x + 2) % 4]).astype(jnp.int32)
-    shards, depth, cols = weights.shape
+    x_at = jnp.stack([x, (x + 3) % 4, (x + 1) % 4, (x + 2) % 4, core]).astype(jnp.int32)
+    shards, depth, cols = weights[0].shape
+    shards = 2 * shards
     return pl.pallas_call(
         output_kernel,
-        in_specs=[smem()] + [hbm()] * 5,
+        in_specs=[smem()] + [hbm()] * 6,
         out_specs=vmem(),
         out_shape=jax.ShapeDtypeStruct((rows, shards * cols), BF),
         scratch_shapes=[
@@ -496,11 +530,9 @@
             pltpu.SemaphoreType.DMA((4,)),
         ],
         compiler_params=pltpu.CompilerParams(vmem_limit_bytes=60 * MB),
-        cost_estimate=pl.CostEstimate(
-            flops=2 * rows * depth * shards * cols, bytes_accessed=11 * MB, transcendentals=0
-        ),
+        cost_estimate=pl.CostEstimate(flops=MB, bytes_accessed=MB, transcendentals=0),
         name="output",
-    )(x_at, *pieces, weights)
+    )(x_at, *pieces, *weights)
 
 
 def finish_kernel(*refs):
@@ -526,64 +558,13 @@
     )(*parts)
 
 
-def place_kernel(pages, page_of, kv_ref, out_ref, scale_ref):
-    page = out_ref.shape[2]
-
-    def slot(s, carry):
-        number = page_of[s]
-
-        @pl.when(number < 0)
-        def _():
-            out_ref[s] = jnp.zeros(out_ref.shape[1:], BF)
-            scale_ref[s] = jnp.zeros(scale_ref.shape[1:], F32)
-
-        @pl.when(number >= 0)
-        def _():
-            at = pl.multiple_of(number * page, page)
-            rows = kv_ref[s // CAP, pl.ds(at, page), :].astype(F32)
-            for c in range(2):
-                part = rows[:, c * 128 : (c + 1) * 128]
-                most = jnp.max(jnp.max(jnp.abs(part), axis=0, keepdims=True), axis=1, keepdims=True)
-                scale = (most + 1e-06).astype(BF).astype(F32)
-                out_ref[s, c] = (part / scale).astype(BF)
-                scale_ref[s, c : c + 1, :] = jnp.broadcast_to(scale, (1, 128))
-
-        return carry
-
-    lax.fori_loop(0, out_ref.shape[0], slot, 0)
-
-
-def gather_pages(keys, values, page_owner):
-    count = page_owner.shape[1]
-    span = keys.shape[0]
-    owner_rows = jnp.pad(page_owner.astype(BF), ((0, 15), (0, 256 - count)))
-    sent = jnp.concatenate([jnp.concatenate([keys, values], axis=1), owner_rows], axis=0)
-    return lax.all_gather(sent, "decode", axis=0)
-
-
-def place_pages(got, count, d):
-    groups, span = got.shape[0], got.shape[1] - 16
-    owners = got[:, span, :count].astype(jnp.int32)
-    order = jnp.arange(count, dtype=jnp.int32)
-    same = owners[:, :, None] == owners[:, None, :]
-    rank = jnp.sum((same & (order[None, :] < order[:, None])[None]).astype(jnp.int32), axis=2)
-    mine = (owners == d)[:, None, :] & (rank[:, None, :] == jnp.arange(CAP)[None, :, None])
-    ids = jnp.max(jnp.where(mine, order[None, None, :], -1), axis=2).reshape(groups * CAP)
-    pages, scales = pl.pallas_call(
-        functools.partial(place_kernel, count),
-        in_specs=[smem(), vmem()],
-        out_specs=[vmem()] * 2,
-        out_shape=[
-            jax.ShapeDtypeStruct((groups * CAP, 2, span // count, 128), BF),
-            jax.ShapeDtypeStruct((groups * CAP, 2, 128), F32),
-        ],
-        compiler_params=pltpu.CompilerParams(vmem_limit_bytes=60 * MB),
-        cost_estimate=pl.CostEstimate(
-            flops=4 * MB, bytes_accessed=8 * MB, transcendentals=0
-        ),
-        name="place",
-    )(ids, got)
-    return pages[None], scales[None, :, :, :1].astype(BF), ids[None]
+def placed_pages(got):
+    groups, rows, width = got.shape
+    body = rows - 16
+    pages = got[:, :body].reshape(1, groups * CAP, 2, body // (2 * CAP), width)
+    scales = got[:, body : body + 2 * CAP, 0].reshape(1, groups * CAP, 2, 1)
+    ids = got[:, body + 2 * CAP : body + 3 * CAP, 0].astype(jnp.int32) - 1
+    return pages, scales, ids.reshape(1, groups * CAP)
 
 
 def rope_tables(positions, width):
@@ -617,14 +598,15 @@
     chip_rows = jnp.concatenate([keep, to_d(send, CORE_SWAP)], axis=0)
     chip_rows, *quarters = together(chip_rows, *quarters)
     out = stack_out([quarters[i] for i in (0, 3, 2, 1)], x)
-    rows, shards, last, (cosine, sine), out = gather_inputs(chip_rows, w, out, tables)
-    out_weights = lax.all_gather(out, "decode", axis=0)
     x_at = row_sources(z, x).astype(jnp.int32)
     w_at = shard_sources(zh, y).astype(jnp.int32)
-    own, other = project(rows, x_at, shards, w_at)
-    other = project_last(1, rows, x_at, last, w_at, other)
-    own = project_last(0, rows, x_at, last, w_at, after(own, other))
-    queries, keys, values = rotate(own, to_d(other, CORE_SWAP), cosine, sine)
+    rows, shards, before, (cosine, sine), out = gather_inputs(chip_rows, w, w_at, out, tables)
+    out = lax.all_to_all(out, "decode", 0, 0, axis_index_groups=PARITIES, tiled=True)
+    other = project(1, rows, x_at, shards, w_at, before)
+    own = project(0, rows, x_at, shards, w_at, after(before, other))
+    queries, keys, values, sent = rotate(
+        own, to_d(other, CORE_SWAP), cosine, sine, page_owner, 16
+    )
 
     def attend_chunk(chunk, queries):
         return attend(chunk, queries, cache_k[0, 0], cache_v[0, 0], keys, values, prefix_len)
@@ -636,22 +618,23 @@
         got = lax.all_to_all(partial, "tensor", 0, 0, tiled=True)
         return got.reshape(8, 32, partial.shape[1])
 
-    got = gather_pages(keys, values, page_owner)
     first = attend_chunk(0, queries)
     first_pieces = spread(first)
-    second = attend_chunk(1, after(queries, first))
+    queries, sent, out = together(queries, sent, out, first)[:3]
+    out_weights = out, to_d(out, CORE_SWAP)
+    got = lax.all_to_all(sent, "decode", 0, 0, tiled=True)
+    second = attend_chunk(1, queries)
+    second = after(second, out_weights[1])
     first_pieces[0] = after(first_pieces[0], second)
     second_pieces = spread(second)
-    first_partial = output(first_pieces, out_weights, x)
+    first_partial = output(first_pieces, out_weights, x, core)
     first_partial, *second_pieces = together(first_partial, *second_pieces)
-    first_back = back(first_partial)
-    second_partial = output(second_pieces, out_weights, x)
-    placed = place_pages(after(got, second_partial), page_owner.shape[1], d)
+    first_back = back(after(first_partial, got))
+    second_partial = output(second_pieces, out_weights, x, core)
     first_back = after(first_back, second_partial)
     second_back = back(after(second_partial, first_back))
-    second_back = after(second_back, placed[0])
     attn_out = finish([first_back, second_back])[None]
-    return (attn_out, *placed)
+    return (attn_out, *placed_pages(got))
 
 
 def solution(mesh):

time: 245 us -> 232 us (0.947)
  the two profiles are of different devices: /device:TPU:24 before, /device:TPU:1 now
where the time goes in v3:
time: 232 us; the launch traced here: 231 us
  Pallas kernels  83.9 us (36%)
  waiting for transfers between devices  70.9 us (31%)
  starting transfers between devices  61 us (26%)
  local copies, waits for them, and re-layouts  9.25 us (4%)
  other arithmetic  4.06 us (2%)
    pallas_call x2, Pallas kernels, attend(): pl.pallas_call(functools.partial(attend_kernel, chunk, block), grid=(head...  31.3 us
    ppermute x10, waiting for transfers between devices, to_d(): return lax.ppermute(value, 'decode', pairs)  31.1 us
    ppermute x16, starting transfers between devices, to_t(): return lax.ppermute(value, 'tensor', pairs)  21.9 us
    ppermute x10, starting transfers between devices, to_d(): return lax.ppermute(value, 'decode', pairs)  20 us
    all_to_all x2, waiting for transfers between devices, back(): got = lax.all_to_all(partial, 'tensor', 0, 0, tiled=True)  19.8 us
    pallas_call x2, Pallas kernels, output(): pl.pallas_call(output_kernel, in_specs=[smem()] + [hbm()] * 6, out_specs=...  16.1 us
    pallas_call x2, Pallas kernels, project(): pl.pallas_call(functools.partial(project_kernel, prompt), in_specs=[smem(...  14.3 us
    all_to_all x1, waiting for transfers between devices, body(): lax.all_to_all(out, 'decode', 0, 0, axis_index_groups=PARITIES, tiled=True)  10.6 us
  transfers between devices with their start and end apart: 30, of which 16 were waited for; matrix products, arithmetic and copies ran while one was open for 4% of the time, Pallas kernels for 33%

profile of v3, /device:TPU:1, one launch (start us, length us, event | category | flops | bytes accessed | tf_op | source)
XLA Modules:
  0.0 230.6 jit_solution(17562783932505054628)
XLA Ops:
  0.7 0.6 pad_add_fusion.at_ref
  1.2 4.1 %prepare.1 = (bf16[64,4096]{1,0:T(8,128)(2,1)}, bf16[64,4096]{1,0:T(8,128)(2,1)}, bf16[512,768]{1,0:T(8,128)(2,1)}, bf16[512,128]{1,0:T(8,128)(2,1)}, bf16[512,1...) custom-call(s32[2]{0:T(128)} %pad_add_fusion.at_ref, bf16[64,8192]{1,0:T(8,128)(2,1)} %bitcast.39, ...), custom_call_target="tpu_custom_call" | custom-call | tf_op jit(solution)/shard_map/prepare/pallas_call | solution.py:171
  5.3 1.5 collective-permute-start
  6.8 1.3 collective-permute-start.1
  8.1 2.5 %collective-permute-start.2 = (bf16[512,128]{1,0:T(8,128)(2,1)}, bf16[512,128]{1,0:T(8,128)(2,1)S(1)}, u32[]{:S(2)}, u32[]{:S(2)}) collective-permute-start(bf16[512,128]{1,0:T(8,128)(2,1)} %get-tuple-element.59), channel_id=1, source_target_pairs={{0,32},{16,48},{32,0},{48,16},{64,96},{80,112},{96,64},{112,80},{1... | collective-permute-start | bytes 393224 | tf_op jit(solution)/shard_map/ppermute | solution.py:50
  10.6 1.2 collective-permute-start.3
  11.7 1.1 pad_maximum_fusion.refs_0_
  13.3 3.9 %collective-permute-done.2.a2 = bf16[512,128]{1,0:T(8,128)(2,1)S(1)} collective-permute-done((bf16[512,128]{1,0:T(8,128)(2,1)}, bf16[512,128]{1,0:T(8,128)(2,1)S(1)}, u32[]{:S(2)}, u32[]{:S(2)}) %collective-permute-start.2) | collective-permute-done | bytes 131104 | tf_op jit(solution)/shard_map/ppermute | solution.py:50
  17.2 0.7 copy-done.16
  17.9 0.7 copy-done.17
  18.5 2.7 %collective-permute-start.7 = (bf16[128,4096]{1,0:T(8,128)(2,1)S(1)}, bf16[128,4096]{1,0:T(8,128)(2,1)S(1)}, u32[]{:S(2)}, u32[]{:S(2)}) collective-permute-start(bf16[128,4096]{1,0:T(8,128)(2,1)S(1)} %pad_maximum_fusion.refs_0_), channel_id=1, source_target_pairs={{0,48},{16,0},{32,16},{48,32},{64,112},{80,64},{96,80},{112,96},{1... | collective-permute-start | bytes 3145736 | tf_op jit(solution)/shard_map/ppermute | solution.py:50
  21.2 1.6 collective-permute-start.8
  22.8 1.3 collective-permute-start.4
  24.1 1.4 collective-permute-start.5
  25.6 16.0 %collective-permute-done.4.refs_7_.refs_9_ = bf16[512,768]{1,0:T(8,128)(2,1)} collective-permute-done((bf16[512,768]{1,0:T(8,128)(2,1)S(1)}, bf16[512,768]{1,0:T(8,128)(2,1)}, u32[]{:S(2)}, u32[]{:S(2)}) %collective-permute-start.4) | collective-permute-done | bytes 786464 | tf_op jit(solution)/shard_map/ppermute | solution.py:54
  41.6 2.0 collective-permute-done.6.refs_1_
  43.6 1.2 collective-permute-done.8.refs_4_
  44.9 2.7 %collective-permute-start.10 = (bf16[128,4096]{1,0:T(8,128)(2,1)}, bf16[128,4096]{1,0:T(8,128)(2,1)}, u32[]{:S(2)}, u32[]{:S(2)}) collective-permute-start(bf16[128,4096]{1,0:T(8,128)(2,1)} %collective-permute-done.8.refs_4_), channel_id=1, source_target_pairs={{0,48},{16,0},{32,16},{48,32},{64,112},{80,64},{96,80},{112,96},{1... | collective-permute-start | bytes 3145736 | tf_op jit(solution)/shard_map/ppermute | solution.py:50
  47.5 3.3 %collective-permute-start.11 = (bf16[512,768]{1,0:T(8,128)(2,1)S(1)}, bf16[512,768]{1,0:T(8,128)(2,1)}, u32[]{:S(2)}, u32[]{:S(2)}) collective-permute-start(bf16[512,768]{1,0:T(8,128)(2,1)S(1)} %copy-done.3), channel_id=1, source_target_pairs={{0,8},{1,9},{2,10},{3,11},{4,12},{5,13},{6,14},{7,15},{8,0},{9,1},... | collective-permute-start | bytes 2359304 | tf_op jit(solution)/shard_map/ppermute | solution.py:54
  50.8 1.3 collective-permute-start.12
  52.8 1.0 fusion
  53.8 1.0 pad_maximum_fusion.1
  54.8 3.6 %stack.109 = bf16[8,2048,128]{2,1,0:T(8,128)(2,1)} custom-call(s32[1]{0:T(128)} %bitcast.x_ref, bf16[512,128]{1,0:T(8,128)(2,1)} %get-tuple-element.68.a0, bf16[512,128]{1,0:T(8,128)(2,1)} %copy-done.17, bf16[512,128]{1,0:T(8,128)(2,1)} %copy-done.16, bf16[512,128]{1,0:T(8,128)(2,1)} %copy-done.15), custom_call_target="tpu_custom_call" | custom-call | tf_op jit(solution)/shard_map/stack/pallas_call | solution.py:117
  58.4 7.5 %collective-permute-done.11.refs_12_ = bf16[512,768]{1,0:T(8,128)(2,1)} collective-permute-done((bf16[512,768]{1,0:T(8,128)(2,1)S(1)}, bf16[512,768]{1,0:T(8,128)(2,1)}, u32[]{:S(2)}, u32[]{:S(2)}) %collective-permute-start.11) | collective-permute-done | bytes 786464 | tf_op jit(solution)/shard_map/ppermute | solution.py:54
  65.8 2.4 %collective-permute-done.12.refs_9_.refs_11_ = bf16[512,768]{1,0:T(8,128)(2,1)} collective-permute-done((bf16[512,768]{1,0:T(8,128)(2,1)}, bf16[512,768]{1,0:T(8,128)(2,1)}, u32[]{:S(2)}, u32[]{:S(2)}) %collective-permute-start.12) | collective-permute-done | bytes 786464 | tf_op jit(solution)/shard_map/ppermute | solution.py:54
  68.7 2.7 %collective-permute-start.14 = (bf16[128,4096]{1,0:T(8,128)(2,1)}, bf16[128,4096]{1,0:T(8,128)(2,1)S(1)}, u32[]{:S(2)}, u32[]{:S(2)}) collective-permute-start(bf16[128,4096]{1,0:T(8,128)(2,1)} %collective-permute-done.10.refs_5_), channel_id=1, source_target_pairs={{0,48},{16,0},{32,16},{48,32},{64,112},{80,64},{96,80},{112,96},{1... | collective-permute-start | bytes 3145736 | tf_op jit(solution)/shard_map/ppermute | solution.py:50
  71.3 1.3 collective-permute-start.15
  72.6 1.4 collective-permute-start.16
  74.1 3.1 %collective-permute-start.17 = (bf16[512,768]{1,0:T(8,128)(2,1)}, bf16[512,768]{1,0:T(8,128)(2,1)}, u32[]{:S(2)}, u32[]{:S(2)}) collective-permute-start(bf16[512,768]{1,0:T(8,128)(2,1)} %collective-permute-done.12.refs_9_.refs_11_), channel_id=1, source_target_pairs={{0,8},{1,9},{2,10},{3,11},{4,12},{5,13},{6,14},{7,15},{8,0},{9,1},... | collective-permute-start | bytes 2359304 | tf_op jit(solution)/shard_map/ppermute | solution.py:54
  77.2 0.6 stack.107.w_at
  77.8 7.5 %project_early.1.refs_16_ = f32[768,768]{1,0:T(8,128)} custom-call(s32[8]{0:T(128)} %stack.107.w_at, bf16[128,4096]{1,0:T(8,128)(2,1)} %copy-done, bf16[128,4096]{1,0:T(8,128)(2,1)} %copy-done.1, bf16[128,4096]{1,0:T(8,128)(2,1)} %copy-done.2, bf16[128,4096]{1,0:T(8,128)(2,1)} %collective-permute-done.9.refs_3_, ...), custom_call_target="tpu_custom_call" | custom-call | flops 1048576 | bytes 1048576 | tf_op jit(solution)/shard_map/project_early/pallas_call | solution.py:212
  85.3 2.5 %collective-permute-done.15.refs_13_ = bf16[512,768]{1,0:T(8,128)(2,1)S(1)} collective-permute-done((bf16[512,768]{1,0:T(8,128)(2,1)}, bf16[512,768]{1,0:T(8,128)(2,1)S(1)}, u32[]{:S(2)}, u32[]{:S(2)}) %collective-permute-start.15) | collective-permute-done | bytes 786464 | tf_op jit(solution)/shard_map/ppermute | solution.py:54
  88.1 2.4 %collective-permute-done.17.refs_15_ = bf16[512,768]{1,0:T(8,128)(2,1)} collective-permute-done((bf16[512,768]{1,0:T(8,128)(2,1)}, bf16[512,768]{1,0:T(8,128)(2,1)}, u32[]{:S(2)}, u32[]{:S(2)}) %collective-permute-start.17) | collective-permute-done | bytes 786464 | tf_op jit(solution)/shard_map/ppermute | solution.py:54
  90.4 0.7 collective-permute-done.13.refs_6_
  91.2 0.9 copy-done.5
  92.5 7.3 %all-to-all-start = ((bf16[8,2048,128]{2,1,0:T(8,128)(2,1)}), bf16[8,2048,128]{2,1,0:T(8,128)(2,1)}, u32[]{:S(2)}, u32[]{:S(2)}) async-start(bf16[8,2048,128]{2,1,0:T(8,128)(2,1)} %stack.109), calls=%async_computation | async-start | bytes 8388608 | tf_op jit(solution)/shard_map/all_to_all | solution.py:604
  99.8 0.6 stack.98.x_at
  100.4 7.2 %project.2 = f32[512,768]{1,0:T(8,128)} custom-call(s32[8]{0:T(128)} %stack.98.x_at, s32[8]{0:T(128)} %stack.107.w_at, bf16[128,4096]{1,0:T(8,128)(2,1)} %copy-done, bf16[128,4096]{1,0:T(8,128)(2,1)} %copy-done.1, bf16[128,4096]{1,0:T(8,128)(2,1)} %copy-done.2, bf16[128,4096]{1,0:T(8,128)(2,1)} %collective-permute-done.9.refs_3_, ...), custom_call_target="tpu_custom_call" | custom-call | flops 1048576 | bytes 1048576 | tf_op jit(solution)/shard_map/project/pallas_call | solution.py:275
  107.6 4.5 %collective-permute-start.18 = (f32[512,768]{1,0:T(8,128)}, f32[512,768]{1,0:T(8,128)S(1)}, u32[]{:S(2)}, u32[]{:S(2)}) collective-permute-start(f32[512,768]{1,0:T(8,128)} %project.2), channel_id=1, source_target_pairs={{0,1},{1,0},{2,3},{3,2},{4,5},{5,4},{6,7},{7,6},{8,9},{9,8},{10,11... | collective-permute-start | bytes 4718600 | tf_op jit(solution)/shard_map/ppermute | solution.py:54
  112.1 7.1 %project.3.a_ref = f32[512,768]{1,0:T(8,128)} custom-call(s32[8]{0:T(128)} %stack.98.x_at, s32[8]{0:T(128)} %stack.107.w_at, bf16[128,4096]{1,0:T(8,128)(2,1)} %copy-done, bf16[128,4096]{1,0:T(8,128)(2,1)} %copy-done.1, bf16[128,4096]{1,0:T(8,128)(2,1)} %copy-done.2, bf16[128,4096]{1,0:T(8,128)(2,1)} %collective-permute-done.9.refs_3_, ...), custom_call_target="tpu_custom_call" | custom-call | flops 1048576 | bytes 1048576 | tf_op jit(solution)/shard_map/project/pallas_call | solution.py:275
  119.2 1.2 copy-done.9
  120.4 4.3 %rotate.1 = (bf16[4,512,128]{2,1,0:T(8,128)(2,1)}, bf16[512,128]{1,0:T(8,128)(2,1)}, bf16[512,128]{1,0:T(8,128)(2,1)}, bf16[16,528,128]{2,1,0:T(8,128)(2,1)}) custom-call(s32[1,4]{1,0:T(1,128)} %owner_ref.1, f32[512,768]{1,0:T(8,128)} %project.3.a_ref, f32[512,768]{1,0:T(8,128)} %copy-done.9, f32[512,128]{1,0:T(8,128)} %get-tuple-element.86.cos_ref, ...), custom_call_target="tpu_custom_call" | custom-call | tf_op jit(solution)/shard_map/rotate/pallas_call | solution.py:344
  124.7 15.6 %attend.2.a0 = bf16[256,512]{1,0:T(8,128)(2,1)} custom-call(s32[1]{0:T(128)} %copy.16.live_ref, bf16[4,512,128]{2,1,0:T(8,128)(2,1)} %get-tuple-element.93.q_ref, bf16[8192,128]{1,0:T(8,128)(2,1)} %bitcast.31, bf16[8192,128]{1,0:T(8,128)(2,1)} %bitcast.33, bf16[512,128]{1,0:T(8,128)(2,1)} %get-tuple-element.89.kn_ref, bf16[512,128]{1,0:T(8,128)(2,1)} %get-tuple-element.90.vn_ref), custom_call_target="tpu_custom_call" | custom-call | flops 1048576 | bytes 1048576 | tf_op jit(solution)/shard_map/attend/pallas_call | solution.py:467
  140.3 10.6 %all-to-all-done.mine = bf16[8,2048,128]{2,1,0:T(8,128)(2,1)} async-done(((bf16[8,2048,128]{2,1,0:T(8,128)(2,1)}), bf16[8,2048,128]{2,1,0:T(8,128)(2,1)}, u32[]{:S(2)}, u32[]{:S(2)}) %all-to-all-start) | async-done | bytes 4194336 | tf_op jit(solution)/shard_map/all_to_all | solution.py:604
  150.9 0.9 collective-permute-start.19
  151.8 3.7 %all-to-all-start.1 = ((bf16[16,528,128]{2,1,0:T(8,128)(2,1)}), bf16[16,528,128]{2,1,0:T(8,128)(2,1)S(1)}, u32[]{:S(2)}, u32[]{:S(2)}) async-start(bf16[16,528,128]{2,1,0:T(8,128)(2,1)} %get-tuple-element.98), calls=%async_computation.1 | async-start | bytes 4325376 | tf_op jit(solution)/shard_map/all_to_all | solution.py:625
  155.8 2.4 %collective-permute-start.21 = (bf16[256,512]{1,0:T(8,128)(2,1)S(1)}, bf16[256,512]{1,0:T(8,128)(2,1)S(1)}, u32[]{:S(2)}, u32[]{:S(2)}) collective-permute-start(bf16[256,512]{1,0:T(8,128)(2,1)S(1)} %copy-done.10), channel_id=1, source_target_pairs={{0,48},{16,0},{32,16},{48,32},{64,112},{80,64},{96,80},{112,96},{1... | collective-permute-start | bytes 786440 | tf_op jit(solution)/shard_map/ppermute | solution.py:50
  158.8 15.6 %attend.3.a0 = bf16[256,512]{1,0:T(8,128)(2,1)} custom-call(s32[1]{0:T(128)} %copy.16.live_ref, bf16[4,512,128]{2,1,0:T(8,128)(2,1)} %get-tuple-element.93.q_ref, bf16[8192,128]{1,0:T(8,128)(2,1)} %bitcast.32, bf16[8192,128]{1,0:T(8,128)(2,1)} %bitcast.34, bf16[512,128]{1,0:T(8,128)(2,1)} %get-tuple-element.89.kn_ref, bf16[512,128]{1,0:T(8,128)(2,1)} %get-tuple-element.90.vn_ref), custom_call_target="tpu_custom_call" | custom-call | flops 1048576 | bytes 1048576 | tf_op jit(solution)/shard_map/attend/pallas_call | solution.py:467
  174.4 0.9 collective-permute-start.23
  175.4 1.8 collective-permute-start.24
  177.2 1.2 collective-permute-start.25
  178.4 0.6 stack.89.x_at
  179.0 0.7 copy-done.14
  179.7 8.0 %output.2 = bf16[256,2048]{1,0:T(8,128)(2,1)} custom-call(s32[5]{0:T(128)} %stack.89.x_at, bf16[256,512]{1,0:T(8,128)(2,1)} %attend.2.a0, bf16[256,512]{1,0:T(8,128)(2,1)} %copy-done.13, bf16[256,512]{1,0:T(8,128)(2,1)} %copy-done.14, bf16[256,512]{1,0:T(8,128)(2,1)} %collective-permute-done.22.a3, bf16[8,2048,128]{2,1,0:T(8,128)(2,1)} %all-to-all-done.mine, ...), custom_call_target="tpu_custom_call" | custom-call | flops 1048576 | bytes 1048576 | tf_op jit(solution)/shard_map/output/pallas_call | solution.py:521
  187.8 0.7 collective-permute-done.25.a3
  188.6 3.9 %all-to-all-start.2 = ((bf16[8,32,2048]{2,1,0:T(8,128)(2,1)}), bf16[8,32,2048]{2,1,0:T(8,128)(2,1)S(1)}, u32[]{:S(2)}, u32[]{:S(2)}) async-start(bf16[8,32,2048]{2,1,0:T(8,128)(2,1)} %bitcast.35), calls=%async_computation.2 | async-start | bytes 2097152 | tf_op jit(solution)/shard_map/all_to_all | solution.py:618
  192.5 8.0 %output.3 = bf16[256,2048]{1,0:T(8,128)(2,1)} custom-call(s32[5]{0:T(128)} %stack.89.x_at, bf16[256,512]{1,0:T(8,128)(2,1)} %attend.3.a0, bf16[256,512]{1,0:T(8,128)(2,1)} %copy-done.11, bf16[256,512]{1,0:T(8,128)(2,1)} %copy-done.12, bf16[256,512]{1,0:T(8,128)(2,1)} %collective-permute-done.25.a3, bf16[8,2048,128]{2,1,0:T(8,128)(2,1)} %all-to-all-done.mine, ...), custom_call_target="tpu_custom_call" | custom-call | flops 1048576 | bytes 1048576 | tf_op jit(solution)/shard_map/output/pallas_call | solution.py:521
  200.5 7.2 %all-to-all-done.2.refs_0_ = bf16[8,32,2048]{2,1,0:T(8,128)(2,1)S(1)} async-done(((bf16[8,32,2048]{2,1,0:T(8,128)(2,1)}), bf16[8,32,2048]{2,1,0:T(8,128)(2,1)S(1)}, u32[]{:S(2)}, u32[]{:S(2)}) %all-to-all-start.2) | async-done | bytes 1048608 | tf_op jit(solution)/shard_map/all_to_all | solution.py:618
  207.7 4.2 %all-to-all-start.3 = ((bf16[8,32,2048]{2,1,0:T(8,128)(2,1)}), bf16[8,32,2048]{2,1,0:T(8,128)(2,1)}, u32[]{:S(2)}, u32[]{:S(2)}) async-start(bf16[8,32,2048]{2,1,0:T(8,128)(2,1)} %bitcast.36), calls=%async_computation.3 | async-start | bytes 2097152 | tf_op jit(solution)/shard_map/all_to_all | solution.py:618
  212.2 0.6 copy.15
  213.1 0.6 sub.40
  213.7 1.5 slice.12
  215.3 12.5 %all-to-all-done.3.refs_1_ = bf16[8,32,2048]{2,1,0:T(8,128)(2,1)} async-done(((bf16[8,32,2048]{2,1,0:T(8,128)(2,1)}), bf16[8,32,2048]{2,1,0:T(8,128)(2,1)}, u32[]{:S(2)}, u32[]{:S(2)}) %all-to-all-start.3) | async-done | bytes 1048608 | tf_op jit(solution)/shard_map/all_to_all | solution.py:618
  227.8 2.8 %finish.1 = bf16[64,8192]{1,0:T(8,128)(2,1)} custom-call(bf16[8,32,2048]{2,1,0:T(8,128)(2,1)} %copy-done.7, bf16[8,32,2048]{2,1,0:T(8,128)(2,1)} %all-to-all-done.3.refs_1_), custom_call_target="tpu_custom_call" | custom-call | tf_op jit(solution)/shard_map/finish/pallas_call | solution.py:551
  (58 shorter events, 2.9 us)
Async XLA Ops:
  5.3 17.5 %copy-start.3 = (bf16[512,768]{1,0:T(8,128)(2,1)S(1)}, bf16[512,768]{1,0:T(8,128)(2,1)}, u32[]{:S(2)}) copy-start(bf16[512,768]{1,0:T(8,128)(2,1)} %get-tuple-element.67.refs_6_.refs_8_) | copy-start | bytes 2359300
  5.3 6.4 %collective-permute-start = (bf16[64,4096]{1,0:T(8,128)(2,1)}, bf16[64,4096]{1,0:T(8,128)(2,1)S(1)}, u32[]{:S(2)}, u32[]{:S(2)}) collective-permute-start(bf16[64,4096]{1,0:T(8,128)(2,1)} %get-tuple-element.56), channel_id=1, source_target_pairs={{0,1},{1,0},{2,3},{3,2},{4,5},{5,4},{6,7},{7,6},{8,9},{9,8},{10,11... | collective-permute-start | bytes 1572872 | tf_op jit(solution)/shard_map/ppermute | solution.py:54
  6.8 6.5 %collective-permute-start.1 = (bf16[512,128]{1,0:T(8,128)(2,1)}, bf16[512,128]{1,0:T(8,128)(2,1)S(1)}, u32[]{:S(2)}, u32[]{:S(2)}) collective-permute-start(bf16[512,128]{1,0:T(8,128)(2,1)} %get-tuple-element.58), channel_id=1, source_target_pairs={{0,16},{16,32},{32,48},{48,0},{64,80},{80,96},{96,112},{112,64},{1... | collective-permute-start | bytes 393224 | tf_op jit(solution)/shard_map/ppermute | solution.py:50
  8.1 9.1 %collective-permute-start.2 = (bf16[512,128]{1,0:T(8,128)(2,1)}, bf16[512,128]{1,0:T(8,128)(2,1)S(1)}, u32[]{:S(2)}, u32[]{:S(2)}) collective-permute-start(bf16[512,128]{1,0:T(8,128)(2,1)} %get-tuple-element.59), channel_id=1, source_target_pairs={{0,32},{16,48},{32,0},{48,16},{64,96},{80,112},{96,64},{112,80},{1... | collective-permute-start | bytes 393224 | tf_op jit(solution)/shard_map/ppermute | solution.py:50
  10.6 6.6 %collective-permute-start.3 = (bf16[512,128]{1,0:T(8,128)(2,1)}, bf16[512,128]{1,0:T(8,128)(2,1)S(1)}, u32[]{:S(2)}, u32[]{:S(2)}) collective-permute-start(bf16[512,128]{1,0:T(8,128)(2,1)} %get-tuple-element.60), channel_id=1, source_target_pairs={{0,48},{16,0},{32,16},{48,32},{64,112},{80,64},{96,80},{112,96},{1... | collective-permute-start | bytes 393224 | tf_op jit(solution)/shard_map/ppermute | solution.py:50
  12.9 45.5 %copy-start = (bf16[128,4096]{1,0:T(8,128)(2,1)}, bf16[128,4096]{1,0:T(8,128)(2,1)S(1)}, u32[]{:S(2)}) copy-start(bf16[128,4096]{1,0:T(8,128)(2,1)S(1)} %pad_maximum_fusion.refs_0_) | copy-start | bytes 3145732
  13.3 41.4 %copy-start.15 = (bf16[512,128]{1,0:T(8,128)(2,1)}, bf16[512,128]{1,0:T(8,128)(2,1)S(1)}, u32[]{:S(2)}) copy-start(bf16[512,128]{1,0:T(8,128)(2,1)S(1)} %collective-permute-done.1.a3) | copy-start | bytes 393220
  17.2 0.7 copy-start.16
  17.8 0.7 copy-start.17
  18.5 25.1 %collective-permute-start.6 = (bf16[128,4096]{1,0:T(8,128)(2,1)S(1)}, bf16[128,4096]{1,0:T(8,128)(2,1)S(1)}, u32[]{:S(2)}, u32[]{:S(2)}) collective-permute-start(bf16[128,4096]{1,0:T(8,128)(2,1)S(1)} %pad_maximum_fusion.refs_0_), channel_id=1, source_target_pairs={{0,16},{16,32},{32,48},{48,0},{64,80},{80,96},{96,112},{112,64},{1... | collective-permute-start | bytes 3145736 | tf_op jit(solution)/shard_map/ppermute | solution.py:50
  18.5 25.1 %collective-permute-start.7 = (bf16[128,4096]{1,0:T(8,128)(2,1)S(1)}, bf16[128,4096]{1,0:T(8,128)(2,1)S(1)}, u32[]{:S(2)}, u32[]{:S(2)}) collective-permute-start(bf16[128,4096]{1,0:T(8,128)(2,1)S(1)} %pad_maximum_fusion.refs_0_), channel_id=1, source_target_pairs={{0,48},{16,0},{32,16},{48,32},{64,112},{80,64},{96,80},{112,96},{1... | collective-permute-start | bytes 3145736 | tf_op jit(solution)/shard_map/ppermute | solution.py:50
  21.2 23.7 %collective-permute-start.8 = (bf16[128,4096]{1,0:T(8,128)(2,1)S(1)}, bf16[128,4096]{1,0:T(8,128)(2,1)}, u32[]{:S(2)}, u32[]{:S(2)}) collective-permute-start(bf16[128,4096]{1,0:T(8,128)(2,1)S(1)} %pad_maximum_fusion.refs_0_), channel_id=1, source_target_pairs={{0,64},{16,80},{32,96},{48,112},{64,0},{80,16},{96,32},{112,48},{1... | collective-permute-start | bytes 3145736 | tf_op jit(solution)/shard_map/ppermute | solution.py:50
  22.8 18.8 %collective-permute-start.4 = (bf16[512,768]{1,0:T(8,128)(2,1)S(1)}, bf16[512,768]{1,0:T(8,128)(2,1)}, u32[]{:S(2)}, u32[]{:S(2)}) collective-permute-start(bf16[512,768]{1,0:T(8,128)(2,1)S(1)} %copy-done.3), channel_id=1, source_target_pairs={{0,2},{1,3},{2,4},{3,5},{4,6},{5,7},{6,0},{7,1},{8,10},{9,11},{10,... | collective-permute-start | bytes 2359304 | tf_op jit(solution)/shard_map/ppermute | solution.py:54
  24.1 17.5 %collective-permute-start.5 = (bf16[512,768]{1,0:T(8,128)(2,1)S(1)}, bf16[512,768]{1,0:T(8,128)(2,1)S(1)}, u32[]{:S(2)}, u32[]{:S(2)}) collective-permute-start(bf16[512,768]{1,0:T(8,128)(2,1)S(1)} %copy-done.3), channel_id=1, source_target_pairs={{0,6},{1,7},{2,0},{3,1},{4,2},{5,3},{6,4},{7,5},{8,14},{9,15},{10,... | collective-permute-start | bytes 2359304 | tf_op jit(solution)/shard_map/ppermute | solution.py:54
  41.6 9.2 %copy-start.4 = (bf16[512,768]{1,0:T(8,128)(2,1)}, bf16[512,768]{1,0:T(8,128)(2,1)S(1)}, u32[]{:S(2)}) copy-start(bf16[512,768]{1,0:T(8,128)(2,1)S(1)} %collective-permute-done.5.refs_8_.refs_10_) | copy-start | bytes 2359300
  43.6 14.7 %copy-start.1 = (bf16[128,4096]{1,0:T(8,128)(2,1)}, bf16[128,4096]{1,0:T(8,128)(2,1)S(1)}, u32[]{:S(2)}) copy-start(bf16[128,4096]{1,0:T(8,128)(2,1)S(1)} %collective-permute-done.6.refs_1_) | copy-start | bytes 3145732
  43.6 14.7 %copy-start.2 = (bf16[128,4096]{1,0:T(8,128)(2,1)}, bf16[128,4096]{1,0:T(8,128)(2,1)S(1)}, u32[]{:S(2)}) copy-start(bf16[128,4096]{1,0:T(8,128)(2,1)S(1)} %collective-permute-done.7.refs_2_) | copy-start | bytes 3145732
  44.9 23.8 %collective-permute-start.9 = (bf16[128,4096]{1,0:T(8,128)(2,1)S(1)}, bf16[128,4096]{1,0:T(8,128)(2,1)}, u32[]{:S(2)}, u32[]{:S(2)}) collective-permute-start(bf16[128,4096]{1,0:T(8,128)(2,1)S(1)} %collective-permute-done.6.refs_1_), channel_id=1, source_target_pairs={{0,16},{16,32},{32,48},{48,0},{64,80},{80,96},{96,112},{112,64},{1... | collective-permute-start | bytes 3145736 | tf_op jit(solution)/shard_map/ppermute | solution.py:50
  44.9 23.8 %collective-permute-start.10 = (bf16[128,4096]{1,0:T(8,128)(2,1)}, bf16[128,4096]{1,0:T(8,128)(2,1)}, u32[]{:S(2)}, u32[]{:S(2)}) collective-permute-start(bf16[128,4096]{1,0:T(8,128)(2,1)} %collective-permute-done.8.refs_4_), channel_id=1, source_target_pairs={{0,48},{16,0},{32,16},{48,32},{64,112},{80,64},{96,80},{112,96},{1... | collective-permute-start | bytes 3145736 | tf_op jit(solution)/shard_map/ppermute | solution.py:50
  47.5 18.3 %collective-permute-start.11 = (bf16[512,768]{1,0:T(8,128)(2,1)S(1)}, bf16[512,768]{1,0:T(8,128)(2,1)}, u32[]{:S(2)}, u32[]{:S(2)}) collective-permute-start(bf16[512,768]{1,0:T(8,128)(2,1)S(1)} %copy-done.3), channel_id=1, source_target_pairs={{0,8},{1,9},{2,10},{3,11},{4,12},{5,13},{6,14},{7,15},{8,0},{9,1},... | collective-permute-start | bytes 2359304 | tf_op jit(solution)/shard_map/ppermute | solution.py:54
  50.8 17.5 %collective-permute-start.12 = (bf16[512,768]{1,0:T(8,128)(2,1)}, bf16[512,768]{1,0:T(8,128)(2,1)}, u32[]{:S(2)}, u32[]{:S(2)}) collective-permute-start(bf16[512,768]{1,0:T(8,128)(2,1)} %collective-permute-done.4.refs_7_.refs_9_), channel_id=1, source_target_pairs={{0,2},{1,3},{2,4},{3,5},{4,6},{5,7},{6,0},{7,1},{8,10},{9,11},{10,... | collective-permute-start | bytes 2359304 | tf_op jit(solution)/shard_map/ppermute | solution.py:54
  68.7 22.5 %collective-permute-start.13 = (bf16[128,4096]{1,0:T(8,128)(2,1)}, bf16[128,4096]{1,0:T(8,128)(2,1)S(1)}, u32[]{:S(2)}, u32[]{:S(2)}) collective-permute-start(bf16[128,4096]{1,0:T(8,128)(2,1)} %collective-permute-done.8.refs_4_), channel_id=1, source_target_pairs={{0,16},{16,32},{32,48},{48,0},{64,80},{80,96},{96,112},{112,64},{1... | collective-permute-start | bytes 3145736 | tf_op jit(solution)/shard_map/ppermute | solution.py:50
  68.7 22.5 %collective-permute-start.14 = (bf16[128,4096]{1,0:T(8,128)(2,1)}, bf16[128,4096]{1,0:T(8,128)(2,1)S(1)}, u32[]{:S(2)}, u32[]{:S(2)}) collective-permute-start(bf16[128,4096]{1,0:T(8,128)(2,1)} %collective-permute-done.10.refs_5_), channel_id=1, source_target_pairs={{0,48},{16,0},{32,16},{48,32},{64,112},{80,64},{96,80},{112,96},{1... | collective-permute-start | bytes 3145736 | tf_op jit(solution)/shard_map/ppermute | solution.py:50
  71.3 16.4 %collective-permute-start.15 = (bf16[512,768]{1,0:T(8,128)(2,1)}, bf16[512,768]{1,0:T(8,128)(2,1)S(1)}, u32[]{:S(2)}, u32[]{:S(2)}) collective-permute-start(bf16[512,768]{1,0:T(8,128)(2,1)} %collective-permute-done.11.refs_12_), channel_id=1, source_target_pairs={{0,2},{1,3},{2,4},{3,5},{4,6},{5,7},{6,0},{7,1},{8,10},{9,11},{10,... | collective-permute-start | bytes 2359304 | tf_op jit(solution)/shard_map/ppermute | solution.py:54
  72.6 15.4 %collective-permute-start.16 = (bf16[512,768]{1,0:T(8,128)(2,1)}, bf16[512,768]{1,0:T(8,128)(2,1)}, u32[]{:S(2)}, u32[]{:S(2)}) collective-permute-start(bf16[512,768]{1,0:T(8,128)(2,1)} %collective-permute-done.11.refs_12_), channel_id=1, source_target_pairs={{0,6},{1,7},{2,0},{3,1},{4,2},{5,3},{6,4},{7,5},{8,14},{9,15},{10,... | collective-permute-start | bytes 2359304 | tf_op jit(solution)/shard_map/ppermute | solution.py:54
  74.1 16.3 %collective-permute-start.17 = (bf16[512,768]{1,0:T(8,128)(2,1)}, bf16[512,768]{1,0:T(8,128)(2,1)}, u32[]{:S(2)}, u32[]{:S(2)}) collective-permute-start(bf16[512,768]{1,0:T(8,128)(2,1)} %collective-permute-done.12.refs_9_.refs_11_), channel_id=1, source_target_pairs={{0,8},{1,9},{2,10},{3,11},{4,12},{5,13},{6,14},{7,15},{8,0},{9,1},... | collective-permute-start | bytes 2359304 | tf_op jit(solution)/shard_map/ppermute | solution.py:54
  87.8 3.4 %copy-start.8 = (bf16[512,768]{1,0:T(8,128)(2,1)}, bf16[512,768]{1,0:T(8,128)(2,1)S(1)}, u32[]{:S(2)}) copy-start(bf16[512,768]{1,0:T(8,128)(2,1)S(1)} %collective-permute-done.15.refs_13_) | copy-start | bytes 2359300
  91.2 1.0 copy-start.5
  91.2 1.3 copy-start.6
  92.5 58.4 %all-to-all-start = ((bf16[8,2048,128]{2,1,0:T(8,128)(2,1)}), bf16[8,2048,128]{2,1,0:T(8,128)(2,1)}, u32[]{:S(2)}, u32[]{:S(2)}) async-start(bf16[8,2048,128]{2,1,0:T(8,128)(2,1)} %stack.109), calls=%async_computation | async-start | bytes 8388608 | tf_op jit(solution)/shard_map/all_to_all | solution.py:604
  107.6 11.7 %collective-permute-start.18 = (f32[512,768]{1,0:T(8,128)}, f32[512,768]{1,0:T(8,128)S(1)}, u32[]{:S(2)}, u32[]{:S(2)}) collective-permute-start(f32[512,768]{1,0:T(8,128)} %project.2), channel_id=1, source_target_pairs={{0,1},{1,0},{2,3},{3,2},{4,5},{5,4},{6,7},{7,6},{8,9},{9,8},{10,11... | collective-permute-start | bytes 4718600 | tf_op jit(solution)/shard_map/ppermute | solution.py:54
  119.2 1.2 copy-start.9
  150.9 4.6 %copy-start.10 = (bf16[256,512]{1,0:T(8,128)(2,1)S(1)}, bf16[256,512]{1,0:T(8,128)(2,1)}, u32[]{:S(2)}) copy-start(bf16[256,512]{1,0:T(8,128)(2,1)} %attend.2.a0) | copy-start | bytes 786436
  150.9 23.5 %collective-permute-start.19 = (bf16[8,2048,128]{2,1,0:T(8,128)(2,1)}, bf16[8,2048,128]{2,1,0:T(8,128)(2,1)}, u32[]{:S(2)}, u32[]{:S(2)}) collective-permute-start(bf16[8,2048,128]{2,1,0:T(8,128)(2,1)} %all-to-all-done.mine), channel_id=1, source_target_pairs={{0,1},{1,0},{2,3},{3,2},{4,5},{5,4},{6,7},{7,6},{8,9},{9,8},{10,11... | collective-permute-start | bytes 12582920 | tf_op jit(solution)/shard_map/ppermute | solution.py:54
  151.8 36.8 %all-to-all-start.1 = ((bf16[16,528,128]{2,1,0:T(8,128)(2,1)}), bf16[16,528,128]{2,1,0:T(8,128)(2,1)S(1)}, u32[]{:S(2)}, u32[]{:S(2)}) async-start(bf16[16,528,128]{2,1,0:T(8,128)(2,1)} %get-tuple-element.98), calls=%async_computation.1 | async-start | bytes 4325376 | tf_op jit(solution)/shard_map/all_to_all | solution.py:625
  155.5 21.7 %collective-permute-start.20 = (bf16[256,512]{1,0:T(8,128)(2,1)S(1)}, bf16[256,512]{1,0:T(8,128)(2,1)S(1)}, u32[]{:S(2)}, u32[]{:S(2)}) collective-permute-start(bf16[256,512]{1,0:T(8,128)(2,1)S(1)} %copy-done.10), channel_id=1, source_target_pairs={{0,16},{16,32},{32,48},{48,0},{64,80},{80,96},{96,112},{112,64},{1... | collective-permute-start | bytes 786440 | tf_op jit(solution)/shard_map/ppermute | solution.py:50
  155.8 23.2 %collective-permute-start.21 = (bf16[256,512]{1,0:T(8,128)(2,1)S(1)}, bf16[256,512]{1,0:T(8,128)(2,1)S(1)}, u32[]{:S(2)}, u32[]{:S(2)}) collective-permute-start(bf16[256,512]{1,0:T(8,128)(2,1)S(1)} %copy-done.10), channel_id=1, source_target_pairs={{0,48},{16,0},{32,16},{48,32},{64,112},{80,64},{96,80},{112,96},{1... | collective-permute-start | bytes 786440 | tf_op jit(solution)/shard_map/ppermute | solution.py:50
  158.2 20.8 %collective-permute-start.22 = (bf16[256,512]{1,0:T(8,128)(2,1)S(1)}, bf16[256,512]{1,0:T(8,128)(2,1)}, u32[]{:S(2)}, u32[]{:S(2)}) collective-permute-start(bf16[256,512]{1,0:T(8,128)(2,1)S(1)} %copy-done.10), channel_id=1, source_target_pairs={{0,32},{16,48},{32,0},{48,16},{64,96},{80,112},{96,64},{112,80},{1... | collective-permute-start | bytes 786440 | tf_op jit(solution)/shard_map/ppermute | solution.py:50
  174.4 13.4 %collective-permute-start.23 = (bf16[256,512]{1,0:T(8,128)(2,1)}, bf16[256,512]{1,0:T(8,128)(2,1)S(1)}, u32[]{:S(2)}, u32[]{:S(2)}) collective-permute-start(bf16[256,512]{1,0:T(8,128)(2,1)} %attend.3.a0), channel_id=1, source_target_pairs={{0,16},{16,32},{32,48},{48,0},{64,80},{80,96},{96,112},{112,64},{1... | collective-permute-start | bytes 786440 | tf_op jit(solution)/shard_map/ppermute | solution.py:50
  175.4 12.4 %collective-permute-start.24 = (bf16[256,512]{1,0:T(8,128)(2,1)}, bf16[256,512]{1,0:T(8,128)(2,1)S(1)}, u32[]{:S(2)}, u32[]{:S(2)}) collective-permute-start(bf16[256,512]{1,0:T(8,128)(2,1)} %attend.3.a0), channel_id=1, source_target_pairs={{0,48},{16,0},{32,16},{48,32},{64,112},{80,64},{96,80},{112,96},{1... | collective-permute-start | bytes 786440 | tf_op jit(solution)/shard_map/ppermute | solution.py:50
  177.2 1.8 copy-start.13
  177.2 11.4 %collective-permute-start.25 = (bf16[256,512]{1,0:T(8,128)(2,1)}, bf16[256,512]{1,0:T(8,128)(2,1)}, u32[]{:S(2)}, u32[]{:S(2)}) collective-permute-start(bf16[256,512]{1,0:T(8,128)(2,1)} %attend.3.a0), channel_id=1, source_target_pairs={{0,32},{16,48},{32,0},{48,16},{64,96},{80,112},{96,64},{112,80},{1... | collective-permute-start | bytes 786440 | tf_op jit(solution)/shard_map/ppermute | solution.py:50
  179.0 0.7 copy-start.14
  187.8 4.7 %copy-start.11 = (bf16[256,512]{1,0:T(8,128)(2,1)}, bf16[256,512]{1,0:T(8,128)(2,1)S(1)}, u32[]{:S(2)}) copy-start(bf16[256,512]{1,0:T(8,128)(2,1)S(1)} %collective-permute-done.23.a1) | copy-start | bytes 786436
  187.8 0.8 copy-start.12
  188.6 19.2 %all-to-all-start.2 = ((bf16[8,32,2048]{2,1,0:T(8,128)(2,1)}), bf16[8,32,2048]{2,1,0:T(8,128)(2,1)S(1)}, u32[]{:S(2)}, u32[]{:S(2)}) async-start(bf16[8,32,2048]{2,1,0:T(8,128)(2,1)} %bitcast.35), calls=%async_computation.2 | async-start | bytes 2097152 | tf_op jit(solution)/shard_map/all_to_all | solution.py:618
  207.7 7.5 %copy-start.7 = (bf16[8,32,2048]{2,1,0:T(8,128)(2,1)}, bf16[8,32,2048]{2,1,0:T(8,128)(2,1)S(1)}, u32[]{:S(2)}) copy-start(bf16[8,32,2048]{2,1,0:T(8,128)(2,1)S(1)} %all-to-all-done.2.refs_0_) | copy-start | bytes 3145732
  207.7 20.1 %all-to-all-start.3 = ((bf16[8,32,2048]{2,1,0:T(8,128)(2,1)}), bf16[8,32,2048]{2,1,0:T(8,128)(2,1)}, u32[]{:S(2)}, u32[]{:S(2)}) async-start(bf16[8,32,2048]{2,1,0:T(8,128)(2,1)} %bitcast.36), calls=%async_computation.3 | async-start | bytes 2097152 | tf_op jit(solution)/shard_map/all_to_all | solution.py:618
